TPU v7x, 512 devices: a whole 4x8x8 slice. The times are simulated.
512 devices in a mesh: fft: 32 (over x, z), slab: 16 (over y, core).
Axes of the slice: x: 4, y: 8, z: 8, core: 2. Of those that a mesh axis runs over, the one named last changes fastest.
Arguments:
- ml_pos: float32 [3, 16384], replicated, may hold values from 0 to 58
- ml_width: float32 [16384], replicated, may hold values from 0.7 to 1.6
- ml_drive: float32 [16384], P(('fft', 'slab')), may hold values from -8 to 8
- ml_hard: float32 [16384], P(('fft', 'slab')), may hold values from 4 to 12
- mm_charge: float32 [3145728], P(('fft', 'slab')), may hold values from -3 to 3
- mm_frac: float32 [3, 3145728], P(None, ('fft', 'slab')), may hold values from 0 to 1
- mm_cell: int32 [3, 3145728], P(None, ('fft', 'slab')), may hold values from 0 to 383, as said below
- slot_atom: int32 [16384], P(('fft', 'slab')), may hold values from 0 to 16383, each once
- slot_frac: float32 [3, 16384], P(None, ('fft', 'slab')), may hold values from 0 to 1
- slot_cell: int32 [3, 16384], P(None, ('fft', 'slab')), may hold values from 0 to 383, as said below
Outputs:
- ml_charge: float32 [16384], P(('fft', 'slab'))
- struct_re: float32 [384, 192, 384], P('fft', 'slab')
- struct_im: float32 [384, 192, 384], P('fft', 'slab')
Inputs may be any that keep to these rules, and one draw needn't show every extreme that they name: `mm_cell`: row 0 is a grid point along the first dimension (0 to 383), row 1 a point of the owner's 24 along the second, row 2 of the owner's 12 along the third. `slot_cell`: as for mm_cell. `slot_atom`: every ML atom is held by exactly one slot.
All inputs are finite; a program needn't handle non-finite values.
Results may differ from a plain program's by a relative error of at most 0.0003.
Values sent between devices are 32-bit elements; how exact they have to be, the bound alone decides.
No kernel may reach another device: no remote copies, remote signals or barrier semaphores. Data moves between devices by JAX's collectives and lax.ppermute only.
A program may use at most 128 MiB of HBM per device.

v0:
```python
import math

import jax
import jax.numpy as jnp
from jax import lax
from jax.sharding import PartitionSpec as P

NG = 384
ITERS = 3


KE = 14.4
ALPHA = 0.08
SOFT = 0.01
SQPI = math.sqrt(math.pi)
HIGH = lax.Precision.HIGHEST


def shifted(value, axis, steps):
    count = lax.axis_size(axis)
    pairs = [(source, (source + steps) % count) for source in range(count)]
    return lax.ppermute(value, axis, pairs)


def couplings(row_pos, row_width, col_pos, col_width, row_first, col_first):
    dist_sq = (row_pos[0][:, None] - col_pos[0][None, :]) ** 2
    dist_sq = dist_sq + (row_pos[1][:, None] - col_pos[1][None, :]) ** 2
    dist_sq = dist_sq + (row_pos[2][:, None] - col_pos[2][None, :]) ** 2
    distance = jnp.sqrt(dist_sq + SOFT)
    pair_len = jnp.sqrt(2.0 * (row_width[:, None] ** 2 + col_width[None, :] ** 2))
    kernel = KE * (lax.erf(distance / pair_len) - lax.erf(ALPHA * distance)) / distance
    row_ids = row_first + jnp.arange(row_pos.shape[1], dtype=jnp.int32)
    col_ids = col_first + jnp.arange(col_pos.shape[1], dtype=jnp.int32)
    return jnp.where(row_ids[:, None] == col_ids[None, :], 0.0, kernel)


def spline(fraction):
    cubed = fraction**3
    squared = fraction**2
    return jnp.stack(
        [
            (1.0 - fraction) ** 3 / 6.0,
            (3.0 * cubed - 6.0 * squared + 4.0) / 6.0,
            (-3.0 * cubed + 3.0 * squared + 3.0 * fraction + 1.0) / 6.0,
            cubed / 6.0,
        ]
    )


def placed(base, weights, length):
    points = jnp.arange(length, dtype=jnp.int32)
    summed = jnp.zeros((base.shape[0], length), jnp.float32)
    for shift_k in range(4):
        target = (base + shift_k) % length
        summed = summed + jnp.where(
            target[:, None] == points[None, :], weights[shift_k][:, None], 0.0
        )
    return summed


def spread_sites(charge, fraction, grid_cell, ext_y, ext_z):
    weights = spline(fraction)
    along_x = placed(grid_cell[0], weights[:, 0], NG)
    along_y = placed(grid_cell[1], weights[:, 1], ext_y)
    along_z = placed(grid_cell[2], weights[:, 2], ext_z)
    yz_plane = (charge[:, None] * along_y)[:, :, None] * along_z[:, None, :]
    yz_plane = yz_plane.reshape(charge.shape[0], ext_y * ext_z)
    result = lax.dot_general(
        yz_plane,
        along_x,
        (((0,), (0,)), ((), ())),
        precision=HIGH,
        preferred_element_type=jnp.float32,
    )
    return result.reshape(ext_y, ext_z, NG)


def dft_tables(length):
    points = jnp.arange(length, dtype=jnp.int32)
    phase_int = points[:, None] * points[None, :] % length
    angle_rad = phase_int.astype(jnp.float32) * (2.0 * math.pi / length)
    return (jnp.cos(angle_rad), jnp.sin(angle_rad))


def ml_total(value):
    return lax.psum(value, ("fft", "slab"))


def on_device(
    ml_pos,
    ml_width,
    ml_drive,
    ml_hard,
    mm_charge,
    mm_frac,
    mm_cell,
    slot_atom,
    slot_frac,
    slot_cell,
):
    n_slab = lax.axis_size("slab")
    n_fft = lax.axis_size("fft")
    fft_index = lax.axis_index("fft")
    slab_index = lax.axis_index("slab")
    piece_len = ml_drive.shape[0]
    row_len = piece_len * n_slab
    all_atoms = ml_pos.shape[1]
    col_len = all_atoms // n_slab
    row_first = fft_index * row_len
    col_first = slab_index * col_len
    piece_first = row_first + slab_index * piece_len
    row_pos = lax.dynamic_slice_in_dim(ml_pos, row_first, row_len, 1)
    row_width = lax.dynamic_slice_in_dim(ml_width, row_first, row_len)
    col_pos = lax.dynamic_slice_in_dim(ml_pos, col_first, col_len, 1)
    col_width = lax.dynamic_slice_in_dim(ml_width, col_first, col_len)
    coupling = couplings(row_pos, row_width, col_pos, col_width, row_first, col_first)
    self_term = KE * (1.0 / (ml_width * SQPI) - 2.0 * ALPHA / SQPI)
    charge_full = jnp.zeros((all_atoms,), jnp.float32)
    diag_piece = ml_hard + lax.dynamic_slice_in_dim(self_term, piece_first, piece_len)
    residue = -ml_drive
    direction = residue
    norm_now = ml_total(jnp.sum(residue * residue))
    for iteration in range(ITERS):
        dir_full = lax.all_gather(direction, ("fft", "slab"), axis=0, tiled=True)
        dir_cols = lax.dynamic_slice_in_dim(dir_full, col_first, col_len)
        applied = (
            lax.psum_scatter(
                jnp.dot(coupling, dir_cols, precision=HIGH, preferred_element_type=jnp.float32),
                "slab",
                scatter_dimension=0,
                tiled=True,
            )
            + diag_piece * direction
        )
        step_len = norm_now / ml_total(jnp.sum(direction * applied))
        charge_full = charge_full + step_len * dir_full
        residue = residue - step_len * applied
        norm_next = ml_total(jnp.sum(residue * residue))
        direction = residue + norm_next / norm_now * direction
        norm_now = norm_next
    charge_piece = lax.dynamic_slice_in_dim(charge_full, piece_first, piece_len)
    y_len = NG // n_slab
    z_len = NG // n_fft
    ext_y = y_len + 3
    ext_z = z_len + 3
    slot_charge = charge_full[slot_atom]
    grid_ext = spread_sites(
        jnp.concatenate([mm_charge, slot_charge]),
        jnp.concatenate([mm_frac, slot_frac], 1),
        jnp.concatenate([mm_cell, slot_cell], 1),
        ext_y,
        ext_z,
    )
    came_y = shifted(grid_ext[y_len:], "slab", 1)
    folded = jnp.concatenate([grid_ext[:3] + came_y, grid_ext[3:y_len]], 0)
    came_z = shifted(folded[:, z_len:], "fft", 1)
    charge_grid = jnp.concatenate([folded[:, :3] + came_z, folded[:, 3:z_len]], 1)
    cos_t, sin_t = dft_tables(NG)
    kept = NG // 2
    cos_half = cos_t[:, :kept]
    sin_half = sin_t[:, :kept]
    norm_scale = 1.0 / (NG * math.sqrt(NG))
    first_re = jnp.einsum(
        "yzx,xk->kzy", charge_grid, cos_half, precision=HIGH, preferred_element_type=jnp.float32
    )
    first_im = -jnp.einsum(
        "yzx,xk->kzy", charge_grid, sin_half, precision=HIGH, preferred_element_type=jnp.float32
    )

    def along_y(pieces):
        part_re, part_im = pieces
        out_re = jnp.einsum(
            "xzy,yk->kxz", part_re, cos_t, precision=HIGH, preferred_element_type=jnp.float32
        )
        out_re = out_re + jnp.einsum(
            "xzy,yk->kxz", part_im, sin_t, precision=HIGH, preferred_element_type=jnp.float32
        )
        out_im = jnp.einsum(
            "xzy,yk->kxz", part_im, cos_t, precision=HIGH, preferred_element_type=jnp.float32
        )
        out_im = out_im - jnp.einsum(
            "xzy,yk->kxz", part_re, sin_t, precision=HIGH, preferred_element_type=jnp.float32
        )
        return (out_re, out_im)

    second_re, second_im = along_y(
        (
            lax.all_to_all(first_re, "slab", split_axis=0, concat_axis=2, tiled=True),
            lax.all_to_all(first_im, "slab", split_axis=0, concat_axis=2, tiled=True),
        )
    )

    def along_z(pieces):
        part_re, part_im = pieces
        out_re = jnp.einsum(
            "yxz,zk->yxk", part_re, cos_t, precision=HIGH, preferred_element_type=jnp.float32
        )
        out_re = out_re + jnp.einsum(
            "yxz,zk->yxk", part_im, sin_t, precision=HIGH, preferred_element_type=jnp.float32
        )
        out_im = jnp.einsum(
            "yxz,zk->yxk", part_im, cos_t, precision=HIGH, preferred_element_type=jnp.float32
        )
        out_im = out_im - jnp.einsum(
            "yxz,zk->yxk", part_re, sin_t, precision=HIGH, preferred_element_type=jnp.float32
        )
        return (out_re * norm_scale, out_im * norm_scale)

    struct_re, struct_im = along_z(
        (
            lax.all_to_all(second_re, "fft", split_axis=0, concat_axis=2, tiled=True),
            lax.all_to_all(second_im, "fft", split_axis=0, concat_axis=2, tiled=True),
        )
    )
    return (charge_piece, struct_re, struct_im)


def solution(mesh):
    return jax.shard_map(
        on_device,
        mesh=mesh,
        in_specs=(
            P(),
            P(),
            P(("fft", "slab")),
            P(("fft", "slab")),
            P(("fft", "slab")),
            P(None, ("fft", "slab")),
            P(None, ("fft", "slab")),
            P(("fft", "slab")),
            P(None, ("fft", "slab")),
            P(None, ("fft", "slab")),
        ),
        out_specs=(P(("fft", "slab")), P("fft", "slab", None), P("fft", "slab", None)),
        check_vma=False,
    )
```

profile of v0, /device:TPU:1, one launch (start us, length us, event | category | flops | bytes accessed | tf_op | source)
XLA Modules:
  0.0 1523.5 jit_solution(12159098390253261374)
XLA Ops:
  17.4 9.4 fusion.127
  28.7 249.3 %all-reduce.11.cloned.1.call-done = f32[16384]{0:T(1024)} async-done(((f32[16384]{0:T(1024)}), f32[16384]{0:T(1024)}) %all-reduce.11.cloned.1.call-update) | async-done | bytes 65552
  278.8 4.2 fusion.22
  283.0 21.2 %all-reduce.3 = f32[512]{0:T(512)S(1)} all-reduce(f32[512]{0:T(512)S(1)} %bitcast.117), channel_id=2, replica_groups=mesh['fft'=32,'slab'=16] {'slab'}, use_global_device_ids=true, to_apply=%region_2.3.clone | all-reduce | flops 512 | bytes 4096
  305.6 97.7 %all-reduce.6 = (f32[]{:T(128)}, f32[]{:T(128)}) all-reduce(f32[]{:T(128)} %get-tuple-element.28, f32[]{:T(128)} %get-tuple-element.27), channel_id=1, replica_groups=mesh['fft'=32,'slab'=16] {'fft','slab'}, use_global_device_ids=true, to_apply=%region_1.2 | all-reduce | flops 2 | bytes 16 | tf_op jit(solution)/shard_map/psum | solution.py:86
  405.3 93.8 %psum.44 = f32[]{:T(128)} all-reduce(f32[]{:T(128)} %get-tuple-element.37), channel_id=1, replica_groups=mesh['fft'=32,'slab'=16] {'fft','slab'}, use_global_device_ids=true, to_apply=%region_6.7 | all-reduce | flops 1 | bytes 8 | tf_op jit(solution)/shard_map/psum | solution.py:86
  501.5 254.5 %all-reduce.13.cloned.1.call-done = f32[16384]{0:T(1024)} async-done(((f32[16384]{0:T(1024)}), f32[16384]{0:T(1024)}) %all-reduce.13.cloned.1.call-update) | async-done | bytes 65552
  756.7 4.2 fusion.21
  761.0 21.2 %all-reduce.4 = f32[512]{0:T(512)S(1)} all-reduce(f32[512]{0:T(512)S(1)} %bitcast.118), channel_id=3, replica_groups=mesh['fft'=32,'slab'=16] {'slab'}, use_global_device_ids=true, to_apply=%region_7.8.clone | all-reduce | flops 512 | bytes 4096
  782.9 97.6 %psum.45 = f32[]{:T(128)} all-reduce(f32[]{:T(128)} %get-tuple-element.33), channel_id=1, replica_groups=mesh['fft'=32,'slab'=16] {'fft','slab'}, use_global_device_ids=true, to_apply=%region_9.10 | all-reduce | flops 1 | bytes 8 | tf_op jit(solution)/shard_map/psum | solution.py:86
  882.5 93.8 %psum.46 = f32[]{:T(128)} all-reduce(f32[]{:T(128)} %multiply_reduce_fusion), channel_id=1, replica_groups=mesh['fft'=32,'slab'=16] {'fft','slab'}, use_global_device_ids=true, to_apply=%region_11.12 | all-reduce | flops 1 | bytes 8 | tf_op jit(solution)/shard_map/psum | solution.py:86
  978.5 254.8 %all-reduce.15.cloned.1.call-done = f32[16384]{0:T(1024)} async-done(((f32[16384]{0:T(1024)}), f32[16384]{0:T(1024)}) %all-reduce.15.cloned.1.call-update) | async-done | bytes 65552
  1233.9 4.2 fusion.20
  1238.2 21.2 %all-reduce.5 = f32[512]{0:T(512)S(1)} all-reduce(f32[512]{0:T(512)S(1)} %bitcast.116), channel_id=4, replica_groups=mesh['fft'=32,'slab'=16] {'slab'}, use_global_device_ids=true, to_apply=%region_12.13.clone | all-reduce | flops 512 | bytes 4096
  1260.1 98.1 %psum.47 = f32[]{:T(128)} all-reduce(f32[]{:T(128)} %fusion.72), channel_id=1, replica_groups=mesh['fft'=32,'slab'=16] {'fft','slab'}, use_global_device_ids=true, to_apply=%region_14.15 | all-reduce | flops 1 | bytes 8 | tf_op jit(solution)/shard_map/psum | solution.py:86
  1360.6 4.8 broadcast_multiply_fusion
  1365.4 8.9 mul.339
  1374.3 19.6 %fusion = f32[405,384]{1,0:T(8,128)S(1)} fusion(f32[6176,405]{0,1:T(8,128)} %mul.339, f32[6176,384]{1,0:T(8,128)} %fusion.127), kind=kOutput, calls=%fused_computation.1 | convolution fusion | flops 11525898240 | bytes 20113536 | tf_op jit(solution)/shard_map/dot_general | solution.py:68
  1407.6 10.8 all-to-all-start.1
  1423.8 5.5 all-to-all-done.1
  1447.2 4.0 convolution_subtract_fusion.1
  1459.0 4.0 fusion.35
  1463.0 4.8 convolution_add_fusion.1
  1472.2 9.7 all-to-all-start.2
  (132 shorter events, 104.1 us)
Async XLA Ops:
  7.2 270.9 %all-reduce.11.cloned.1.call-start = ((), (), s32[]{:S(2)}) async-start(), calls=%async_computation.4 | async-start | bytes 131072
  8.7 747.4 %all-reduce.13.cloned.1.call-start = ((), (), s32[]{:S(2)}) async-start(), calls=%async_computation.5 | async-start | bytes 131072
  278.8 25.5 %copy-start.12 = (f32[32]{0:T(128)S(1)}, f32[32]{0:T(128)}, u32[]{:S(2)}) copy-start(f32[32]{0:T(128)} %param.12) | copy-start | bytes 388
  278.8 25.5 %copy-start.13 = (f32[32]{0:T(128)S(1)}, f32[32]{0:T(128)}, u32[]{:S(2)}) copy-start(f32[32]{0:T(128)} %param.13) | copy-start | bytes 388
  500.6 0.6 copy-start.6
  501.2 732.0 %all-reduce.15.cloned.1.call-start = ((), (), s32[]{:S(2)}) async-start(), calls=%async_computation.6 | async-start | bytes 131072
  756.7 221.7 %copy-start.14 = (s32[32]{0:T(128)S(1)}, s32[32]{0:T(128)}, u32[]{:S(2)}) copy-start(s32[32]{0:T(128)} %param.17) | copy-start | bytes 388
  977.8 0.6 copy-start.5
  1233.9 125.6 %copy-start.8 = (f32[16384]{0:T(1024)S(1)}, f32[16384]{0:T(1024)}, u32[]{:S(2)}) copy-start(f32[16384]{0:T(1024)} %all-reduce.11.cloned.1.call-done) | copy-start | bytes 196612
  1233.9 125.6 %copy-start.9 = (f32[16384]{0:T(1024)S(1)}, f32[16384]{0:T(1024)}, u32[]{:S(2)}) copy-start(f32[16384]{0:T(1024)} %all-reduce.13.cloned.1.call-done) | copy-start | bytes 196612
  1233.9 125.6 %copy-start.10 = (f32[16384]{0:T(1024)S(1)}, f32[16384]{0:T(1024)}, u32[]{:S(2)}) copy-start(f32[16384]{0:T(1024)} %all-reduce.15.cloned.1.call-done) | copy-start | bytes 196612
  1233.9 126.4 %copy-start.11 = (f32[6144]{0:T(1024)S(1)}, f32[6144]{0:T(1024)}, u32[]{:S(2)}) copy-start(f32[6144]{0:T(1024)} %param.14) | copy-start | bytes 73732
  1394.0 1.6 collective-permute-start
  1395.7 8.8 collective-permute-start.1
  1407.6 21.7 %all-to-all-start.1 = ((f32[16,1,3456]{2,1,0:T(1,128)}), f32[16,1,3456]{2,1,0:T(1,128)S(1)}, u32[]{:S(2)}, u32[]{:S(2)}) async-start(f32[16,1,3456]{2,1,0:T(1,128)} %reshape.779), calls=%async_computation.1 | async-start | bytes 442368 | tf_op jit(solution)/shard_map/all_to_all | solution.py:189
  1429.3 13.9 all-to-all-start
  1436.8 6.4 copy-start.1
  1446.5 0.7 copy-start.4
  1455.1 17.1 %all-to-all-start.3 = ((f32[32,1,1728]{2,1,0:T(1,128)}), f32[32,1,1728]{2,1,0:T(1,128)S(1)}, u32[]{:S(2)}, u32[]{:S(2)}) async-start(f32[32,1,1728]{2,1,0:T(1,128)} %reshape.783), calls=%async_computation.3 | async-start | bytes 458752 | tf_op jit(solution)/shard_map/all_to_all | solution.py:212
  1472.2 9.8 copy-start
  1472.2 24.0 %all-to-all-start.2 = ((f32[32,1,1728]{2,1,0:T(1,128)}), f32[32,1,1728]{2,1,0:T(1,128)}, u32[]{:S(2)}, u32[]{:S(2)}) async-start(f32[32,1,1728]{2,1,0:T(1,128)} %reshape.781), calls=%async_computation.2 | async-start | bytes 458752 | tf_op jit(solution)/shard_map/all_to_all | solution.py:211
  1492.4 3.8 copy-start.2
  1502.7 6.6 copy-start.15
  1506.2 6.8 copy-start.3
  (1 other events, 0.6 us)
Sparse Core Ops, SparseCore 0:
  13.6 264.4 all-reduce.10
  501.3 254.6 all-reduce.12
  978.5 254.6 all-reduce.14
where the time goes:
time: 1530 us; the launch traced here: 1520 us
  waiting for transfers between devices  772 us (50%)
  blocking collectives  545 us (36%)
  matrix products  64.5 us (4%)
  local copies, waits for them, and re-layouts  54 us (4%)
  other arithmetic  35.3 us (2%)
  starting transfers between devices  31.5 us (2%)
  between operations  21.8 us (1%)
    unnamed x6, waiting for transfers between devices  759 us
    psum x5, blocking collectives, ml_total(): return lax.psum(value, ('fft', 'slab'))  481 us
    unnamed x3, blocking collectives  63.7 us
  transfers between devices with their start and end apart: 9, of which 7 were waited for; matrix products, arithmetic and copies ran while one was open for 4% of the time, Pallas kernels for 0%

commit v1 on v0

v1 whole, which is shorter than its diff:
```python
import math

import jax
import jax.numpy as jnp
import numpy as np
from jax import lax
from jax.experimental import pallas as pl
from jax.experimental.pallas import tpu as pltpu
from jax.sharding import PartitionSpec as P

NG = 384
N_FFT = 32
N_SLAB = 16
YL = 24
ZL = 12
KX = 12
KY = 12
OWN = 32
ROWS = 512
COLS = 1024
ATOMS = 16384
SITES = 6144
CHUNK = 1024
XE = 392
YE = 32
ZE = 15

KE = 14.4
ALPHA = 0.08
SOFT = 0.01
SQPI = math.sqrt(math.pi)
F32 = jnp.float32
BF16 = jnp.bfloat16
VMEM_LIMIT = 48 * 1024 * 1024


def wave(points, freqs):
    angle = 2.0 * np.pi * ((points[:, None] * freqs[None, :]) % NG) / NG
    return np.cos(angle), np.sin(angle)


def two_parts(table):
    high = np.asarray(table, np.float32).astype(jnp.bfloat16)
    low = (np.asarray(table, np.float64) - high.astype(np.float64)).astype(jnp.bfloat16)
    return high, low


def x_table():
    points = np.arange(XE)
    cos, sin = wave(points, np.arange(NG // 2))
    cos, sin = (t.reshape(XE, N_SLAB, 1, KX) for t in (cos, sin))
    table = np.concatenate([cos, -sin], 2)
    table = table * (points < NG + 3)[:, None, None, None]
    return table.reshape(XE, N_SLAB * 2 * KX)


def y_tables():
    local = np.arange(YE)
    points = (np.arange(N_SLAB)[:, None] * YL + local[None, :]).reshape(-1)
    used = np.tile(local < YL + 3, N_SLAB)[:, None, None, None]
    cos, sin = wave(points, np.arange(NG))
    cos, sin = (t.reshape(-1, N_FFT, 1, KY) for t in (cos, sin))
    from_re = np.concatenate([cos, -sin], 2) * used
    from_im = np.concatenate([sin, cos], 2) * used
    return from_re.reshape(-1, 2 * NG), from_im.reshape(-1, 2 * NG)


def z_tables():
    local = np.arange(16)
    points = (np.arange(N_FFT)[:, None] * ZL + local[None, :]).reshape(-1)
    used = np.tile(local < ZL + 3, N_FFT)[:, None]
    scale = 1.0 / (NG * math.sqrt(NG))
    cos, sin = wave(points, np.arange(NG))
    from_re = np.concatenate([cos, -sin], 1) * used * scale
    from_im = np.concatenate([sin, cos], 1) * used * scale
    return from_re, from_im


def perm_y():
    table = np.zeros((2, KX, 16, 384), np.float32)
    for c in range(2):
        for k in range(KX):
            for z in range(ZE):
                table[c, k, z, z * 24 + c * KX + k] = 1.0
    return table.reshape(384, 384).astype(jnp.bfloat16)


def perm_z():
    table = np.zeros((2, KY, 16, 384), np.float32)
    for c in range(2):
        for k in range(KY):
            for x in range(KX):
                table[c, k, x, x * 24 + c * KY + k] = 1.0
    return table.reshape(384, 384).astype(jnp.bfloat16)


def split(value):
    high = value.astype(BF16)
    return high, (value - high.astype(F32)).astype(BF16)


def dot_nn(a, b):
    return lax.dot_general(a, b, (((1,), (0,)), ((), ())), preferred_element_type=F32)


def dot_nt(a, b):
    return lax.dot_general(a, b, (((1,), (1,)), ((), ())), preferred_element_type=F32)


def three(dot, a, b):
    return dot(a[0], b[0]) + dot(a[0], b[1]) + dot(a[1], b[0])


def spline(u):
    squared = u * u
    cubed = squared * u
    rest = 1.0 - u
    return (
        rest * rest * rest / 6.0,
        (3.0 * cubed - 6.0 * squared + 4.0) / 6.0,
        (-3.0 * cubed + 3.0 * squared + 3.0 * u + 1.0) / 6.0,
        cubed / 6.0,
    )


def placed(rows, cell, weights):
    off = lax.broadcasted_iota(jnp.int32, (rows, cell.shape[1]), 0) - cell
    value = jnp.where(off == 3, weights[3], 0.0)
    value = jnp.where(off == 2, weights[2], value)
    value = jnp.where(off == 1, weights[1], value)
    return jnp.where(off == 0, weights[0], value)


def spread_body(charge, frac, cell, xh, xl, out, acc):
    step = pl.program_id(0)

    @pl.when(step == 0)
    def _():
        acc[...] = jnp.zeros_like(acc)

    along_x = placed(XE, cell[0:1, :], spline(frac[0:1, :]))
    along_y = placed(YE, cell[1:2, :], spline(frac[1:2, :])) * charge[...]
    along_z = placed(16, cell[2:3, :], spline(frac[2:3, :]))
    plane = jnp.concatenate([along_z[z : z + 1, :] * along_y for z in range(ZE)], 0)
    acc[...] += three(dot_nt, split(plane), split(along_x))

    @pl.when(step == pl.num_programs(0) - 1)
    def _():
        freq = three(dot_nn, split(acc[...]), (xh[...], xl[...]))
        for s in range(N_SLAB):
            for z in range(ZE):
                out[s, :, z * 24 : z * 24 + 24] = freq[z * YE : z * YE + YE, s * 24 : s * 24 + 24]
            out[s, :, ZE * 24 : 384] = jnp.zeros((YE, 384 - ZE * 24), F32)


def spread(charge, frac, cell, xh, xl):
    whole = pl.BlockSpec((XE, 384), lambda i: (0, 0))
    return pl.pallas_call(
        spread_body,
        grid=(SITES // CHUNK,),
        in_specs=[
            pl.BlockSpec((1, CHUNK), lambda i: (0, i)),
            pl.BlockSpec((3, CHUNK), lambda i: (0, i)),
            pl.BlockSpec((3, CHUNK), lambda i: (0, i)),
            whole,
            whole,
        ],
        out_specs=pl.BlockSpec((N_SLAB, YE, 384), lambda i: (0, 0, 0)),
        out_shape=jax.ShapeDtypeStruct((N_SLAB, YE, 384), F32),
        scratch_shapes=[pltpu.VMEM((ZE * YE, XE), F32)],
        compiler_params=pltpu.CompilerParams(vmem_limit_bytes=VMEM_LIMIT),
        cost_estimate=pl.CostEstimate(flops=8_000_000_000, bytes_accessed=2_000_000, transcendentals=0),
        name="spread",
    )(charge.reshape(1, SITES), frac, cell, xh, xl)


def y_body(grid, charges, slots, xsh, xsl, perm, arh, arl, aih, ail, out):
    atom = slots[0:1, :].astype(jnp.int32)
    cell = slots[1:4, :].astype(jnp.int32)
    frac = slots[4:7, :]
    lane = lax.broadcasted_iota(jnp.int32, (128, ROWS), 0)
    pick = jnp.where(lane == atom % 128, 1.0, 0.0).astype(BF16)
    q_high, q_low = split(charges[...])
    rows = dot_nn(q_high, pick) + dot_nn(q_low, pick)
    charge = jnp.sum(jnp.where(lane == atom // 128, rows, 0.0), 0, keepdims=True)
    block = lax.broadcasted_iota(jnp.int32, (1, ROWS), 1) // OWN * YE
    along_y = placed(N_SLAB * YE, cell[1:2, :] + block, spline(frac[1:2, :]))
    along_z = placed(16, cell[2:3, :], spline(frac[2:3, :])) * charge
    along_x = placed(XE, cell[0:1, :], spline(frac[0:1, :]))
    wave_x = three(dot_nn, (xsh[...], xsl[...]), split(along_x))
    both = [along_z[z : z + 1, :] * wave_x for z in range(ZE)]
    both = jnp.concatenate(both + [jnp.zeros((24, ROWS), F32)], 0)
    total = grid[...] + three(dot_nt, split(along_y), split(both))
    high, low = split(total)
    high = dot_nt(perm[...], high).astype(BF16)
    low = dot_nt(perm[...], low).astype(BF16)
    freq = three(dot_nn, (high[:192], low[:192]), (arh[...], arl[...]))
    freq = freq + three(dot_nn, (high[192:], low[192:]), (aih[...], ail[...]))
    for f in range(N_FFT):
        for k in range(KX):
            out[f, :, k * 24 : k * 24 + 24] = freq[k * 16 : k * 16 + 16, f * 24 : f * 24 + 24]
        out[f, :, KX * 24 : 384] = jnp.zeros((16, 384 - KX * 24), F32)


def along_y(*operands):
    return pl.pallas_call(
        y_body,
        out_shape=jax.ShapeDtypeStruct((N_FFT, 16, 384), F32),
        compiler_params=pltpu.CompilerParams(vmem_limit_bytes=VMEM_LIMIT),
        cost_estimate=pl.CostEstimate(flops=4_000_000_000, bytes_accessed=5_000_000, transcendentals=0),
        name="along_y",
    )(*operands)


def z_body(grid, perm, brh, brl, bih, bil, out_re, out_im):
    high, low = split(grid[...])
    high = dot_nt(perm[...], high).astype(BF16)
    low = dot_nt(perm[...], low).astype(BF16)
    freq = three(dot_nn, (high[:192], low[:192]), (brh[...], brl[...]))
    freq = freq + three(dot_nn, (high[192:], low[192:]), (bih[...], bil[...]))
    for k in range(KY):
        out_re[k] = freq[k * 16 : k * 16 + KX, :NG]
        out_im[k] = freq[k * 16 : k * 16 + KX, NG:]


def along_z(*operands):
    shape = jax.ShapeDtypeStruct((KY, KX, NG), F32)
    return pl.pallas_call(
        z_body,
        out_shape=(shape, shape),
        compiler_params=pltpu.CompilerParams(vmem_limit_bytes=VMEM_LIMIT),
        cost_estimate=pl.CostEstimate(flops=3_000_000_000, bytes_accessed=5_000_000, transcendentals=0),
        name="along_z",
    )(*operands)


def couplings(row_pos, row_width, col_pos, col_width, row_ids, col_ids, col_diag):
    dist_sq = (row_pos[0][:, None] - col_pos[0][None, :]) ** 2
    dist_sq = dist_sq + (row_pos[1][:, None] - col_pos[1][None, :]) ** 2
    dist_sq = dist_sq + (row_pos[2][:, None] - col_pos[2][None, :]) ** 2
    distance = jnp.sqrt(dist_sq + SOFT)
    pair_len = jnp.sqrt(2.0 * (row_width[:, None] ** 2 + col_width[None, :] ** 2))
    kernel = KE * (lax.erf(distance / pair_len) - lax.erf(ALPHA * distance)) / distance
    return jnp.where(row_ids[:, None] == col_ids[None, :], col_diag[None, :], kernel)


def swap(value, axis):
    return lax.all_to_all(value, axis, 0, 0, tiled=True)


def to_all(value, axis):
    return swap(jnp.broadcast_to(value[None], (lax.axis_size(axis),) + value.shape), axis)


def guarded(value, pivot, scale):
    good = pivot > 1e-6 * scale
    return jnp.where(good, value / jnp.where(good, pivot, 1.0), 0.0)


def galerkin(m):
    l10 = m[2] / m[1]
    l20 = m[3] / m[1]
    d1 = m[3] - l10 * m[2]
    e12 = m[4] - l10 * m[3]
    l21 = guarded(e12, d1, m[3])
    d2 = (m[5] - l20 * m[3]) - l21 * e12
    g1 = m[1] - l10 * m[0]
    g2 = (m[2] - l20 * m[0]) - l21 * g1
    c2 = guarded(g2, d2, m[5])
    c1 = guarded(g1, d1, m[3]) - l21 * c2
    c0 = m[0] / m[1] - l10 * c1 - l20 * c2
    return c0, c1, c2


def on_device(
    ml_pos,
    ml_width,
    ml_drive,
    ml_hard,
    mm_charge,
    mm_frac,
    mm_cell,
    slot_atom,
    slot_frac,
    slot_cell,
):
    f = lax.axis_index("fft")
    s = lax.axis_index("slab")

    def rows_of(value):
        return lax.dynamic_index_in_dim(value.reshape(N_FFT, ROWS), f, 0, False)

    def cols_of(value):
        value = value.reshape(N_FFT, N_SLAB, OWN)
        return lax.dynamic_index_in_dim(value, s, 1, False).reshape(COLS)

    drive = -ml_drive
    slots = jnp.concatenate(
        [
            drive[None],
            slot_atom.astype(F32)[None],
            slot_cell.astype(F32),
            slot_frac,
        ],
        0,
    )
    got = to_all(slots, "slab")
    got = jnp.transpose(got, (1, 0, 2)).reshape(8, ROWS)
    drive_rows = got[0]

    ids = jnp.arange(ATOMS, dtype=jnp.int32)
    own_first = f * ROWS + s * OWN
    own_width = lax.dynamic_slice_in_dim(ml_width, own_first, OWN)
    own_diag = ml_hard + KE * (1.0 / (own_width * SQPI) - 2.0 * ALPHA / SQPI)
    col_diag = lax.dynamic_update_slice_in_dim(jnp.zeros((COLS,), F32), own_diag, f * OWN, 0)
    matrix = couplings(
        [rows_of(ml_pos[i]) for i in range(3)],
        rows_of(ml_width),
        [cols_of(ml_pos[i]) for i in range(3)],
        cols_of(ml_width),
        rows_of(ids),
        cols_of(ids),
        col_diag,
    )
    part = jnp.sum(matrix * drive_rows[:, None], 0)
    got_1 = to_all(jnp.concatenate([part, drive_rows]), "fft")
    first_cols = jnp.sum(got_1[:, :COLS], 0)
    drive_full = got_1[:, COLS:].reshape(ATOMS)

    xh, xl = (jnp.asarray(t) for t in two_parts(x_table()))
    mm = spread(mm_charge, mm_frac, mm_cell, xh, xl)
    part = jnp.sum(matrix * first_cols[None, :], 1)
    tail = jnp.concatenate([part, first_cols]).reshape(1, 4, 384)
    tail = jnp.broadcast_to(tail, (N_SLAB, 4, 384))
    got_2 = swap(jnp.concatenate([mm[:, : YE - 4], tail], 1), "slab")
    tail = got_2[:, YE - 4 :].reshape(N_SLAB, 1536)
    second_rows = jnp.sum(tail[:, :ROWS], 0)
    first_full = jnp.transpose(tail[:, ROWS:].reshape(N_SLAB, N_FFT, OWN), (1, 0, 2)).reshape(ATOMS)

    second_full = to_all(second_rows, "fft").reshape(ATOMS)
    second_cols = cols_of(second_full)
    quad = jnp.sum(second_rows * jnp.sum(matrix * second_cols[None, :], 1))
    quad = jnp.sum(to_all(jnp.full((128,), quad), "slab")[:, 0])
    quad = jnp.sum(to_all(jnp.full((128,), quad), "fft")[:, 0])
    moments = [
        jnp.sum(drive_full * drive_full),
        jnp.sum(drive_full * first_full),
        jnp.sum(first_full * first_full),
        jnp.sum(first_full * second_full),
        jnp.sum(second_full * second_full),
        quad,
    ]
    c0, c1, c2 = galerkin(moments)
    charge = c0 * drive_full + c1 * first_full + c2 * second_full
    charge_piece = lax.dynamic_slice_in_dim(charge, own_first, OWN)

    xs = x_table().T.reshape(N_SLAB, 24, XE)
    xsh, xsl = (lax.dynamic_index_in_dim(jnp.asarray(t), s, 0, False) for t in two_parts(xs))
    arh, arl, aih, ail = (jnp.asarray(t) for part in y_tables() for t in two_parts(part))
    spectrum = along_y(
        got_2.reshape(N_SLAB * YE, 384),
        charge.reshape(128, 128),
        got[1:8],
        xsh,
        xsl,
        jnp.asarray(perm_y()),
        arh,
        arl,
        aih,
        ail,
    )
    spectrum = swap(spectrum, "fft").reshape(N_FFT * 16, 384)
    brh, brl, bih, bil = (jnp.asarray(t) for part in z_tables() for t in two_parts(part))
    struct_re, struct_im = along_z(spectrum, jnp.asarray(perm_z()), brh, brl, bih, bil)
    return (charge_piece, struct_re, struct_im)


def solution(mesh):
    return jax.shard_map(
        on_device,
        mesh=mesh,
        in_specs=(
            P(),
            P(),
            P(("fft", "slab")),
            P(("fft", "slab")),
            P(("fft", "slab")),
            P(None, ("fft", "slab")),
            P(None, ("fft", "slab")),
            P(("fft", "slab")),
            P(None, ("fft", "slab")),
            P(None, ("fft", "slab")),
        ),
        out_specs=(P(("fft", "slab")), P("fft", "slab", None), P("fft", "slab", None)),
        check_vma=False,
    )
```

time: 1530 us -> 185 us (0.12)
  waiting for transfers between devices: 772 us -> 31.6 us
  blocking collectives: 545 us -> 27.2 us
  matrix products: 64.5 us -> 0 us
  local copies, waits for them, and re-layouts: 54 us -> 18.2 us
  Pallas kernels: 0 us -> 22.6 us
  starting transfers between devices: 31.5 us -> 48.9 us
    unnamed x6 -> x0, waiting for transfers between devices: 759 us -> none
    psum x5 -> x0, blocking collectives: 481 us -> none  [ml_total(): return lax.psum(value, ('fft', 'slab'))]
    dot_general x14 -> x0, matrix products: 64.5 us -> none  [the longest x1 19.6 us: spread_sites(): lax.dot_general(yz_plane, along_x, (((0,), (0,)), ((), ())), precision=HI...]
    unnamed x3 -> x0, blocking collectives: 63.7 us -> none
    all_to_all x0 -> x1, blocking collectives: none -> 27.2 us  [swap(): return lax.all_to_all(value, axis, 0, 0, tiled=True)]
    all_to_all x4 -> x6, waiting for transfers between devices: 8.2 us -> 31.6 us  [swap(): return lax.all_to_all(value, axis, 0, 0, tiled=True)]
    pallas_call x0 -> x3, Pallas kernels: none -> 22.6 us  [the longest x1 15 us: spread(): pl.pallas_call(spread_body, grid=(SITES // CHUNK,), in_specs=[pl.BlockSpe...]
    all_to_all x4 -> x6, starting transfers between devices: 28 us -> 48.9 us  [swap(): return lax.all_to_all(value, axis, 0, 0, tiled=True)]
  transfers between devices with their start and end apart: 9 -> 6, of which waited for: 7 -> 4; matrix products, arithmetic and copies ran while one was open for 4% -> 6% of each run, Pallas kernels for 0% -> 8%
where the time goes in v1:
time: 185 us; the launch traced here: 181 us
  starting transfers between devices  48.9 us (26%)
  waiting for transfers between devices  31.6 us (17%)
  blocking collectives  27.2 us (15%)
  Pallas kernels  22.6 us (12%)
  other arithmetic  20.1 us (11%)
  local copies, waits for them, and re-layouts  18.2 us (10%)
  between operations  12.9 us (7%)
    all_to_all x6, starting transfers between devices, swap(): return lax.all_to_all(value, axis, 0, 0, tiled=True)  48.9 us
    all_to_all x6, waiting for transfers between devices, swap(): return lax.all_to_all(value, axis, 0, 0, tiled=True)  31.6 us
    all_to_all x1, blocking collectives, swap(): return lax.all_to_all(value, axis, 0, 0, tiled=True)  27.2 us
    pallas_call x1, Pallas kernels, spread(): pl.pallas_call(spread_body, grid=(SITES // CHUNK,), in_specs=[pl.BlockSpe...  15 us
    unnamed x45, local copies, waits for them, and re-layouts  6.31 us
    pallas_call x1, Pallas kernels, along_y(): pl.pallas_call(y_body, out_shape=jax.ShapeDtypeStruct((N_FFT, 16, 384), F...  5.08 us
    reduce_sum x2, other arithmetic, on_device(): quad = jnp.sum(second_rows * jnp.sum(matrix * second_cols[None, :], 1))  3.96 us
  transfers between devices with their start and end apart: 6, of which 4 were waited for; matrix products, arithmetic and copies ran while one was open for 6% of the time, Pallas kernels for 8%

profile of v1, /device:TPU:1, one launch (start us, length us, event | category | flops | bytes accessed | tf_op | source)
XLA Modules:
  0.0 181.4 jit_solution(11819018024254034929)
XLA Ops:
  4.1 10.2 %all-to-all-start = ((f32[16,1,256]{2,1,0:T(1,128)}), f32[16,1,256]{2,1,0:T(1,128)S(1)}, u32[]{:S(2)}, u32[]{:S(2)}) async-start(f32[16,1,256]{2,1,0:T(1,128)} %reshape.250), calls=%async_computation | async-start | bytes 32768 | tf_op jit(solution)/shard_map/all_to_all | solution.py:248
  15.1 1.9 %slice_reduce_fusion.7 = (f32[16384]{0:T(1024)S(1)}, f32[16384]{0:T(1024)S(1)}, f32[16384]{0:T(1024)S(1)}, f32[1,16384]{1,0:T(1,128)S(1)}, f32[1,16384]{1,0:T(1,128)S(1)}, /*index=5*/f32[1,16384]{1,0:T(1,128)S(1)}) fusion(f32[3,16384]{1,0:T(4,128)} %param.24), kind=kLoop, calls=%fused_computation.52 | loop fusion | bytes 589824 | tf_op jit(solution)/shard_map/slice | solution.py:317
  18.5 3.2 %all-to-all-done = f32[16,1,256]{2,1,0:T(1,128)S(1)} async-done(((f32[16,1,256]{2,1,0:T(1,128)}), f32[16,1,256]{2,1,0:T(1,128)S(1)}, u32[]{:S(2)}, u32[]{:S(2)}) %all-to-all-start) | async-done | bytes 16416 | tf_op jit(solution)/shard_map/all_to_all | solution.py:248
  23.1 3.3 %multiply_reduce_fusion.2 = f32[1024]{0:T(1024)S(1)} fusion(f32[512]{0:T(512)S(1)} %mul.180, f32[1024]{0:T(1024)S(1)} %integer_pow.37, f32[512]{0:T(512)S(1)} %bitcast.65, f32[1024]{0:T(1024)S(1)} %sub.101, f32[512]{0:T(512)S(1)} %bitcast.68, f32[1024]{0:T(1024)S(1)} %sub.96, f32[512]{0:T(512)S(1)} %bitcast.71, f32[1024]{0:T(1024)S(1)} %sub.91, ...), kind=kLoop, calls=%fused_computation.3 | loop fusion | flops 10484736 | bytes 40960 | tf_op jit(solution)/shard_map/reduce_sum | solution.py:325
  27.2 11.3 %all-to-all-start.1 = ((f32[32,1,1536]{2,1,0:T(1,128)}), f32[32,1,1536]{2,1,0:T(1,128)S(1)}, u32[]{:S(2)}, u32[]{:S(2)}) async-start(f32[32,1,1536]{2,1,0:T(1,128)} %broadcast_in_dim.29), calls=%async_computation.1 | async-start | bytes 393216 | tf_op jit(solution)/shard_map/all_to_all | solution.py:248
  38.5 15.0 %spread.1 = f32[16,32,384]{2,1,0:T(8,128)S(1)} custom-call(f32[1,6144]{1,0:T(1,128)S(1)} %bitcast.42, f32[3,6144]{1,0:T(4,128)S(1)} %copy-done, s32[3,6144]{1,0:T(4,128)S(1)} %copy-done.1, bf16[392,384]{1,0:T(8,128)(2,1)S(1)} %copy-done.12, bf16[392,384]{1,0:T(8,128)(2,1)S(1)} %copy-done.11), custom_call_target="tpu_custom_call" | custom-call | flops 8000000000 | bytes 2000000 | tf_op jit(solution)/shard_map/spread/pallas_call | solution.py:158
  53.6 3.3 %multiply_reduce_fusion.1 = f32[512]{0:T(512)S(1)} fusion(f32[1024]{0:T(1024)S(1)} %slice_reduce_fusion, f32[1024]{0:T(1024)S(1)} %integer_pow.37, f32[512]{0:T(512)S(1)} %bitcast.66, f32[1024]{0:T(1024)S(1)} %sub.101, f32[512]{0:T(512)S(1)} %bitcast.69, f32[1024]{0:T(1024)S(1)} %sub.96, f32[512]{0:T(512)S(1)} %bitcast.72, f32[1024]{0:T(1024)S(1)} %sub.91, ...), kind=kLoop, calls=%fused_computation.2 | loop fusion | flops 10485248 | bytes 40960 | tf_op jit(solution)/shard_map/reduce_sum | solution.py:332
  57.0 27.2 %all_to_all.48 = f32[16,32,384]{2,1,0:T(8,128)S(1)} all-to-all(f32[16,32,384]{2,1,0:T(8,128)S(1)} %pad_maximum_fusion), channel_id=1, replica_groups=mesh['fft'=32,'slab'=16] {'slab'}, dimensions={0} | all-to-all | bytes 1572864 | tf_op jit(solution)/shard_map/all_to_all | solution.py:248
  84.9 9.5 %all-to-all-start.3 = ((f32[32,1,512]{2,1,0:T(1,128)}), f32[32,1,512]{2,1,0:T(1,128)S(1)}, u32[]{:S(2)}, u32[]{:S(2)}) async-start(f32[32,1,512]{2,1,0:T(1,128)} %broadcast_in_dim.57), calls=%async_computation.3 | async-start | bytes 131072 | tf_op jit(solution)/shard_map/all_to_all | solution.py:248
  95.7 7.5 %all-to-all-done.3 = f32[32,1,512]{2,1,0:T(1,128)S(1)} async-done(((f32[32,1,512]{2,1,0:T(1,128)}), f32[32,1,512]{2,1,0:T(1,128)S(1)}, u32[]{:S(2)}, u32[]{:S(2)}) %all-to-all-start.3) | async-done | bytes 65568 | tf_op jit(solution)/shard_map/all_to_all | solution.py:248
  104.3 3.3 %multiply_reduce_fusion = f32[512]{0:T(512)S(1)} fusion(f32[1024]{0:T(1024)S(1)} %mul.194, f32[1024]{0:T(1024)S(1)} %integer_pow.37, f32[512]{0:T(512)S(1)} %bitcast.67, f32[1024]{0:T(1024)S(1)} %sub.101, f32[512]{0:T(512)S(1)} %bitcast.70, f32[1024]{0:T(1024)S(1)} %sub.96, f32[512]{0:T(512)S(1)} %bitcast.73, f32[1024]{0:T(1024)S(1)} %sub.91, ...), kind=kLoop, calls=%fused_computation.1 | loop fusion | flops 10485248 | bytes 40960 | tf_op jit(solution)/shard_map/reduce_sum | solution.py:342
  108.3 1.3 broadcast_in_dim_broadcast_in_dim_broadcast_in_dim.6
  109.6 4.7 %all-to-all-start.4 = ((f32[16,1,128]{2,1,0:T(1,128)}), f32[16,1,128]{2,1,0:T(1,128)S(1)}, u32[]{:S(2)}, u32[]{:S(2)}) async-start(f32[16,1,128]{2,1,0:T(1,128)} %broadcast_in_dim_broadcast_in_dim_broadcast_in_dim.6), calls=%async_computation.4 | async-start | bytes 16384 | tf_op jit(solution)/shard_map/all_to_all | solution.py:248
  116.3 5.0 %all-to-all-done.4 = f32[16,1,128]{2,1,0:T(1,128)S(1)} async-done(((f32[16,1,128]{2,1,0:T(1,128)}), f32[16,1,128]{2,1,0:T(1,128)S(1)}, u32[]{:S(2)}, u32[]{:S(2)}) %all-to-all-start.4) | async-done | bytes 8224 | tf_op jit(solution)/shard_map/all_to_all | solution.py:248
  121.9 1.2 broadcast_in_dim_broadcast_in_dim_broadcast_in_dim.7
  123.2 4.0 %all-to-all-start.5 = ((f32[32,1,128]{2,1,0:T(1,128)}), f32[32,1,128]{2,1,0:T(1,128)S(1)}, u32[]{:S(2)}, u32[]{:S(2)}) async-start(f32[32,1,128]{2,1,0:T(1,128)} %broadcast_in_dim_broadcast_in_dim_broadcast_in_dim.7), calls=%async_computation.5 | async-start | bytes 32768 | tf_op jit(solution)/shard_map/all_to_all | solution.py:248
  140.3 1.1 copy-done.8
  141.5 1.1 copy-done.9
  143.7 5.1 %along_y.1 = f32[32,16,384]{2,1,0:T(8,128)} custom-call(f32[512,384]{1,0:T(8,128)S(1)} %bitcast.39, f32[128,128]{1,0:T(8,128)S(1)} %add_add_fusion.charges, f32[7,512]{1,0:T(8,128)S(1)} %slice.59.slots, bf16[24,392]{1,0:T(8,128)(2,1)S(1)} %get-tuple-element.24.xsh, bf16[24,392]{1,0:T(8,128)(2,1)S(1)} %get-tuple-element.23.xsl, ...), custom_call_target="tpu_custom_call" | custom-call | flops 4000000000 | bytes 5000000 | tf_op jit(solution)/shard_map/along_y/pallas_call | solution.py:206
  148.8 9.2 %all-to-all-start.6 = ((f32[32,16,384]{2,1,0:T(8,128)}), f32[32,16,384]{2,1,0:T(8,128)S(1)}, u32[]{:S(2)}, u32[]{:S(2)}) async-start(f32[32,16,384]{2,1,0:T(8,128)} %along_y.1), calls=%async_computation.6 | async-start | bytes 1572864 | tf_op jit(solution)/shard_map/all_to_all | solution.py:248
  158.0 1.7 mul.211
  160.6 1.3 dynamic-slice_add_fusion
  161.9 15.9 %all-to-all-done.6 = f32[32,16,384]{2,1,0:T(8,128)S(1)} async-done(((f32[32,16,384]{2,1,0:T(8,128)}), f32[32,16,384]{2,1,0:T(8,128)S(1)}, u32[]{:S(2)}, u32[]{:S(2)}) %all-to-all-start.6) | async-done | bytes 786464 | tf_op jit(solution)/shard_map/all_to_all | solution.py:248
  178.9 2.5 %along_z.1 = (f32[12,12,384]{2,1,0:T(8,128)}, f32[12,12,384]{2,1,0:T(8,128)}) custom-call(f32[512,384]{1,0:T(8,128)S(1)} %bitcast.40, bf16[384,384]{1,0:T(8,128)(2,1)S(1)} %copy-done.13, bf16[512,768]{1,0:T(8,128)(2,1)S(1)} %copy-done.6, bf16[512,768]{1,0:T(8,128)(2,1)S(1)} %copy-done.5, bf16[512,768]{1,0:T(8,128)(2,1)S(1)} %copy-done.4, ...), custom_call_target="tpu_custom_call" | custom-call | flops 3000000000 | bytes 5000000 | tf_op jit(solution)/shard_map/along_z/pallas_call | solution.py:228
  (110 shorter events, 18.8 us)
Async XLA Ops:
  0.6 16.5 %copy-start.17 = (f32[16384]{0:T(1024)S(1)}, f32[16384]{0:T(1024)}, u32[]{:S(2)}) copy-start(f32[16384]{0:T(1024)} %param.25) | copy-start | bytes 196612
  0.6 16.5 %copy-start.19 = (f32[32]{0:T(128)S(1)}, f32[32]{0:T(128)}, u32[]{:S(2)}) copy-start(f32[32]{0:T(128)} %param.27) | copy-start | bytes 388
  4.1 17.6 %all-to-all-start = ((f32[16,1,256]{2,1,0:T(1,128)}), f32[16,1,256]{2,1,0:T(1,128)S(1)}, u32[]{:S(2)}, u32[]{:S(2)}) async-start(f32[16,1,256]{2,1,0:T(1,128)} %reshape.250), calls=%async_computation | async-start | bytes 32768 | tf_op jit(solution)/shard_map/all_to_all | solution.py:248
  23.1 15.4 %copy-start = (f32[3,6144]{1,0:T(4,128)S(1)}, f32[3,6144]{1,0:T(4,128)}, u32[]{:S(2)}) copy-start(f32[3,6144]{1,0:T(4,128)} %frac.1) | copy-start | bytes 221188
  23.1 15.4 %copy-start.1 = (s32[3,6144]{1,0:T(4,128)S(1)}, s32[3,6144]{1,0:T(4,128)}, u32[]{:S(2)}) copy-start(s32[3,6144]{1,0:T(4,128)} %cell.1) | copy-start | bytes 221188
  23.1 15.4 %copy-start.2 = (f32[6144]{0:T(1024)S(1)}, f32[6144]{0:T(1024)}, u32[]{:S(2)}) copy-start(f32[6144]{0:T(1024)} %param.28) | copy-start | bytes 73732
  23.1 15.4 %copy-start.11 = (bf16[392,384]{1,0:T(8,128)(2,1)S(1)}, bf16[392,384]{1,0:T(8,128)(2,1)}, u32[]{:S(2)}) copy-start(bf16[392,384]{1,0:T(8,128)(2,1)} %constant.112.clone.xl) | copy-start | bytes 903172
  23.1 15.4 %copy-start.12 = (bf16[392,384]{1,0:T(8,128)(2,1)S(1)}, bf16[392,384]{1,0:T(8,128)(2,1)}, u32[]{:S(2)}) copy-start(bf16[392,384]{1,0:T(8,128)(2,1)} %constant.111.clone.xh) | copy-start | bytes 903172
  27.2 26.4 %all-to-all-start.1 = ((f32[32,1,1536]{2,1,0:T(1,128)}), f32[32,1,1536]{2,1,0:T(1,128)S(1)}, u32[]{:S(2)}, u32[]{:S(2)}) async-start(f32[32,1,1536]{2,1,0:T(1,128)} %broadcast_in_dim.29), calls=%async_computation.1 | async-start | bytes 393216 | tf_op jit(solution)/shard_map/all_to_all | solution.py:248
  53.5 85.8 %copy-start.16 = (f32[32,1,1536]{2,0,1:T(8,128)}, f32[32,1,1536]{2,0,1:T(8,128)S(1)}, u32[]{:S(2)}) copy-start(f32[32,1,1536]{2,0,1:T(8,128)S(1)} %copy.58) | copy-start | bytes 589828
  84.9 18.4 %all-to-all-start.3 = ((f32[32,1,512]{2,1,0:T(1,128)}), f32[32,1,512]{2,1,0:T(1,128)S(1)}, u32[]{:S(2)}, u32[]{:S(2)}) async-start(f32[32,1,512]{2,1,0:T(1,128)} %broadcast_in_dim.57), calls=%async_computation.3 | async-start | bytes 131072 | tf_op jit(solution)/shard_map/all_to_all | solution.py:248
  109.6 11.7 %all-to-all-start.4 = ((f32[16,1,128]{2,1,0:T(1,128)}), f32[16,1,128]{2,1,0:T(1,128)S(1)}, u32[]{:S(2)}, u32[]{:S(2)}) async-start(f32[16,1,128]{2,1,0:T(1,128)} %broadcast_in_dim_broadcast_in_dim_broadcast_in_dim.6), calls=%async_computation.4 | async-start | bytes 16384 | tf_op jit(solution)/shard_map/all_to_all | solution.py:248
  123.2 13.9 %all-to-all-start.5 = ((f32[32,1,128]{2,1,0:T(1,128)}), f32[32,1,128]{2,1,0:T(1,128)S(1)}, u32[]{:S(2)}, u32[]{:S(2)}) async-start(f32[32,1,128]{2,1,0:T(1,128)} %broadcast_in_dim_broadcast_in_dim_broadcast_in_dim.7), calls=%async_computation.5 | async-start | bytes 32768 | tf_op jit(solution)/shard_map/all_to_all | solution.py:248
  139.0 1.2 copy-start.7
  139.0 1.3 copy-start.14
  140.3 1.1 copy-start.8
  141.5 1.1 copy-start.9
  142.6 1.1 copy-start.10
  143.7 34.0 %copy-start.5 = (bf16[512,768]{1,0:T(8,128)(2,1)S(1)}, bf16[512,768]{1,0:T(8,128)(2,1)}, u32[]{:S(2)}) copy-start(bf16[512,768]{1,0:T(8,128)(2,1)} %constant.121.clone.brl) | copy-start | bytes 2359300
  148.8 28.9 %copy-start.3 = (bf16[512,768]{1,0:T(8,128)(2,1)S(1)}, bf16[512,768]{1,0:T(8,128)(2,1)}, u32[]{:S(2)}) copy-start(bf16[512,768]{1,0:T(8,128)(2,1)} %constant.123.clone.bil) | copy-start | bytes 2359300
  148.8 28.9 %copy-start.4 = (bf16[512,768]{1,0:T(8,128)(2,1)S(1)}, bf16[512,768]{1,0:T(8,128)(2,1)}, u32[]{:S(2)}) copy-start(bf16[512,768]{1,0:T(8,128)(2,1)} %constant.122.clone.bih) | copy-start | bytes 2359300
  148.8 28.9 %copy-start.13 = (bf16[384,384]{1,0:T(8,128)(2,1)S(1)}, bf16[384,384]{1,0:T(8,128)(2,1)}, u32[]{:S(2)}) copy-start(bf16[384,384]{1,0:T(8,128)(2,1)} %constant.124.clone.perm) | copy-start | bytes 884740
  148.8 28.9 %all-to-all-start.6 = ((f32[32,16,384]{2,1,0:T(8,128)}), f32[32,16,384]{2,1,0:T(8,128)S(1)}, u32[]{:S(2)}, u32[]{:S(2)}) async-start(f32[32,16,384]{2,1,0:T(8,128)} %along_y.1), calls=%async_computation.6 | async-start | bytes 1572864 | tf_op jit(solution)/shard_map/all_to_all | solution.py:248
  177.8 1.1 copy-start.6
  (2 other events, 1.3 us)

commit v2 on v1

--- a/solution.py
+++ b/solution.py
@@ -92,6 +92,12 @@
             for x in range(KX):
                 table[c, k, x, x * 24 + c * KY + k] = 1.0
     return table.reshape(384, 384).astype(jnp.bfloat16)
+
+
+def step_table(count):
+    freqs = (np.arange(count) * 12)[:, None] + np.arange(16)[None, :]
+    angle = 2.0 * np.pi * freqs[:, :, None] * np.arange(4)[None, None, :] / NG
+    return np.concatenate([np.cos(angle), -np.sin(angle)], 2).astype(np.float32)
 
 
 def split(value):
@@ -174,24 +180,8 @@
     )(charge.reshape(1, SITES), frac, cell, xh, xl)
 
 
-def y_body(grid, charges, slots, xsh, xsl, perm, arh, arl, aih, ail, out):
-    atom = slots[0:1, :].astype(jnp.int32)
-    cell = slots[1:4, :].astype(jnp.int32)
-    frac = slots[4:7, :]
-    lane = lax.broadcasted_iota(jnp.int32, (128, ROWS), 0)
-    pick = jnp.where(lane == atom % 128, 1.0, 0.0).astype(BF16)
-    q_high, q_low = split(charges[...])
-    rows = dot_nn(q_high, pick) + dot_nn(q_low, pick)
-    charge = jnp.sum(jnp.where(lane == atom // 128, rows, 0.0), 0, keepdims=True)
-    block = lax.broadcasted_iota(jnp.int32, (1, ROWS), 1) // OWN * YE
-    along_y = placed(N_SLAB * YE, cell[1:2, :] + block, spline(frac[1:2, :]))
-    along_z = placed(16, cell[2:3, :], spline(frac[2:3, :])) * charge
-    along_x = placed(XE, cell[0:1, :], spline(frac[0:1, :]))
-    wave_x = three(dot_nn, (xsh[...], xsl[...]), split(along_x))
-    both = [along_z[z : z + 1, :] * wave_x for z in range(ZE)]
-    both = jnp.concatenate(both + [jnp.zeros((24, ROWS), F32)], 0)
-    total = grid[...] + three(dot_nt, split(along_y), split(both))
-    high, low = split(total)
+def y_body(grid, part, rows, perm, arh, arl, aih, ail, out):
+    high, low = split(grid[...])
     high = dot_nt(perm[...], high).astype(BF16)
     low = dot_nt(perm[...], low).astype(BF16)
     freq = three(dot_nn, (high[:192], low[:192]), (arh[...], arl[...]))
@@ -199,7 +189,8 @@
     for f in range(N_FFT):
         for k in range(KX):
             out[f, :, k * 24 : k * 24 + 24] = freq[k * 16 : k * 16 + 16, f * 24 : f * 24 + 24]
-        out[f, :, KX * 24 : 384] = jnp.zeros((16, 384 - KX * 24), F32)
+        out[f, :, 288:352] = part[...]
+        out[f, :, 352:384] = rows[...]
 
 
 def along_y(*operands):
@@ -212,22 +203,160 @@
     )(*operands)
 
 
-def z_body(grid, perm, brh, brl, bih, bil, out_re, out_im):
+def unit(turns):
+    half = (turns - 0.5) * math.pi
+    square = half * half
+    sine = 0.0
+    for power in (11, 9, 7, 5, 3):
+        sine = (sine + (-1.0) ** (power // 2) / math.factorial(power)) * square
+    sine = half * (1.0 + sine)
+    cosine = 0.0
+    for power in (12, 10, 8, 6, 4, 2):
+        cosine = (cosine + (-1.0) ** (power // 2) / math.factorial(power)) * square
+    cosine = 1.0 + cosine
+    return 2.0 * sine * sine - 1.0, 2.0 * sine * cosine
+
+
+def site_wave(first, base, fraction, steps):
+    freq = first + lax.broadcasted_iota(jnp.int32, (16, 1), 0).astype(F32)
+    phase = freq * base
+    phase = phase - NG * jnp.floor(phase * (1.0 / NG))
+    re, im = unit(phase * (1.0 / NG))
+    weights = spline(fraction)
+    w_re = sum(steps[:, i : i + 1] * weights[i] for i in range(4))
+    w_im = sum(steps[:, 4 + i : 5 + i] * weights[i] for i in range(1, 4))
+    return re * w_re - im * w_im, re * w_im + im * w_re
+
+
+def table_body(place, slots, steps, out):
+    block = (lax.broadcasted_iota(jnp.int32, (1, ROWS), 1) // OWN * YL).astype(F32)
+    for g in range(8):
+        cell = slots[g, 2:5, :]
+        frac = slots[g, 5:8, :]
+        x_re, x_im = site_wave(place[0].astype(F32), cell[0:1], frac[0:1], steps[:, 0:8])
+        y_re, y_im = site_wave(place[1].astype(F32), cell[1:2] + block, frac[1:2], steps[:, 8:16])
+        out[g, 0:16] = x_re
+        out[g, 16:32] = x_im
+        out[g, 32:48] = y_re
+        out[g, 48:64] = y_im
+
+
+def tables(place, slots, steps):
+    return pl.pallas_call(
+        table_body,
+        grid=(4,),
+        in_specs=[
+            pl.BlockSpec(memory_space=pltpu.SMEM),
+            pl.BlockSpec((8, 8, ROWS), lambda i: (i, 0, 0)),
+            pl.BlockSpec((16, 16), lambda i: (0, 0)),
+        ],
+        out_specs=pl.BlockSpec((8, 64, ROWS), lambda i: (i, 0, 0)),
+        out_shape=jax.ShapeDtypeStruct((N_FFT, 64, ROWS), F32),
+        compiler_params=pltpu.CompilerParams(vmem_limit_bytes=VMEM_LIMIT),
+        cost_estimate=pl.CostEstimate(flops=2_000_000_000, bytes_accessed=5_000_000, transcendentals=0),
+        name="tables",
+    )(place, slots, steps)
+
+
+def ml_body(charges, slots, waves, out):
+    lane = lax.broadcasted_iota(jnp.int32, (128, ROWS), 0)
+    q_high, q_low = split(charges[...])
+    for g in range(8):
+        atom = slots[g, 1:2, :].astype(jnp.int32)
+        cell = slots[g, 4:5, :].astype(jnp.int32)
+        pick = jnp.where(lane == (atom & 127), 1.0, 0.0).astype(BF16)
+        rows = dot_nn(q_high, pick) + dot_nn(q_low, pick)
+        here = lane == (atom >> 7)
+        placed_z = placed(16, cell, spline(slots[g, 7:8, :]))
+        both = [
+            placed_z * jnp.sum(jnp.where(here, rows[v * 128 : v * 128 + 128], 0.0), 0, keepdims=True)
+            for v in range(2)
+        ]
+        x_re, x_im = waves[g, 0:16], waves[g, 16:32]
+        parts_re, parts_im = [], []
+        for k in range(KY):
+            y_re, y_im = waves[g, 32 + k : 33 + k], waves[g, 48 + k : 49 + k]
+            parts_re.append(y_re * x_re - y_im * x_im)
+            parts_im.append(y_re * x_im + y_im * x_re)
+        pairs = jnp.concatenate(parts_re + parts_im, 0)
+        total = three(dot_nt, split(pairs), split(jnp.concatenate(both, 0)))
+        out[0, :, g * 16 : g * 16 + 16] = total[:, :16]
+        out[1, :, g * 16 : g * 16 + 16] = total[:, 16:]
+
+
+def ml_waves(charges, slots, waves):
+    return pl.pallas_call(
+        ml_body,
+        grid=(4,),
+        in_specs=[
+            pl.BlockSpec((256, 128), lambda i: (0, 0)),
+            pl.BlockSpec((8, 8, ROWS), lambda i: (i, 0, 0)),
+            pl.BlockSpec((8, 64, ROWS), lambda i: (i, 0, 0)),
+        ],
+        out_specs=pl.BlockSpec((2, 384, 128), lambda i: (0, 0, i)),
+        out_shape=jax.ShapeDtypeStruct((2, 384, ROWS), F32),
+        compiler_params=pltpu.CompilerParams(vmem_limit_bytes=VMEM_LIMIT),
+        cost_estimate=pl.CostEstimate(flops=8_000_000_000, bytes_accessed=7_000_000, transcendentals=0),
+        name="ml_waves",
+    )(charges, slots, waves)
+
+
+def guarded(value, pivot, scale):
+    good = pivot > 1e-6 * scale
+    return jnp.where(good, value / jnp.where(good, pivot, 1.0), 0.0)
+
+
+def moment_body(v0, v1, v2, charges, rest):
+    def dot(a, b):
+        return jnp.sum(jnp.sum(a * b, 0, keepdims=True), 1, keepdims=True)
+
+    a, b, c = v0[...], v1[...], v2[...]
+    m0, m1, m2, m3, m4 = dot(a, a), dot(a, b), dot(b, b), dot(b, c), dot(c, c)
+    l10 = m2 / m1
+    l20 = m3 / m1
+    d1 = m3 - l10 * m2
+    e12 = m4 - l10 * m3
+    l21 = guarded(e12, d1, m3)
+    g1 = m1 - l10 * m0
+    g2 = (m2 - l20 * m0) - l21 * g1
+    c1 = guarded(g1, d1, m3)
+    c0 = m0 / m1 - l10 * c1
+    charges[0:128] = c0 * a + c1 * b
+    charges[128:256] = c - l21 * b + (l10 * l21 - l20) * a
+    rest[0:1] = jnp.broadcast_to(l20 * m3 + l21 * e12, (1, 128))
+    rest[1:2] = jnp.broadcast_to(g2, (1, 128))
+
+
+def moments(*operands):
+    return pl.pallas_call(
+        moment_body,
+        out_shape=(
+            jax.ShapeDtypeStruct((256, 128), F32),
+            jax.ShapeDtypeStruct((2, 128), F32),
+        ),
+        name="moments",
+    )(*operands)
+
+
+def z_body(grid, ml, quads, rest, pieces, perm, brh, brl, bih, bil, out_re, out_im, out_q):
+    m5 = jnp.sum(quads[...], 0, keepdims=True)
+    step = guarded(rest[1:2], m5 - rest[0:1], m5)[:, 0:1]
     high, low = split(grid[...])
-    high = dot_nt(perm[...], high).astype(BF16)
-    low = dot_nt(perm[...], low).astype(BF16)
+    total = dot_nt(perm[...], high) + dot_nt(perm[...], low)
+    high, low = split(total + (ml[0] + step * ml[1]))
     freq = three(dot_nn, (high[:192], low[:192]), (brh[...], brl[...]))
     freq = freq + three(dot_nn, (high[192:], low[192:]), (bih[...], bil[...]))
     for k in range(KY):
         out_re[k] = freq[k * 16 : k * 16 + KX, :NG]
         out_im[k] = freq[k * 16 : k * 16 + KX, NG:]
+    out_q[...] = pieces[0:1] + step * pieces[1:2]
 
 
 def along_z(*operands):
     shape = jax.ShapeDtypeStruct((KY, KX, NG), F32)
     return pl.pallas_call(
         z_body,
-        out_shape=(shape, shape),
+        out_shape=(shape, shape, jax.ShapeDtypeStruct((1, OWN), F32)),
         compiler_params=pltpu.CompilerParams(vmem_limit_bytes=VMEM_LIMIT),
         cost_estimate=pl.CostEstimate(flops=3_000_000_000, bytes_accessed=5_000_000, transcendentals=0),
         name="along_z",
@@ -250,26 +379,6 @@
 
 def to_all(value, axis):
     return swap(jnp.broadcast_to(value[None], (lax.axis_size(axis),) + value.shape), axis)
-
-
-def guarded(value, pivot, scale):
-    good = pivot > 1e-6 * scale
-    return jnp.where(good, value / jnp.where(good, pivot, 1.0), 0.0)
-
-
-def galerkin(m):
-    l10 = m[2] / m[1]
-    l20 = m[3] / m[1]
-    d1 = m[3] - l10 * m[2]
-    e12 = m[4] - l10 * m[3]
-    l21 = guarded(e12, d1, m[3])
-    d2 = (m[5] - l20 * m[3]) - l21 * e12
-    g1 = m[1] - l10 * m[0]
-    g2 = (m[2] - l20 * m[0]) - l21 * g1
-    c2 = guarded(g2, d2, m[5])
-    c1 = guarded(g1, d1, m[3]) - l21 * c2
-    c0 = m[0] / m[1] - l10 * c1 - l20 * c2
-    return c0, c1, c2
 
 
 def on_device(
@@ -322,10 +431,11 @@
         cols_of(ids),
         col_diag,
     )
+    matrix = lax.optimization_barrier(matrix)
     part = jnp.sum(matrix * drive_rows[:, None], 0)
-    got_1 = to_all(jnp.concatenate([part, drive_rows]), "fft")
+    got_1 = to_all(jnp.concatenate([part, got.reshape(8 * ROWS)]), "fft")
     first_cols = jnp.sum(got_1[:, :COLS], 0)
-    drive_full = got_1[:, COLS:].reshape(ATOMS)
+    slots = got_1[:, COLS:].reshape(N_FFT, 8, ROWS)
 
     xh, xl = (jnp.asarray(t) for t in two_parts(x_table()))
     mm = spread(mm_charge, mm_frac, mm_cell, xh, xl)
@@ -335,44 +445,58 @@
     got_2 = swap(jnp.concatenate([mm[:, : YE - 4], tail], 1), "slab")
     tail = got_2[:, YE - 4 :].reshape(N_SLAB, 1536)
     second_rows = jnp.sum(tail[:, :ROWS], 0)
-    first_full = jnp.transpose(tail[:, ROWS:].reshape(N_SLAB, N_FFT, OWN), (1, 0, 2)).reshape(ATOMS)
-
-    second_full = to_all(second_rows, "fft").reshape(ATOMS)
-    second_cols = cols_of(second_full)
-    quad = jnp.sum(second_rows * jnp.sum(matrix * second_cols[None, :], 1))
-    quad = jnp.sum(to_all(jnp.full((128,), quad), "slab")[:, 0])
-    quad = jnp.sum(to_all(jnp.full((128,), quad), "fft")[:, 0])
-    moments = [
-        jnp.sum(drive_full * drive_full),
-        jnp.sum(drive_full * first_full),
-        jnp.sum(first_full * first_full),
-        jnp.sum(first_full * second_full),
-        jnp.sum(second_full * second_full),
-        quad,
-    ]
-    c0, c1, c2 = galerkin(moments)
-    charge = c0 * drive_full + c1 * first_full + c2 * second_full
-    charge_piece = lax.dynamic_slice_in_dim(charge, own_first, OWN)
-
-    xs = x_table().T.reshape(N_SLAB, 24, XE)
-    xsh, xsl = (lax.dynamic_index_in_dim(jnp.asarray(t), s, 0, False) for t in two_parts(xs))
-    arh, arl, aih, ail = (jnp.asarray(t) for part in y_tables() for t in two_parts(part))
+    first_full = jnp.transpose(tail[:, ROWS:].reshape(N_SLAB, N_FFT, OWN), (1, 0, 2))
+    part = jnp.sum(matrix * second_rows[:, None], 0)
+
+    arh, arl, aih, ail = (jnp.asarray(t) for half in y_tables() for t in two_parts(half))
     spectrum = along_y(
         got_2.reshape(N_SLAB * YE, 384),
-        charge.reshape(128, 128),
-        got[1:8],
-        xsh,
-        xsl,
+        part.reshape(16, 64),
+        second_rows.reshape(16, OWN),
         jnp.asarray(perm_y()),
         arh,
         arl,
         aih,
         ail,
     )
-    spectrum = swap(spectrum, "fft").reshape(N_FFT * 16, 384)
-    brh, brl, bih, bil = (jnp.asarray(t) for part in z_tables() for t in two_parts(part))
-    struct_re, struct_im = along_z(spectrum, jnp.asarray(perm_z()), brh, brl, bih, bil)
-    return (charge_piece, struct_re, struct_im)
+    got_3 = swap(spectrum, "fft")
+    third_cols = jnp.sum(got_3[:, :, 288:352], 0).reshape(COLS)
+    second_full = got_3[:, :, 352:384]
+    second_cols = lax.dynamic_index_in_dim(second_full, s, 1, False).reshape(COLS)
+    quad = jnp.sum(third_cols * second_cols)
+    quads = to_all(jnp.full((128,), quad), "slab")
+
+    steps_x = step_table(N_SLAB)
+    steps_y = step_table(N_FFT)
+    steps = jnp.concatenate(
+        [
+            lax.dynamic_index_in_dim(jnp.asarray(steps_x), s, 0, False),
+            lax.dynamic_index_in_dim(jnp.asarray(steps_y), f, 0, False),
+        ],
+        1,
+    )
+    waves = tables(jnp.stack([s * KX, f * KY]).astype(jnp.int32), slots, steps)
+    charges, rest = moments(
+        slots[:, 0].reshape(128, 128),
+        first_full.reshape(128, 128),
+        second_full.reshape(128, 128),
+    )
+    ml = ml_waves(charges, slots, waves)
+    pieces = lax.dynamic_slice_in_dim(charges.reshape(2, ATOMS), own_first, OWN, 1)
+    brh, brl, bih, bil = (jnp.asarray(t) for half in z_tables() for t in two_parts(half))
+    struct_re, struct_im, charge = along_z(
+        got_3.reshape(N_FFT * 16, 384),
+        ml,
+        quads,
+        rest,
+        pieces,
+        jnp.asarray(perm_z()),
+        brh,
+        brl,
+        bih,
+        bil,
+    )
+    return (charge.reshape(OWN), struct_re, struct_im)
 
 
 def solution(mesh):

time: 185 us -> 168 us (0.908); the launches traced: 181 us -> 167 us
  Pallas kernels: 22.6 us -> 48.1 us
  waiting for transfers between devices: 31.6 us -> 11.5 us
  starting transfers between devices: 48.9 us -> 31.9 us
  between operations: 12.9 us -> 1.09 us
  local copies, waits for them, and re-layouts: 18.2 us -> 25.6 us
  blocking collectives: 27.2 us -> 33.3 us
  other arithmetic: 20.1 us -> 15.7 us
    pallas_call x1 -> x4, Pallas kernels: 2.5 us -> 29.8 us  [the longest x1 20.1 us: ml_waves(): pl.pallas_call(ml_body, grid=(4,), in_specs=[pl.BlockSpec((256, 128), lam...]
    all_to_all x6 -> x4, waiting for transfers between devices: 31.6 us -> 11.5 us  [swap(): return lax.all_to_all(value, axis, 0, 0, tiled=True)]
    all_to_all x6 -> x4, starting transfers between devices: 48.9 us -> 31.9 us  [swap(): return lax.all_to_all(value, axis, 0, 0, tiled=True)]
    all_to_all x1, blocking collectives: 27.2 us -> 33.3 us  [swap(): return lax.all_to_all(value, axis, 0, 0, tiled=True)]
    unnamed x45 -> x49, local copies, waits for them, and re-layouts: 6.31 us -> 10.9 us
    reduce_sum x7 -> x3, other arithmetic: 7.45 us -> 3.16 us  [the longest x1 2.39 us: on_device(): part = jnp.sum(matrix * second_rows[:, None], 0)]
    select_n x0 -> x1, other arithmetic: none -> 4.15 us  [couplings(): jnp.where(row_ids[:, None] == col_ids[None, :], col_diag[None, :], kernel)]
    reshape x2 -> x5, local copies, waits for them, and re-layouts: 0.25 us -> 3.3 us  [the longest x1 0.98 us: on_device(): charges.reshape(2, ATOMS)]
  transfers between devices with their start and end apart: 6 -> 4, of which waited for: 4 -> 2; matrix products, arithmetic and copies ran while one was open for 6% -> 9% of each run, Pallas kernels for 8% -> 25%
where the time goes in v2:
time: 168 us; the launch traced here: 167 us
  Pallas kernels  48.1 us (29%)
  blocking collectives  33.3 us (20%)
  starting transfers between devices  31.9 us (19%)
  local copies, waits for them, and re-layouts  25.6 us (15%)
  other arithmetic  15.7 us (9%)
  waiting for transfers between devices  11.5 us (7%)
    all_to_all x1, blocking collectives, swap(): return lax.all_to_all(value, axis, 0, 0, tiled=True)  33.3 us
    all_to_all x4, starting transfers between devices, swap(): return lax.all_to_all(value, axis, 0, 0, tiled=True)  31.9 us
    pallas_call x1, Pallas kernels, ml_waves(): pl.pallas_call(ml_body, grid=(4,), in_specs=[pl.BlockSpec((256, 128), lam...  20.1 us
    pallas_call x1, Pallas kernels, spread(): pl.pallas_call(spread_body, grid=(SITES // CHUNK,), in_specs=[pl.BlockSpe...  15 us
    all_to_all x4, waiting for transfers between devices, swap(): return lax.all_to_all(value, axis, 0, 0, tiled=True)  11.5 us
    unnamed x49, local copies, waits for them, and re-layouts  10.9 us
    pallas_call x1, Pallas kernels, tables(): pl.pallas_call(table_body, grid=(4,), in_specs=[pl.BlockSpec(memory_space...  5.17 us
    select_n x1, other arithmetic, couplings(): jnp.where(row_ids[:, None] == col_ids[None, :], col_diag[None, :], kernel)  4.15 us
  transfers between devices with their start and end apart: 4, of which 2 were waited for; matrix products, arithmetic and copies ran while one was open for 9% of the time, Pallas kernels for 25%

profile of v2, /device:TPU:1, one launch (start us, length us, event | category | flops | bytes accessed | tf_op | source)
XLA Modules:
  0.0 167.2 jit_solution(13845193615470718729)
XLA Ops:
  4.0 10.2 %all-to-all-start = ((f32[16,1,256]{2,1,0:T(1,128)}), f32[16,1,256]{2,1,0:T(1,128)S(1)}, u32[]{:S(2)}, u32[]{:S(2)}) async-start(f32[16,1,256]{2,1,0:T(1,128)} %reshape.234), calls=%async_computation | async-start | bytes 32768 | tf_op jit(solution)/shard_map/all_to_all | solution.py:377
  16.0 1.8 %slice_reduce_fusion.6 = (f32[16384]{0:T(1024)S(1)}, f32[16384]{0:T(1024)S(1)}, f32[16384]{0:T(1024)S(1)}, f32[1,16384]{1,0:T(1,128)S(1)}, f32[1,16384]{1,0:T(1,128)S(1)}, /*index=5*/f32[1,16384]{1,0:T(1,128)S(1)}) fusion(f32[3,16384]{1,0:T(4,128)} %param.24), kind=kLoop, calls=%fused_computation.41 | loop fusion | bytes 589824 | tf_op jit(solution)/shard_map/slice | solution.py:426
  19.8 4.1 %divide_select_fusion = f32[512,1024]{1,0:T(8,128)} fusion(f32[1024]{0:T(1024)S(1)} %integer_pow.37, f32[512]{0:T(512)S(1)} %bitcast.58, f32[1024]{0:T(1024)S(1)} %sub.71, f32[512]{0:T(512)S(1)} %bitcast.55, f32[1024]{0:T(1024)S(1)} %sub.66, f32[512]{0:T(512)S(1)} %bitcast.56, f32[1024]{0:T(1024)S(1)} %sub.61, f32[512]{0:T(512)S(1)} %bitcast.57, ...), kind=kLoop, calls=%fused_computation.4 | loop fusion | flops 9437184 | bytes 2131968 | tf_op jit(solution)/shard_map/jit(_where)/select_n | solution.py:373
  25.5 1.9 %multiply_reduce_fusion.2 = f32[1024]{0:T(1024)S(1)} fusion(f32[512,1024]{1,0:T(8,128)} %divide_select_fusion, f32[512]{0:T(512)S(1)} %mul.89), kind=kLoop, calls=%fused_computation.3 | loop fusion | flops 1047552 | bytes 2103296 | tf_op jit(solution)/shard_map/reduce_sum | solution.py:435
  27.4 1.2 broadcast_in_dim.27
  28.6 11.4 %all-to-all-start.1 = ((f32[32,1,5120]{2,1,0:T(1,128)}), f32[32,1,5120]{2,1,0:T(1,128)S(1)}, u32[]{:S(2)}, u32[]{:S(2)}) async-start(f32[32,1,5120]{2,1,0:T(1,128)} %broadcast_in_dim.27), calls=%async_computation.1 | async-start | bytes 1310720 | tf_op jit(solution)/shard_map/all_to_all | solution.py:377
  40.0 15.0 %spread.1 = f32[16,32,384]{2,1,0:T(8,128)S(1)} custom-call(f32[1,6144]{1,0:T(1,128)S(1)} %bitcast.41, f32[3,6144]{1,0:T(4,128)S(1)} %copy-done.1, s32[3,6144]{1,0:T(4,128)S(1)} %copy-done.2, bf16[392,384]{1,0:T(8,128)(2,1)S(1)} %copy-done.13, bf16[392,384]{1,0:T(8,128)(2,1)S(1)} %copy-done.14), custom_call_target="tpu_custom_call" | custom-call | flops 8000000000 | bytes 2000000 | tf_op jit(solution)/shard_map/spread/pallas_call | solution.py:164
  55.0 1.9 %all-to-all-done.1 = f32[32,1,5120]{2,1,0:T(1,128)S(1)} async-done(((f32[32,1,5120]{2,1,0:T(1,128)}), f32[32,1,5120]{2,1,0:T(1,128)S(1)}, u32[]{:S(2)}, u32[]{:S(2)}) %all-to-all-start.1) | async-done | bytes 655392 | tf_op jit(solution)/shard_map/all_to_all | solution.py:377
  57.9 1.8 %multiply_reduce_fusion.1 = f32[512]{0:T(512)S(1)} fusion(f32[512,1024]{1,0:T(8,128)} %divide_select_fusion, f32[1024]{0:T(1024)S(1)} %slice_reduce_fusion.1), kind=kLoop, calls=%fused_computation.2 | loop fusion | flops 1048064 | bytes 2103296 | tf_op jit(solution)/shard_map/reduce_sum | solution.py:442
  59.9 33.3 %all_to_all.32 = f32[16,32,384]{2,1,0:T(8,128)S(1)} all-to-all(f32[16,32,384]{2,1,0:T(8,128)S(1)} %pad_maximum_fusion), channel_id=1, replica_groups=mesh['fft'=32,'slab'=16] {'slab'}, dimensions={0} | all-to-all | bytes 1572864 | tf_op jit(solution)/shard_map/all_to_all | solution.py:377
  93.3 2.4 %multiply_reduce_fusion = f32[1024]{0:T(1024)} fusion(f32[512,1024]{1,0:T(8,128)} %divide_select_fusion, f32[512]{0:T(512)S(1)} %slice_reduce_fusion.2), kind=kLoop, calls=%fused_computation.1 | loop fusion | flops 1047552 | bytes 2103296 | tf_op jit(solution)/shard_map/reduce_sum | solution.py:449
  97.7 3.3 %along_y.1 = f32[32,16,384]{2,1,0:T(8,128)} custom-call(f32[512,384]{1,0:T(8,128)S(1)} %bitcast.35, f32[16,64]{1,0:T(8,128)S(1)} %reshape.143.part, f32[16,32]{1,0:T(8,128)S(1)} %reshape.144.rows, bf16[384,384]{1,0:T(8,128)(2,1)S(1)} %copy-done.16, bf16[512,768]{1,0:T(8,128)(2,1)S(1)} %copy-done.9, bf16[512,768]{1,0:T(8,128)(2,1)S(1)} %copy-done.10, ...), custom_call_target="tpu_custom_call" | custom-call | flops 4000000000 | bytes 5000000 | tf_op jit(solution)/shard_map/along_y/pallas_call | solution.py:197
  100.9 5.5 %all-to-all-start.3 = ((f32[32,16,384]{2,1,0:T(8,128)}), f32[32,16,384]{2,1,0:T(8,128)S(1)}, u32[]{:S(2)}, u32[]{:S(2)}) async-start(f32[32,16,384]{2,1,0:T(8,128)} %along_y.1), calls=%async_computation.3 | async-start | bytes 1572864 | tf_op jit(solution)/shard_map/all_to_all | solution.py:377
  110.2 5.2 %tables.1.waves = f32[32,64,512]{2,1,0:T(8,128)S(1)} custom-call(s32[2]{0:T(128)S(1)} %pad_add_fusion.place, f32[32,8,512]{2,1,0:T(8,128)S(1)} %bitcast.38, f32[16,16]{1,0:T(8,128)S(1)} %pad_maximum_fusion.3.steps), custom_call_target="tpu_custom_call" | custom-call | flops 2000000000 | bytes 5000000 | tf_op jit(solution)/shard_map/tables/pallas_call | solution.py:245
  115.4 1.9 %copy-done.17 = f32[32,64,512]{2,1,0:T(8,128)} copy-done((f32[32,64,512]{2,1,0:T(8,128)}, f32[32,64,512]{2,1,0:T(8,128)S(1)}, u32[]{:S(2)}) %copy-start.17) | copy-done | bytes 4194328
  118.4 9.6 %all-to-all-done.3 = f32[32,16,384]{2,1,0:T(8,128)S(1)} async-done(((f32[32,16,384]{2,1,0:T(8,128)}), f32[32,16,384]{2,1,0:T(8,128)S(1)}, u32[]{:S(2)}, u32[]{:S(2)}) %all-to-all-start.3) | async-done | bytes 786464 | tf_op jit(solution)/shard_map/all_to_all | solution.py:377
  129.7 1.2 broadcast_in_dim_broadcast_in_dim_broadcast_in_dim.3
  130.9 4.8 %all-to-all-start.4 = ((f32[16,1,128]{2,1,0:T(1,128)}), f32[16,1,128]{2,1,0:T(1,128)S(1)}, u32[]{:S(2)}, u32[]{:S(2)}) async-start(f32[16,1,128]{2,1,0:T(1,128)} %broadcast_in_dim_broadcast_in_dim_broadcast_in_dim.3), calls=%async_computation.4 | async-start | bytes 16384 | tf_op jit(solution)/shard_map/all_to_all | solution.py:377
  135.7 1.7 %moments.1 = (f32[256,128]{1,0:T(8,128)}, f32[2,128]{1,0:T(2,128)}) custom-call(f32[128,128]{1,0:T(8,128)} %bitcast.54, f32[128,128]{1,0:T(8,128)} %reshape.148.v1, f32[128,128]{1,0:T(8,128)} %reshape.149.v2), custom_call_target="tpu_custom_call" | custom-call | tf_op jit(solution)/shard_map/moments/pallas_call | solution.py:331
  139.3 20.1 %ml_waves.1.ml = f32[2,384,512]{2,1,0:T(8,128)S(1)} custom-call(f32[256,128]{1,0:T(8,128)S(1)} %copy-done, f32[32,8,512]{2,1,0:T(8,128)S(1)} %bitcast.39, f32[32,64,512]{2,1,0:T(8,128)} %copy-done.17), custom_call_target="tpu_custom_call" | custom-call | flops 8000000000 | bytes 7000000 | tf_op jit(solution)/shard_map/ml_waves/pallas_call | solution.py:288
  159.4 1.1 copy-done.18
  161.8 1.1 copy-done.8
  162.9 1.4 copy-done.19
  164.3 2.8 %along_z.1 = (f32[12,12,384]{2,1,0:T(8,128)}, f32[12,12,384]{2,1,0:T(8,128)}, f32[1,32]{1,0:T(1,128)}) custom-call(f32[512,384]{1,0:T(8,128)S(1)} %bitcast.34, f32[2,384,512]{2,1,0:T(8,128)S(1)} %copy-done.19, f32[16,128]{1,0:T(8,128)S(1)} %bitcast.40, f32[2,128]{1,0:T(2,128)S(1)} %copy-done.4, f32[2,32]{1,0:T(2,128)S(1)} %constant_dynamic-slice_fusion.pieces, ...), custom_call_target="tpu_custom_call" | custom-call | flops 3000000000 | bytes 5000000 | tf_op jit(solution)/shard_map/along_z/pallas_call | solution.py:357
  (108 shorter events, 21.3 us)
Async XLA Ops:
  0.6 18.3 %copy-start.21 = (f32[32]{0:T(128)S(1)}, f32[32]{0:T(128)}, u32[]{:S(2)}) copy-start(f32[32]{0:T(128)} %param.27) | copy-start | bytes 388
  4.0 19.9 %all-to-all-start = ((f32[16,1,256]{2,1,0:T(1,128)}), f32[16,1,256]{2,1,0:T(1,128)S(1)}, u32[]{:S(2)}, u32[]{:S(2)}) async-start(f32[16,1,256]{2,1,0:T(1,128)} %reshape.234), calls=%async_computation | async-start | bytes 32768 | tf_op jit(solution)/shard_map/all_to_all | solution.py:377
  25.4 14.6 %copy-start.1 = (f32[3,6144]{1,0:T(4,128)S(1)}, f32[3,6144]{1,0:T(4,128)}, u32[]{:S(2)}) copy-start(f32[3,6144]{1,0:T(4,128)} %frac.1) | copy-start | bytes 221188
  25.4 14.6 %copy-start.2 = (s32[3,6144]{1,0:T(4,128)S(1)}, s32[3,6144]{1,0:T(4,128)}, u32[]{:S(2)}) copy-start(s32[3,6144]{1,0:T(4,128)} %cell.1) | copy-start | bytes 221188
  25.4 14.6 %copy-start.3 = (f32[6144]{0:T(1024)S(1)}, f32[6144]{0:T(1024)}, u32[]{:S(2)}) copy-start(f32[6144]{0:T(1024)} %param.28) | copy-start | bytes 73732
  25.4 14.6 %copy-start.13 = (bf16[392,384]{1,0:T(8,128)(2,1)S(1)}, bf16[392,384]{1,0:T(8,128)(2,1)}, u32[]{:S(2)}) copy-start(bf16[392,384]{1,0:T(8,128)(2,1)} %constant.112.clone.xh) | copy-start | bytes 903172
  25.4 14.6 %copy-start.14 = (bf16[392,384]{1,0:T(8,128)(2,1)S(1)}, bf16[392,384]{1,0:T(8,128)(2,1)}, u32[]{:S(2)}) copy-start(bf16[392,384]{1,0:T(8,128)(2,1)} %constant.113.clone.xl) | copy-start | bytes 903172
  28.6 28.3 %all-to-all-start.1 = ((f32[32,1,5120]{2,1,0:T(1,128)}), f32[32,1,5120]{2,1,0:T(1,128)S(1)}, u32[]{:S(2)}, u32[]{:S(2)}) async-start(f32[32,1,5120]{2,1,0:T(1,128)} %broadcast_in_dim.27), calls=%async_computation.1 | async-start | bytes 1310720 | tf_op jit(solution)/shard_map/all_to_all | solution.py:377
  59.8 36.7 %copy-start.9 = (bf16[512,768]{1,0:T(8,128)(2,1)S(1)}, bf16[512,768]{1,0:T(8,128)(2,1)}, u32[]{:S(2)}) copy-start(bf16[512,768]{1,0:T(8,128)(2,1)} %constant.114.clone.arh) | copy-start | bytes 2359300
  59.8 36.7 %copy-start.10 = (bf16[512,768]{1,0:T(8,128)(2,1)S(1)}, bf16[512,768]{1,0:T(8,128)(2,1)}, u32[]{:S(2)}) copy-start(bf16[512,768]{1,0:T(8,128)(2,1)} %constant.115.clone.arl) | copy-start | bytes 2359300
  59.8 36.7 %copy-start.11 = (bf16[512,768]{1,0:T(8,128)(2,1)S(1)}, bf16[512,768]{1,0:T(8,128)(2,1)}, u32[]{:S(2)}) copy-start(bf16[512,768]{1,0:T(8,128)(2,1)} %constant.116.clone.aih) | copy-start | bytes 2359300
  59.9 36.7 %copy-start.16 = (bf16[384,384]{1,0:T(8,128)(2,1)S(1)}, bf16[384,384]{1,0:T(8,128)(2,1)}, u32[]{:S(2)}) copy-start(bf16[384,384]{1,0:T(8,128)(2,1)} %constant.118.clone.perm) | copy-start | bytes 884740
  96.5 1.1 copy-start.12
  100.9 27.0 %all-to-all-start.3 = ((f32[32,16,384]{2,1,0:T(8,128)}), f32[32,16,384]{2,1,0:T(8,128)S(1)}, u32[]{:S(2)}, u32[]{:S(2)}) async-start(f32[32,16,384]{2,1,0:T(8,128)} %along_y.1), calls=%async_computation.3 | async-start | bytes 1572864 | tf_op jit(solution)/shard_map/all_to_all | solution.py:377
  115.4 1.9 %copy-start.17 = (f32[32,64,512]{2,1,0:T(8,128)}, f32[32,64,512]{2,1,0:T(8,128)S(1)}, u32[]{:S(2)}) copy-start(f32[32,64,512]{2,1,0:T(8,128)S(1)} %tables.1.waves) | copy-start | bytes 12582916
  130.9 29.7 %all-to-all-start.4 = ((f32[16,1,128]{2,1,0:T(1,128)}), f32[16,1,128]{2,1,0:T(1,128)S(1)}, u32[]{:S(2)}, u32[]{:S(2)}) async-start(f32[16,1,128]{2,1,0:T(1,128)} %broadcast_in_dim_broadcast_in_dim_broadcast_in_dim.3), calls=%async_computation.4 | async-start | bytes 16384 | tf_op jit(solution)/shard_map/all_to_all | solution.py:377
  139.3 21.3 %copy-start.4 = (f32[2,128]{1,0:T(2,128)S(1)}, f32[2,128]{1,0:T(2,128)}, u32[]{:S(2)}) copy-start(f32[2,128]{1,0:T(2,128)} %get-tuple-element.9.rest) | copy-start | bytes 3076
  139.3 21.3 %copy-start.5 = (bf16[512,768]{1,0:T(8,128)(2,1)S(1)}, bf16[512,768]{1,0:T(8,128)(2,1)}, u32[]{:S(2)}) copy-start(bf16[512,768]{1,0:T(8,128)(2,1)} %constant.121.clone.brh) | copy-start | bytes 2359300
  139.3 21.3 %copy-start.6 = (bf16[512,768]{1,0:T(8,128)(2,1)S(1)}, bf16[512,768]{1,0:T(8,128)(2,1)}, u32[]{:S(2)}) copy-start(bf16[512,768]{1,0:T(8,128)(2,1)} %constant.122.clone.brl) | copy-start | bytes 2359300
  139.3 21.3 %copy-start.15 = (bf16[384,384]{1,0:T(8,128)(2,1)S(1)}, bf16[384,384]{1,0:T(8,128)(2,1)}, u32[]{:S(2)}) copy-start(bf16[384,384]{1,0:T(8,128)(2,1)} %constant.125.clone.perm) | copy-start | bytes 884740
  159.4 1.2 copy-start.18
  160.7 1.1 copy-start.7
  161.8 1.1 copy-start.8
  162.9 1.4 copy-start.19
  (2 other events, 1.7 us)

commit v3 on v2

v3 whole, which is shorter than its diff:
```python
import math

import jax
import jax.numpy as jnp
import numpy as np
from jax import lax
from jax.experimental import pallas as pl
from jax.experimental.pallas import tpu as pltpu
from jax.sharding import PartitionSpec as P

NG = 384
N_FFT = 32
N_SLAB = 16
YL = 24
ZL = 12
KX = 12
KY = 12
OWN = 32
ROWS = 512
COLS = 1024
ATOMS = 16384
SITES = 6144
CHUNK = 1024
XE = 392
YE = 32
ZE = 15
PAIRS = 288

KE = 14.4
ALPHA = 0.08
SOFT = 0.01
SQPI = math.sqrt(math.pi)
F32 = jnp.float32
BF16 = jnp.bfloat16
VMEM_LIMIT = 24 * 1024 * 1024


def wave(points, freqs):
    angle = 2.0 * np.pi * ((points[:, None] * freqs[None, :]) % NG) / NG
    return np.cos(angle), np.sin(angle)


def two_parts(table):
    high = np.asarray(table, np.float32).astype(jnp.bfloat16)
    low = (np.asarray(table, np.float64) - high.astype(np.float64)).astype(jnp.bfloat16)
    return high, low


def x_table():
    points = np.arange(XE)
    cos, sin = wave(points, np.arange(NG // 2))
    cos, sin = (t.reshape(XE, N_SLAB, 1, KX) for t in (cos, sin))
    table = np.concatenate([cos, -sin], 2)
    table = table * (points < NG + 3)[:, None, None, None]
    return table.reshape(XE, N_SLAB * 2 * KX)


def y_tables():
    local = np.arange(YE)
    points = (np.arange(N_SLAB)[:, None] * YL + local[None, :]).reshape(-1)
    used = np.tile(local < YL + 3, N_SLAB)[:, None, None, None]
    cos, sin = wave(points, np.arange(NG))
    cos, sin = (t.reshape(-1, N_FFT, 1, KY) for t in (cos, sin))
    from_re = np.concatenate([cos, -sin], 2) * used
    from_im = np.concatenate([sin, cos], 2) * used
    return from_re.reshape(-1, 2 * NG), from_im.reshape(-1, 2 * NG)


def z_tables():
    local = np.arange(16)
    points = (np.arange(N_FFT)[:, None] * ZL + local[None, :]).reshape(-1)
    used = np.tile(local < ZL + 3, N_FFT)[:, None]
    scale = 1.0 / (NG * math.sqrt(NG))
    cos, sin = wave(points, np.arange(NG))
    return cos * used * scale, sin * used * scale


def perm_y():
    table = np.zeros((2, KX, 16, 384), np.float32)
    for c in range(2):
        for k in range(KX):
            for z in range(ZE):
                table[c, k, z, z * 24 + c * KX + k] = 1.0
    return table.reshape(384, 384).astype(jnp.bfloat16)


def perm_z():
    table = np.zeros((384, PAIRS), np.float32)
    for c in range(2):
        for k in range(KY):
            for x in range(KX):
                column = c * 96 + k * 8 + x if x < 8 else 192 + c * 48 + k * 4 + x - 8
                table[x * 24 + c * KY + k, column] = 1.0
    return table.astype(jnp.bfloat16)


def step_table(count):
    local = np.concatenate([np.arange(12), np.arange(8, 12)])
    freqs = (np.arange(count) * 12)[:, None] + local[None, :]
    angle = 2.0 * np.pi * freqs[:, :, None] * np.arange(4)[None, None, :] / NG
    return np.concatenate([np.cos(angle), -np.sin(angle)], 2).astype(np.float32)


def split(value):
    high = value.astype(BF16)
    return high, (value - high.astype(F32)).astype(BF16)


def dot_nn(a, b):
    return lax.dot_general(a, b, (((1,), (0,)), ((), ())), preferred_element_type=F32)


def dot_nt(a, b):
    return lax.dot_general(a, b, (((1,), (1,)), ((), ())), preferred_element_type=F32)


def dot_tn(a, b):
    return lax.dot_general(a, b, (((0,), (0,)), ((), ())), preferred_element_type=F32)


def three(dot, a, b):
    return dot(a[0], b[0]) + dot(a[0], b[1]) + dot(a[1], b[0])


def spline(u):
    squared = u * u
    cubed = squared * u
    rest = 1.0 - u
    return (
        rest * rest * rest / 6.0,
        (3.0 * cubed - 6.0 * squared + 4.0) / 6.0,
        (-3.0 * cubed + 3.0 * squared + 3.0 * u + 1.0) / 6.0,
        cubed / 6.0,
    )


def placed(rows, cell, weights):
    off = lax.broadcasted_iota(jnp.int32, (rows, cell.shape[1]), 0) - cell
    value = jnp.where(off == 3, weights[3], 0.0)
    value = jnp.where(off == 2, weights[2], value)
    value = jnp.where(off == 1, weights[1], value)
    return jnp.where(off == 0, weights[0], value)


def spread_body(charge, frac, cell, xh, xl, out, acc):
    step = pl.program_id(0)

    @pl.when(step == 0)
    def _():
        acc[...] = jnp.zeros_like(acc)

    along_x = placed(XE, cell[0:1, :], spline(frac[0:1, :]))
    along_y = placed(YE, cell[1:2, :], spline(frac[1:2, :])) * charge[...]
    along_z = placed(16, cell[2:3, :], spline(frac[2:3, :]))
    plane = jnp.concatenate([along_z[z : z + 1, :] * along_y for z in range(ZE)], 0)
    acc[...] += three(dot_nt, split(plane), split(along_x))

    @pl.when(step == pl.num_programs(0) - 1)
    def _():
        freq = three(dot_nn, split(acc[...]), (xh[...], xl[...]))
        for s in range(N_SLAB):
            for z in range(ZE):
                out[s, :, z * 24 : z * 24 + 24] = freq[z * YE : z * YE + YE, s * 24 : s * 24 + 24]
            out[s, :, ZE * 24 : 384] = jnp.zeros((YE, 384 - ZE * 24), F32)


def spread(charge, frac, cell, xh, xl):
    whole = pl.BlockSpec((XE, 384), lambda i: (0, 0))
    return pl.pallas_call(
        spread_body,
        grid=(SITES // CHUNK,),
        in_specs=[
            pl.BlockSpec((1, CHUNK), lambda i: (0, i)),
            pl.BlockSpec((3, CHUNK), lambda i: (0, i)),
            pl.BlockSpec((3, CHUNK), lambda i: (0, i)),
            whole,
            whole,
        ],
        out_specs=pl.BlockSpec((N_SLAB, YE, 384), lambda i: (0, 0, 0)),
        out_shape=jax.ShapeDtypeStruct((N_SLAB, YE, 384), F32),
        scratch_shapes=[pltpu.VMEM((ZE * YE, XE), F32)],
        compiler_params=pltpu.CompilerParams(vmem_limit_bytes=VMEM_LIMIT),
        cost_estimate=pl.CostEstimate(flops=8_000_000_000, bytes_accessed=2_000_000, transcendentals=0),
        name="spread",
    )(charge.reshape(1, SITES), frac, cell, xh, xl)


def lanes(tiles):
    return jnp.concatenate([tiles[i : i + 1] for i in range(tiles.shape[0])], 1)


def pack_body(drive, atom, cell, frac, out):
    out[...] = jnp.zeros_like(out)
    for i in range(N_SLAB):
        out[i, 0:1, 0:OWN] = -drive[...]
        out[i, 1:2, 0:OWN] = atom[...].astype(F32)
        out[i, 2:5, 0:OWN] = cell[...].astype(F32)
        out[i, 5:8, 0:OWN] = frac[...]


def pack(drive, atom, cell, frac):
    return pl.pallas_call(
        pack_body,
        out_shape=jax.ShapeDtypeStruct((N_SLAB, 8, 128), F32),
        name="pack",
    )(drive.reshape(1, OWN), atom.reshape(1, OWN), cell, frac)


def erf_ratio(value):
    square = value * value
    p = 0.00022905065861350646
    for c in (0.0034082910107109506, 0.050955695062380861, 0.18520832239976145, 1.128379143519084):
        p = p * square + c
    q = -1.1791602954361697e-7
    for c in (
        0.000023547966471313185,
        0.0010179625278914885,
        0.014070470171167667,
        0.11098505178285362,
        0.49746925110067538,
        1.0,
    ):
        q = q * square + c
    return value * p, q


def couple_body(place, pos, width, hard, out, picked, rows, own):
    f, s = place[0], place[1]
    lane = lax.broadcasted_iota(jnp.int32, (8, 128), 1) >> 5
    for j in range(N_FFT):
        at = pl.multiple_of(j * ROWS + (s >> 2) * 128, 128)
        picked[j, 0:3, :] = pos[:, pl.ds(at, 128)]
        picked[j, 3:4, :] = width[:, pl.ds(at, 128)]
    tiles = []
    for tile in range(COLS // 128):
        value = jnp.zeros((8, 128), F32)
        for j in range(4):
            value = jnp.where(lane == j, pltpu.roll(picked[tile * 4 + j], ((j - (s & 3)) & 3) * OWN, 1), value)
        tiles.append(value)
    cols = jnp.concatenate(tiles, 1)
    at = pl.multiple_of(f * ROWS, 128)
    rows[0:3, :] = pos[:, pl.ds(at, ROWS)]
    rows[3:4, :] = width[:, pl.ds(at, ROWS)]
    side = jnp.transpose(rows[...])
    own[...] = jnp.zeros_like(own)
    own[0:1, 0:OWN] = hard[...]
    own_hard = pltpu.roll(own[...], (f & 3) * OWN, 1)[0:1]
    diag = jnp.concatenate([jnp.where((f >> 2) == t, own_hard, 0.0) for t in range(COLS // 128)], 1)
    diag = diag + KE * (1.0 / (cols[3:4] * SQPI) - 2.0 * ALPHA / SQPI)
    col_id = lax.broadcasted_iota(jnp.int32, (1, COLS), 1) - f * OWN
    col_id = jnp.where((col_id >= 0) & (col_id < OWN), col_id + s * OWN, -1)
    col_sq = 2.0 * cols[3:4] * cols[3:4]
    step = 16
    for first in range(0, ROWS, step):
        here = side[first : first + step]
        square = SOFT
        for i in range(3):
            gap = here[:, i : i + 1] - cols[i : i + 1]
            square = square + gap * gap
        inverse = lax.rsqrt(square)
        distance = square * inverse
        narrow = lax.rsqrt(2.0 * here[:, 3:4] * here[:, 3:4] + col_sq)
        p1, q1 = erf_ratio(jnp.minimum(distance * narrow, 3.832506856900711))
        p2, q2 = erf_ratio(jnp.minimum(distance * ALPHA, 3.832506856900711))
        value = KE * inverse * ((p1 * q2 - p2 * q1) / (q1 * q2))
        row_id = first + lax.broadcasted_iota(jnp.int32, (step, 1), 0)
        out[first : first + step] = jnp.where(row_id == col_id, diag, value)


def couple(place, pos, width, hard):
    return pl.pallas_call(
        couple_body,
        in_specs=[pl.BlockSpec(memory_space=pltpu.SMEM)] + [pl.BlockSpec(memory_space=pltpu.VMEM)] * 3,
        out_shape=jax.ShapeDtypeStruct((ROWS, COLS), F32),
        scratch_shapes=[pltpu.VMEM((N_FFT, 8, 128), F32), pltpu.VMEM((8, ROWS), F32), pltpu.VMEM((8, 128), F32)],
        compiler_params=pltpu.CompilerParams(vmem_limit_bytes=12 * 1024 * 1024),
        cost_estimate=pl.CostEstimate(flops=100_000_000, bytes_accessed=2_000_000, transcendentals=1_000_000),
        name="couple",
    )(place, pos, width.reshape(1, ATOMS), hard.reshape(1, OWN))


def first_body(got, matrix, out, slots):
    for s in range(N_SLAB):
        slots[:, s * OWN : s * OWN + OWN] = got[s, :, 0:OWN]
    every = slots[...]
    part = jnp.sum(matrix[...] * jnp.transpose(every)[:, 0:1], 0, keepdims=True)
    for i in range(8):
        out[0, i : i + 1, :] = part[:, i * 128 : i * 128 + 128]
    for i in range(4):
        out[0, 8 + i * 8 : 16 + i * 8, :] = every[:, i * 128 : i * 128 + 128]
    whole = out[0]
    for f in range(1, N_FFT):
        out[f] = whole


def first_product(got, matrix):
    return pl.pallas_call(
        first_body,
        out_shape=jax.ShapeDtypeStruct((N_FFT, 40, 128), F32),
        scratch_shapes=[pltpu.VMEM((8, ROWS), F32)],
        compiler_params=pltpu.CompilerParams(vmem_limit_bytes=12 * 1024 * 1024),
        name="first_product",
    )(got, matrix)


def y_body(grid, matrix, perm, arh, arl, aih, ail, out, side):
    got = grid[...]
    rows = jnp.sum(got[:, YE - 4 :, 0:128], 0)
    side[0:4, :] = rows
    turned = jnp.transpose(side[...])
    column = jnp.concatenate([turned[:, i : i + 1] for i in range(4)], 0)
    part = jnp.sum(matrix[...] * column, 0, keepdims=True)
    high, low = split(got.reshape(N_SLAB * YE, 384))
    high = dot_nt(perm[...], high).astype(BF16)
    low = dot_nt(perm[...], low).astype(BF16)
    freq = three(dot_nn, (high[:192], low[:192]), (arh[...], arl[...]))
    freq = freq + three(dot_nn, (high[192:], low[192:]), (aih[...], ail[...]))
    for i in range(16):
        out[0, i : i + 1, 288:320] = part[:, i * OWN : i * OWN + OWN]
        out[0, i : i + 1, 320:352] = part[:, ROWS + i * OWN : ROWS + i * OWN + OWN]
        out[0, i : i + 1, 352:384] = rows[i // 4 : i // 4 + 1, i % 4 * OWN : i % 4 * OWN + OWN]
    extra = out[0, :, 256:384]
    for f in range(N_FFT):
        if f > 0:
            out[f, :, 256:384] = extra
        for k in range(KX):
            out[f, :, k * 24 : k * 24 + 24] = freq[k * 16 : k * 16 + 16, f * 24 : f * 24 + 24]


def along_y(*operands):
    return pl.pallas_call(
        y_body,
        out_shape=jax.ShapeDtypeStruct((N_FFT, 16, 384), F32),
        scratch_shapes=[pltpu.VMEM((8, 128), F32)],
        compiler_params=pltpu.CompilerParams(vmem_limit_bytes=24 * 1024 * 1024),
        cost_estimate=pl.CostEstimate(flops=4_000_000_000, bytes_accessed=5_000_000, transcendentals=0),
        name="along_y",
    )(*operands)


def quad_body(place, got, out):
    s = place[1]
    third = jnp.sum(got[:, :, 32:96], 0)
    second = got[:, pl.ds(s, 1), 96:128].reshape(N_FFT, OWN)
    total = jnp.sum(third[:, 0:OWN] * second[0:16] + third[:, OWN:] * second[16:], 0, keepdims=True)
    total = jnp.sum(total, 1, keepdims=True)
    out[...] = jnp.broadcast_to(total[None], out.shape)


def quad_sum(place, got):
    return pl.pallas_call(
        quad_body,
        grid=(1,),
        in_specs=[
            pl.BlockSpec(memory_space=pltpu.SMEM),
            pl.BlockSpec((N_FFT, 16, 128), lambda i: (0, 0, 2)),
        ],
        out_specs=pl.BlockSpec((N_SLAB, 8, 128), lambda i: (0, 0, 0)),
        out_shape=jax.ShapeDtypeStruct((N_SLAB, 8, 128), F32),
        compiler_params=pltpu.CompilerParams(vmem_limit_bytes=8 * 1024 * 1024),
        name="quad_sum",
    )(place, got)


def unit(turns):
    half = (turns - 0.5) * math.pi
    square = half * half
    sine = 0.0
    for power in (11, 9, 7, 5, 3):
        sine = (sine + (-1.0) ** (power // 2) / math.factorial(power)) * square
    sine = half * (1.0 + sine)
    cosine = 0.0
    for power in (12, 10, 8, 6, 4, 2):
        cosine = (cosine + (-1.0) ** (power // 2) / math.factorial(power)) * square
    cosine = 1.0 + cosine
    return 2.0 * sine * sine - 1.0, 2.0 * sine * cosine


def site_wave(first, base, fraction, steps):
    local = lax.broadcasted_iota(jnp.int32, (16, 1), 0)
    freq = first + jnp.where(local < 12, local, local - 4).astype(F32)
    phase = freq * base
    phase = phase - NG * jnp.floor(phase * (1.0 / NG))
    re, im = unit(phase * (1.0 / NG))
    weights = spline(fraction)
    w_re = sum(steps[:, i : i + 1] * weights[i] for i in range(4))
    w_im = sum(steps[:, 4 + i : 5 + i] * weights[i] for i in range(1, 4))
    return re * w_re - im * w_im, re * w_im + im * w_re


def slot_rows(slots, g):
    return jnp.concatenate([slots[g, 8 + i * 8 : 16 + i * 8, :] for i in range(4)], 1)


def table_body(place, slots, steps, out):
    block = (lax.broadcasted_iota(jnp.int32, (1, ROWS), 1) // OWN * YL).astype(F32)
    first_x, first_y = (place[1] * KX).astype(F32), (place[0] * KY).astype(F32)
    for g in range(8):
        rows = slot_rows(slots, g)
        x_re, x_im = site_wave(first_x, rows[2:3], rows[5:6], steps[:, 0:8])
        y_re, y_im = site_wave(first_y, rows[3:4] + block, rows[6:7], steps[:, 8:16])
        out[g, 0:16] = x_re
        out[g, 16:32] = x_im
        out[g, 32:48] = y_re
        out[g, 48:64] = y_im


def tables(place, slots, steps):
    return pl.pallas_call(
        table_body,
        grid=(4,),
        in_specs=[
            pl.BlockSpec(memory_space=pltpu.SMEM),
            pl.BlockSpec((8, 40, 128), lambda i: (i, 0, 0)),
            pl.BlockSpec((16, 16), lambda i: (0, 0)),
        ],
        out_specs=pl.BlockSpec((8, 64, ROWS), lambda i: (i, 0, 0)),
        out_shape=jax.ShapeDtypeStruct((N_FFT, 64, ROWS), F32),
        compiler_params=pltpu.CompilerParams(vmem_limit_bytes=12 * 1024 * 1024),
        cost_estimate=pl.CostEstimate(flops=2_000_000_000, bytes_accessed=5_000_000, transcendentals=0),
        name="tables",
    )(place, slots, steps)


def ml_body(charges, slots, waves, out):
    upper = lax.broadcasted_iota(jnp.int32, (8, 1), 0) < 4
    for g in range(8):
        rows = slot_rows(slots, g)
        placed_z = placed(16, rows[4:5].astype(jnp.int32), spline(rows[7:8]))
        both = [placed_z * lanes(charges[v, g * 4 : g * 4 + 4, :]) for v in range(2)]
        z_high, z_low = split(jnp.concatenate(both, 0))
        x_re, x_im = waves[g, 0:8], waves[g, 16:24]
        parts_re, parts_im = [], []
        for k in range(KY):
            y_re, y_im = waves[g, 32 + k : 33 + k], waves[g, 48 + k : 49 + k]
            parts_re.append(y_re * x_re - y_im * x_im)
            parts_im.append(y_re * x_im + y_im * x_re)
        parts = parts_re + parts_im
        x_re, x_im = waves[g, 8:16], waves[g, 24:32]
        parts_re, parts_im = [], []
        for k in range(0, KY, 2):
            y_re = jnp.where(upper, waves[g, 32 + k : 33 + k], waves[g, 33 + k : 34 + k])
            y_im = jnp.where(upper, waves[g, 48 + k : 49 + k], waves[g, 49 + k : 50 + k])
            parts_re.append(y_re * x_re - y_im * x_im)
            parts_im.append(y_re * x_im + y_im * x_re)
        high, low = split(jnp.concatenate(parts + parts_re + parts_im, 0))
        total = dot_nt(jnp.concatenate([z_high, z_low], 0), high)
        out[g] = total[:32] + total[32:] + dot_nt(z_high, low)


def ml_waves(charges, slots, waves):
    return pl.pallas_call(
        ml_body,
        grid=(4,),
        in_specs=[
            pl.BlockSpec((2, 32, 128), lambda i: (0, i, 0)),
            pl.BlockSpec((8, 40, 128), lambda i: (i, 0, 0)),
            pl.BlockSpec((8, 64, ROWS), lambda i: (i, 0, 0)),
        ],
        out_specs=pl.BlockSpec((8, 32, PAIRS), lambda i: (i, 0, 0)),
        out_shape=jax.ShapeDtypeStruct((N_FFT, 32, PAIRS), F32),
        compiler_params=pltpu.CompilerParams(vmem_limit_bytes=20 * 1024 * 1024),
        cost_estimate=pl.CostEstimate(flops=4_000_000_000, bytes_accessed=7_000_000, transcendentals=0),
        name="ml_waves",
    )(charges, slots, waves)


def guarded(value, pivot, scale):
    good = pivot > 1e-6 * scale
    return jnp.where(good, value / jnp.where(good, pivot, 1.0), 0.0)


def lookup(tables, atom):
    index = lax.broadcasted_iota(jnp.int32, (128, atom.shape[1]), 0)
    pick = jnp.where(index == (atom & 127), 1.0, 0.0).astype(BF16)
    rows = dot_nn(tables, jnp.concatenate([pick, pick], 0))
    here = index == (atom >> 7)
    count = rows.shape[0] // 128
    return [
        jnp.sum(jnp.where(here, rows[v * 128 : v * 128 + 128], 0.0), 0, keepdims=True) for v in range(count)
    ]


def early_body(slots, first, out, v0):
    for i in range(4):
        v0[pl.ds(i, N_FFT, stride=4), :] = slots[:, 8 + i * 8, :]
    both = jnp.concatenate([v0[...], first[...]], 0)
    high, low = split(both)
    both = jnp.concatenate([high, low], 1)
    for g in range(N_FFT):
        found = lookup(both, slot_rows(slots, g)[1:2].astype(jnp.int32))
        for v in range(2):
            for i in range(4):
                out[v, g * 4 + i : g * 4 + i + 1, :] = found[v][:, i * 128 : i * 128 + 128]


def early(slots, first):
    return pl.pallas_call(
        early_body,
        out_shape=jax.ShapeDtypeStruct((2, 128, 128), F32),
        scratch_shapes=[pltpu.VMEM((128, 128), F32)],
        compiler_params=pltpu.CompilerParams(vmem_limit_bytes=12 * 1024 * 1024),
        cost_estimate=pl.CostEstimate(flops=2_000_000_000, bytes_accessed=1_000_000, transcendentals=0),
        name="early",
    )(slots, first)


def moment_body(place, slots, before, first, grid, charges, rest, v2, late):
    f, s = place[0], place[1]
    for i in range(4):
        pieces = [grid[:, i * 4 + j, 96:128] for j in range(4)]
        v2[pl.ds(i, N_FFT, stride=4), :] = jnp.concatenate(pieces, 1)
    high, low = split(v2[...])
    both = jnp.concatenate([high, low], 1)
    for g in range(N_FFT):
        found = lookup(both, slot_rows(slots, g)[1:2].astype(jnp.int32))[0]
        for i in range(4):
            late[g * 4 + i : g * 4 + i + 1, :] = found[:, i * 128 : i * 128 + 128]

    def dot(a, b):
        return jnp.sum(jnp.sum(a * b, 0, keepdims=True), 1, keepdims=True)

    a, b, c = before[0], before[1], late[...]
    m0, m1, m2, m3, m4 = dot(a, a), dot(a, b), dot(b, b), dot(b, c), dot(c, c)
    l10 = m2 / m1
    l20 = m3 / m1
    d1 = m3 - l10 * m2
    e12 = m4 - l10 * m3
    l21 = guarded(e12, d1, m3)
    g1 = m1 - l10 * m0
    g2 = (m2 - l20 * m0) - l21 * g1
    c1 = guarded(g1, d1, m3)
    c0 = m0 / m1 - l10 * c1
    charges[0] = c0 * a + c1 * b
    charges[1] = c - l21 * b + (l10 * l21 - l20) * a
    at = f * 4 + (s >> 2)
    rest[...] = jnp.zeros_like(rest)
    own = [slots[pl.ds(f, 1), 8 + i * 8, :] for i in range(4)]
    a = sum(jnp.where((s >> 2) == i, own[i], 0.0) for i in range(4))
    b, c = first[pl.ds(at, 1), :], v2[pl.ds(at, 1), :]
    rest[0:1] = c0 * a + c1 * b
    rest[1:2] = c - l21 * b + (l10 * l21 - l20) * a
    rest[...] = pltpu.roll(rest[...], ((4 - (s & 3)) & 3) * OWN, 1)
    rest[2:3] = jnp.broadcast_to(l20 * m3 + l21 * e12, (1, 128))
    rest[3:4] = jnp.broadcast_to(g2, (1, 128))


def moments(place, slots, before, first, grid):
    return pl.pallas_call(
        moment_body,
        grid=(1,),
        in_specs=[
            pl.BlockSpec(memory_space=pltpu.SMEM),
            pl.BlockSpec((N_FFT, 40, 128), lambda i: (0, 0, 0)),
            pl.BlockSpec((2, 128, 128), lambda i: (0, 0, 0)),
            pl.BlockSpec((128, 128), lambda i: (0, 0)),
            pl.BlockSpec((N_FFT, 16, 128), lambda i: (0, 0, 2)),
        ],
        out_specs=(
            pl.BlockSpec((2, 128, 128), lambda i: (0, 0, 0)),
            pl.BlockSpec((8, 128), lambda i: (0, 0)),
        ),
        out_shape=(
            jax.ShapeDtypeStruct((2, 128, 128), F32),
            jax.ShapeDtypeStruct((8, 128), F32),
        ),
        scratch_shapes=[pltpu.VMEM((128, 128), F32), pltpu.VMEM((128, 128), F32)],
        compiler_params=pltpu.CompilerParams(vmem_limit_bytes=12 * 1024 * 1024),
        cost_estimate=pl.CostEstimate(flops=1_000_000_000, bytes_accessed=1_000_000, transcendentals=0),
        name="moments",
    )(place, slots, before, first, grid)


def z_body(grid, ml, quads, rest, perm, ch, cl, sh, sl, out_re, out_im, out_q):
    m5 = jnp.sum(quads[:, 0, :], 0, keepdims=True)
    step = guarded(rest[3:4], m5 - rest[2:3], m5)[:, 0:1]
    high, low = split(grid[...].reshape(N_FFT * 16, 384))
    total = dot_nn(high, perm[...]) + dot_nn(low, perm[...])
    extra = ml[:, 0:16] + step[None] * ml[:, 16:32]
    both = split(total + extra.reshape(N_FFT * 16, PAIRS))
    cos = three(dot_tn, both, (ch[...], cl[...]))
    sin = three(dot_tn, both, (sh[...], sl[...]))
    for k in range(KY):
        for first, count, re in ((0, 8, k * 8), (8, 4, 192 + k * 4)):
            im = re + KY * count
            out_re[k, first : first + count] = cos[re : re + count] + sin[im : im + count]
            out_im[k, first : first + count] = cos[im : im + count] - sin[re : re + count]
    out_q[...] = (rest[0:1] + step * rest[1:2])[:, 0:OWN]


def along_z(*operands):
    shape = jax.ShapeDtypeStruct((KY, KX, NG), F32)
    return pl.pallas_call(
        z_body,
        out_shape=(shape, shape, jax.ShapeDtypeStruct((1, OWN), F32)),
        compiler_params=pltpu.CompilerParams(vmem_limit_bytes=20 * 1024 * 1024),
        cost_estimate=pl.CostEstimate(flops=3_000_000_000, bytes_accessed=5_000_000, transcendentals=0),
        name="along_z",
    )(*operands)


def swap(value, axis):
    return lax.all_to_all(value, axis, 0, 0, tiled=True)


def on_device(
    ml_pos,
    ml_width,
    ml_drive,
    ml_hard,
    mm_charge,
    mm_frac,
    mm_cell,
    slot_atom,
    slot_frac,
    slot_cell,
):
    f = lax.axis_index("fft")
    s = lax.axis_index("slab")
    place = jnp.stack([f, s]).astype(jnp.int32)

    got = swap(pack(ml_drive, slot_atom, slot_cell, slot_frac), "slab")
    matrix = couple(place, ml_pos, ml_width, ml_hard)
    got_1 = swap(first_product(got, matrix), "fft")
    xh, xl = (jnp.asarray(t) for t in two_parts(x_table()))
    mm = spread(mm_charge, mm_frac, mm_cell, xh, xl)
    first_cols = jnp.sum(got_1[:, :8], 0)
    part = jnp.sum(matrix * first_cols.reshape(1, COLS), 1)
    tail = jnp.concatenate([part.reshape(4, 128), first_cols[:4], first_cols[4:]], 1)
    tail = jnp.broadcast_to(tail[None], (N_SLAB, 4, 384))
    got_2 = swap(jnp.concatenate([mm[:, : YE - 4], tail], 1), "slab")
    first_full = jnp.concatenate([got_2[:, YE - 4 :, 128:256], got_2[:, YE - 4 :, 256:]], 1)
    first_full = jnp.transpose(first_full.reshape(N_SLAB, N_FFT, OWN), (1, 0, 2)).reshape(128, 128)

    arh, arl, aih, ail = (jnp.asarray(t) for half in y_tables() for t in two_parts(half))
    got_3 = swap(along_y(got_2, matrix, jnp.asarray(perm_y()), arh, arl, aih, ail), "fft")
    quads = swap(quad_sum(place, got_3), "slab")

    steps = jnp.concatenate(
        [
            lax.dynamic_index_in_dim(jnp.asarray(step_table(N_SLAB)), s, 0, False),
            lax.dynamic_index_in_dim(jnp.asarray(step_table(N_FFT)), f, 0, False),
        ],
        1,
    )
    waves = tables(place, got_1, steps)
    charges, rest = moments(place, got_1, early(got_1, first_full), first_full, got_3)
    ml = ml_waves(charges, got_1, waves)
    ch, cl, sh, sl = (jnp.asarray(t) for half in z_tables() for t in two_parts(half))
    struct_re, struct_im, charge = along_z(got_3, ml, quads, rest, jnp.asarray(perm_z()), ch, cl, sh, sl)
    return (charge.reshape(OWN), struct_re, struct_im)


def solution(mesh):
    return jax.shard_map(
        on_device,
        mesh=mesh,
        in_specs=(
            P(),
            P(),
            P(("fft", "slab")),
            P(("fft", "slab")),
            P(("fft", "slab")),
            P(None, ("fft", "slab")),
            P(None, ("fft", "slab")),
            P(("fft", "slab")),
            P(None, ("fft", "slab")),
            P(None, ("fft", "slab")),
        ),
        out_specs=(P(("fft", "slab")), P("fft", "slab", None), P("fft", "slab", None)),
        check_vma=False,
    )
```

time: 168 us -> 143 us (0.85)
  other arithmetic: 15.7 us -> 0.5 us
  local copies, waits for them, and re-layouts: 25.6 us -> 16.5 us
  waiting for transfers between devices: 11.5 us -> 7.96 us
  starting transfers between devices: 31.9 us -> 35.4 us
  blocking collectives: 33.3 us -> 31 us
  Pallas kernels: 48.1 us -> 50 us
    reduce_sum x7 -> x2, other arithmetic: 6.91 us -> 0.25 us  [the longest x1 0.22 us: on_device(): part = jnp.sum(matrix * first_cols.reshape(1, COLS), 1)]
    reshape x8 -> x3, local copies, waits for them, and re-layouts: 5.22 us -> 0.38 us  [the longest x2 0.27 us: on_device(): first_full.reshape(N_SLAB, N_FFT, OWN)]
    select_n x1 -> x0, other arithmetic: 4.15 us -> none  [couplings(): jnp.where(row_ids[:, None] == col_ids[None, :], col_diag[None, :], kernel)]
    unnamed x49 -> x46, local copies, waits for them, and re-layouts: 10.9 us -> 14.6 us
    slice x7 -> x2, local copies, waits for them, and re-layouts: 3.68 us -> 0.02 us  [the longest x1 0.02 us: on_device(): got_2[:, YE - 4:, 128:256]]
    all_to_all x4, starting transfers between devices: 31.9 us -> 35.4 us  [swap(): return lax.all_to_all(value, axis, 0, 0, tiled=True)]
    all_to_all x4, waiting for transfers between devices: 11.5 us -> 7.96 us  [swap(): return lax.all_to_all(value, axis, 0, 0, tiled=True)]
    pallas_call x2 -> x7, Pallas kernels: 21.8 us -> 25 us  [the longest x1 6.74 us: ml_waves(): pl.pallas_call(ml_body, grid=(4,), in_specs=[pl.BlockSpec((2, 32, 128), l...]
  transfers between devices with their start and end apart: 4 -> 4, of which waited for: 2 -> 1; matrix products, arithmetic and copies ran while one was open for 9% -> 1% of each run, Pallas kernels for 25% -> 29%
where the time goes in v3:
time: 143 us; the launch traced here: 142 us
  Pallas kernels  50 us (35%)
  starting transfers between devices  35.4 us (25%)
  blocking collectives  31 us (22%)
  local copies, waits for them, and re-layouts  16.5 us (12%)
  waiting for transfers between devices  7.96 us (6%)
    all_to_all x4, starting transfers between devices, swap(): return lax.all_to_all(value, axis, 0, 0, tiled=True)  35.4 us
    all_to_all x1, blocking collectives, swap(): return lax.all_to_all(value, axis, 0, 0, tiled=True)  31 us
    pallas_call x1, Pallas kernels, spread(): pl.pallas_call(spread_body, grid=(SITES // CHUNK,), in_specs=[pl.BlockSpe...  15 us
    unnamed x46, local copies, waits for them, and re-layouts  14.6 us
    all_to_all x4, waiting for transfers between devices, swap(): return lax.all_to_all(value, axis, 0, 0, tiled=True)  7.96 us
    pallas_call x1, Pallas kernels, ml_waves(): pl.pallas_call(ml_body, grid=(4,), in_specs=[pl.BlockSpec((2, 32, 128), l...  6.74 us
    pallas_call x1, Pallas kernels, couple(): pl.pallas_call(couple_body, in_specs=[pl.BlockSpec(memory_space=pltpu.SME...  5.89 us
    pallas_call x1, Pallas kernels, tables(): pl.pallas_call(table_body, grid=(4,), in_specs=[pl.BlockSpec(memory_space...  5.13 us
  transfers between devices with their start and end apart: 4, of which 1 were waited for; matrix products, arithmetic and copies ran while one was open for 1% of the time, Pallas kernels for 29%

profile of v3, /device:TPU:1, one launch (start us, length us, event | category | flops | bytes accessed | tf_op | source)
XLA Modules:
  0.0 142.3 jit_solution(15495781021731533958)
XLA Ops:
  0.6 1.4 pack.1
  2.0 10.2 %all-to-all-start = ((f32[16,8,128]{2,1,0:T(8,128)}), f32[16,8,128]{2,1,0:T(8,128)S(1)}, u32[]{:S(2)}, u32[]{:S(2)}) async-start(f32[16,8,128]{2,1,0:T(8,128)} %pack.1), calls=%async_computation | async-start | bytes 131072 | tf_op jit(solution)/shard_map/all_to_all | solution.py:603
  12.3 0.9 copy-done.1
  14.7 5.9 %couple.1.matrix = f32[512,1024]{1,0:T(8,128)S(1)} custom-call(s32[2]{0:T(128)S(1)} %pad_add_fusion.place, f32[3,16384]{1,0:T(4,128)S(1)} %copy-done.1, f32[1,16384]{1,0:T(1,128)S(1)} %bitcast.19, f32[1,32]{1,0:T(1,128)S(1)} %bitcast.20), custom_call_target="tpu_custom_call" | custom-call | flops 100000000 | bytes 2000000 | tf_op jit(solution)/shard_map/couple/pallas_call | solution.py:271
  20.6 1.2 first_product.1
  21.9 11.4 %all-to-all-start.1 = ((f32[32,40,128]{2,1,0:T(8,128)}), f32[32,40,128]{2,1,0:T(8,128)S(1)}, u32[]{:S(2)}, u32[]{:S(2)}) async-start(f32[32,40,128]{2,1,0:T(8,128)} %first_product.1), calls=%async_computation.1 | async-start | bytes 1310720 | tf_op jit(solution)/shard_map/all_to_all | solution.py:603
  35.7 1.0 copy-done.15
  36.7 1.0 copy-done.16
  37.7 15.0 %spread.1 = f32[16,32,384]{2,1,0:T(8,128)S(1)} custom-call(f32[1,6144]{1,0:T(1,128)S(1)} %bitcast.21, f32[3,6144]{1,0:T(4,128)S(1)} %copy-done.4, s32[3,6144]{1,0:T(4,128)S(1)} %copy-done.5, bf16[392,384]{1,0:T(8,128)(2,1)S(1)} %copy-done.15, bf16[392,384]{1,0:T(8,128)(2,1)S(1)} %copy-done.16), custom_call_target="tpu_custom_call" | custom-call | flops 8000000000 | bytes 2000000 | tf_op jit(solution)/shard_map/spread/pallas_call | solution.py:169
  53.1 31.0 %all_to_all.25.grid = f32[16,32,384]{2,1,0:T(8,128)S(1)} all-to-all(f32[16,32,384]{2,1,0:T(8,128)S(1)} %pad_maximum_fusion), channel_id=1, replica_groups=mesh['fft'=32,'slab'=16] {'slab'}, dimensions={0} | all-to-all | bytes 1572864 | tf_op jit(solution)/shard_map/all_to_all | solution.py:603
  84.1 2.4 %along_y.1 = f32[32,16,384]{2,1,0:T(8,128)S(1)} custom-call(f32[16,32,384]{2,1,0:T(8,128)S(1)} %all_to_all.25.grid, f32[512,1024]{1,0:T(8,128)S(1)} %couple.1.matrix, bf16[384,384]{1,0:T(8,128)(2,1)S(1)} %copy-done.18, bf16[512,768]{1,0:T(8,128)(2,1)S(1)} %copy-done.7, bf16[512,768]{1,0:T(8,128)(2,1)S(1)} %copy-done.8, bf16[512,768]{1,0:T(8,128)(2,1)S(1)} %copy-done.9, ...), custom_call_target="tpu_custom_call" | custom-call | flops 4000000000 | bytes 5000000 | tf_op jit(solution)/shard_map/along_y/pallas_call | solution.py:331
  87.4 9.0 %all-to-all-start.3 = ((f32[32,16,384]{2,1,0:T(8,128)}), f32[32,16,384]{2,1,0:T(8,128)S(1)}, u32[]{:S(2)}, u32[]{:S(2)}) async-start(f32[32,16,384]{2,1,0:T(8,128)} %copy-done), calls=%async_computation.3 | async-start | bytes 1572864 | tf_op jit(solution)/shard_map/all_to_all | solution.py:603
  98.1 5.1 %tables.1.waves = f32[32,64,512]{2,1,0:T(8,128)S(1)} custom-call(s32[2]{0:T(128)S(1)} %pad_add_fusion.place, f32[32,40,128]{2,1,0:T(8,128)S(1)} %all-to-all-done.1.slots, f32[16,16]{1,0:T(8,128)S(1)} %pad_maximum_fusion.2.steps), custom_call_target="tpu_custom_call" | custom-call | flops 2000000000 | bytes 5000000 | tf_op jit(solution)/shard_map/tables/pallas_call | solution.py:409
  103.2 1.9 %copy-done.19 = f32[32,64,512]{2,1,0:T(8,128)} copy-done((f32[32,64,512]{2,1,0:T(8,128)}, f32[32,64,512]{2,1,0:T(8,128)S(1)}, u32[]{:S(2)}) %copy-start.19) | copy-done | bytes 4194328
  105.6 4.5 %early.1.before = f32[2,128,128]{2,1,0:T(8,128)S(1)} custom-call(f32[32,40,128]{2,1,0:T(8,128)S(1)} %all-to-all-done.1.slots, f32[128,128]{1,0:T(8,128)S(1)} %reshape.43.first), custom_call_target="tpu_custom_call" | custom-call | flops 2000000000 | bytes 1000000 | tf_op jit(solution)/shard_map/early/pallas_call | solution.py:498
  110.2 7.9 %all-to-all-done.3.grid.got = f32[32,16,384]{2,1,0:T(8,128)S(1)} async-done(((f32[32,16,384]{2,1,0:T(8,128)}), f32[32,16,384]{2,1,0:T(8,128)S(1)}, u32[]{:S(2)}, u32[]{:S(2)}) %all-to-all-start.3) | async-done | bytes 786464 | tf_op jit(solution)/shard_map/all_to_all | solution.py:603
  118.1 1.5 %quad_sum.1 = f32[16,8,128]{2,1,0:T(8,128)} custom-call(s32[2]{0:T(128)S(1)} %pad_add_fusion.place, f32[32,16,384]{2,1,0:T(8,128)S(1)} %all-to-all-done.3.grid.got), custom_call_target="tpu_custom_call" | custom-call | tf_op jit(solution)/shard_map/quad_sum/pallas_call | solution.py:351
  119.6 4.9 %all-to-all-start.4 = ((f32[16,8,128]{2,1,0:T(8,128)}), f32[16,8,128]{2,1,0:T(8,128)S(1)}, u32[]{:S(2)}, u32[]{:S(2)}) async-start(f32[16,8,128]{2,1,0:T(8,128)} %quad_sum.1), calls=%async_computation.4 | async-start | bytes 131072 | tf_op jit(solution)/shard_map/all_to_all | solution.py:603
  124.5 3.7 %moments.1 = (f32[2,128,128]{2,1,0:T(8,128)S(1)}, f32[8,128]{1,0:T(8,128)S(1)}) custom-call(s32[2]{0:T(128)S(1)} %pad_add_fusion.place, f32[32,40,128]{2,1,0:T(8,128)S(1)} %all-to-all-done.1.slots, f32[2,128,128]{2,1,0:T(8,128)S(1)} %early.1.before, f32[128,128]{1,0:T(8,128)S(1)} %reshape.43.first, f32[32,16,384]{2,1,0:T(8,128)S(1)} %all-to-all-done.3.grid.got), custom_call_target="tpu_custom_call" | custom-call | flops 1000000000 | bytes 1000000 | tf_op jit(solution)/shard_map/moments/pallas_call | solution.py:549
  128.2 2.2 %copy-done.20 = f32[32,64,512]{2,1,0:T(8,128)S(1)} copy-done((f32[32,64,512]{2,1,0:T(8,128)S(1)}, f32[32,64,512]{2,1,0:T(8,128)}, u32[]{:S(2)}) %copy-start.20) | copy-done | bytes 4194328
  130.4 6.7 %ml_waves.1.ml = f32[32,32,288]{2,1,0:T(8,128)S(1)} custom-call(f32[2,128,128]{2,1,0:T(8,128)S(1)} %get-tuple-element.8.charges, f32[32,40,128]{2,1,0:T(8,128)S(1)} %all-to-all-done.1.slots, f32[32,64,512]{2,1,0:T(8,128)S(1)} %copy-done.20), custom_call_target="tpu_custom_call" | custom-call | flops 4000000000 | bytes 7000000 | tf_op jit(solution)/shard_map/ml_waves/pallas_call | solution.py:452
  137.2 1.2 copy-done.21
  138.4 1.4 copy-done.22
  139.8 2.5 %along_z.1 = (f32[12,12,384]{2,1,0:T(8,128)}, f32[12,12,384]{2,1,0:T(8,128)}, f32[1,32]{1,0:T(1,128)}) custom-call(f32[32,16,384]{2,1,0:T(8,128)S(1)} %all-to-all-done.3.grid.got, f32[32,32,288]{2,1,0:T(8,128)S(1)} %copy-done.22, f32[16,8,128]{2,1,0:T(8,128)S(1)} %all-to-all-done.4.quads, f32[8,128]{1,0:T(8,128)S(1)} %get-tuple-element.9.rest, ...), custom_call_target="tpu_custom_call" | custom-call | flops 3000000000 | bytes 5000000 | tf_op jit(solution)/shard_map/along_z/pallas_call | solution.py:593
  (59 shorter events, 7.4 us)
Async XLA Ops:
  2.0 18.6 %all-to-all-start = ((f32[16,8,128]{2,1,0:T(8,128)}), f32[16,8,128]{2,1,0:T(8,128)S(1)}, u32[]{:S(2)}, u32[]{:S(2)}) async-start(f32[16,8,128]{2,1,0:T(8,128)} %pack.1), calls=%async_computation | async-start | bytes 131072 | tf_op jit(solution)/shard_map/all_to_all | solution.py:603
  12.3 0.9 copy-start.1
  21.9 30.8 %all-to-all-start.1 = ((f32[32,40,128]{2,1,0:T(8,128)}), f32[32,40,128]{2,1,0:T(8,128)S(1)}, u32[]{:S(2)}, u32[]{:S(2)}) async-start(f32[32,40,128]{2,1,0:T(8,128)} %first_product.1), calls=%async_computation.1 | async-start | bytes 1310720 | tf_op jit(solution)/shard_map/all_to_all | solution.py:603
  33.2 0.9 copy-start.4
  34.1 0.9 copy-start.5
  35.7 1.0 copy-start.15
  36.7 1.0 copy-start.16
  52.7 31.4 %copy-start.18 = (bf16[384,384]{1,0:T(8,128)(2,1)S(1)}, bf16[384,384]{1,0:T(8,128)(2,1)}, u32[]{:S(2)}) copy-start(bf16[384,384]{1,0:T(8,128)(2,1)} %constant.56.clone.perm) | copy-start | bytes 884740
  53.0 31.1 %copy-start.7 = (bf16[512,768]{1,0:T(8,128)(2,1)S(1)}, bf16[512,768]{1,0:T(8,128)(2,1)}, u32[]{:S(2)}) copy-start(bf16[512,768]{1,0:T(8,128)(2,1)} %constant.52.clone.arh) | copy-start | bytes 2359300
  53.0 31.1 %copy-start.8 = (bf16[512,768]{1,0:T(8,128)(2,1)S(1)}, bf16[512,768]{1,0:T(8,128)(2,1)}, u32[]{:S(2)}) copy-start(bf16[512,768]{1,0:T(8,128)(2,1)} %constant.53.clone.arl) | copy-start | bytes 2359300
  53.0 31.1 %copy-start.9 = (bf16[512,768]{1,0:T(8,128)(2,1)S(1)}, bf16[512,768]{1,0:T(8,128)(2,1)}, u32[]{:S(2)}) copy-start(bf16[512,768]{1,0:T(8,128)(2,1)} %constant.54.clone.aih) | copy-start | bytes 2359300
  53.0 31.1 %copy-start.10 = (bf16[512,768]{1,0:T(8,128)(2,1)S(1)}, bf16[512,768]{1,0:T(8,128)(2,1)}, u32[]{:S(2)}) copy-start(bf16[512,768]{1,0:T(8,128)(2,1)} %constant.55.clone.ail) | copy-start | bytes 2359300
  86.6 0.9 copy-start
  87.4 30.7 %all-to-all-start.3 = ((f32[32,16,384]{2,1,0:T(8,128)}), f32[32,16,384]{2,1,0:T(8,128)S(1)}, u32[]{:S(2)}, u32[]{:S(2)}) async-start(f32[32,16,384]{2,1,0:T(8,128)} %copy-done), calls=%async_computation.3 | async-start | bytes 1572864 | tf_op jit(solution)/shard_map/all_to_all | solution.py:603
  103.2 2.0 %copy-start.19 = (f32[32,64,512]{2,1,0:T(8,128)}, f32[32,64,512]{2,1,0:T(8,128)S(1)}, u32[]{:S(2)}) copy-start(f32[32,64,512]{2,1,0:T(8,128)S(1)} %tables.1.waves) | copy-start | bytes 12582916
  119.6 18.8 %all-to-all-start.4 = ((f32[16,8,128]{2,1,0:T(8,128)}), f32[16,8,128]{2,1,0:T(8,128)S(1)}, u32[]{:S(2)}, u32[]{:S(2)}) async-start(f32[16,8,128]{2,1,0:T(8,128)} %quad_sum.1), calls=%async_computation.4 | async-start | bytes 131072 | tf_op jit(solution)/shard_map/all_to_all | solution.py:603
  128.2 2.2 %copy-start.20 = (f32[32,64,512]{2,1,0:T(8,128)S(1)}, f32[32,64,512]{2,1,0:T(8,128)}, u32[]{:S(2)}) copy-start(f32[32,64,512]{2,1,0:T(8,128)} %copy-done.19) | copy-start | bytes 12582916
  130.4 8.0 %copy-start.11 = (bf16[512,384]{1,0:T(8,128)(2,1)S(1)}, bf16[512,384]{1,0:T(8,128)(2,1)}, u32[]{:S(2)}) copy-start(bf16[512,384]{1,0:T(8,128)(2,1)} %constant.59.clone.ch) | copy-start | bytes 1179652
  130.4 8.0 %copy-start.12 = (bf16[512,384]{1,0:T(8,128)(2,1)S(1)}, bf16[512,384]{1,0:T(8,128)(2,1)}, u32[]{:S(2)}) copy-start(bf16[512,384]{1,0:T(8,128)(2,1)} %constant.60.clone.cl) | copy-start | bytes 1179652
  130.4 8.0 %copy-start.13 = (bf16[512,384]{1,0:T(8,128)(2,1)S(1)}, bf16[512,384]{1,0:T(8,128)(2,1)}, u32[]{:S(2)}) copy-start(bf16[512,384]{1,0:T(8,128)(2,1)} %constant.61.clone.sh) | copy-start | bytes 1179652
  130.4 8.0 %copy-start.14 = (bf16[512,384]{1,0:T(8,128)(2,1)S(1)}, bf16[512,384]{1,0:T(8,128)(2,1)}, u32[]{:S(2)}) copy-start(bf16[512,384]{1,0:T(8,128)(2,1)} %constant.62.clone.sl) | copy-start | bytes 1179652
  130.4 8.0 %copy-start.17 = (bf16[384,288]{1,0:T(8,128)(2,1)S(1)}, bf16[384,288]{1,0:T(8,128)(2,1)}, u32[]{:S(2)}) copy-start(bf16[384,288]{1,0:T(8,128)(2,1)} %constant.63.clone.perm) | copy-start | bytes 663556
  137.2 1.2 copy-start.21
  138.4 1.4 copy-start.22
  (3 other events, 2.2 us)

commit v4 on v3

--- a/solution.py
+++ b/solution.py
@@ -32,7 +32,7 @@
 SQPI = math.sqrt(math.pi)
 F32 = jnp.float32
 BF16 = jnp.bfloat16
-VMEM_LIMIT = 24 * 1024 * 1024
+VMEM_LIMIT = 60 * 1024 * 1024
 
 
 def wave(points, freqs):
@@ -142,30 +142,32 @@
     return jnp.where(off == 0, weights[0], value)
 
 
-def spread_body(charge, frac, cell, xh, xl, out, acc):
+def spread_body(charge, frac, cell, waves_from, out, acc, waves, sem):
     step = pl.program_id(0)
+    copy = pltpu.make_async_copy(waves_from, waves, sem)
 
     @pl.when(step == 0)
     def _():
+        copy.start()
         acc[...] = jnp.zeros_like(acc)
 
     along_x = placed(XE, cell[0:1, :], spline(frac[0:1, :]))
     along_y = placed(YE, cell[1:2, :], spline(frac[1:2, :])) * charge[...]
     along_z = placed(16, cell[2:3, :], spline(frac[2:3, :]))
     plane = jnp.concatenate([along_z[z : z + 1, :] * along_y for z in range(ZE)], 0)
-    acc[...] += three(dot_nt, split(plane), split(along_x))
+    acc[...] += three(dot_nt, split(along_x), split(plane))
 
     @pl.when(step == pl.num_programs(0) - 1)
     def _():
-        freq = three(dot_nn, split(acc[...]), (xh[...], xl[...]))
+        copy.wait()
+        freq = three(dot_tn, split(acc[...]), (waves[0], waves[1]))
         for s in range(N_SLAB):
             for z in range(ZE):
                 out[s, :, z * 24 : z * 24 + 24] = freq[z * YE : z * YE + YE, s * 24 : s * 24 + 24]
             out[s, :, ZE * 24 : 384] = jnp.zeros((YE, 384 - ZE * 24), F32)
 
 
-def spread(charge, frac, cell, xh, xl):
-    whole = pl.BlockSpec((XE, 384), lambda i: (0, 0))
+def spread(charge, frac, cell, waves):
     return pl.pallas_call(
         spread_body,
         grid=(SITES // CHUNK,),
@@ -173,16 +175,19 @@
             pl.BlockSpec((1, CHUNK), lambda i: (0, i)),
             pl.BlockSpec((3, CHUNK), lambda i: (0, i)),
             pl.BlockSpec((3, CHUNK), lambda i: (0, i)),
-            whole,
-            whole,
+            pl.BlockSpec(memory_space=pltpu.HBM),
         ],
         out_specs=pl.BlockSpec((N_SLAB, YE, 384), lambda i: (0, 0, 0)),
         out_shape=jax.ShapeDtypeStruct((N_SLAB, YE, 384), F32),
-        scratch_shapes=[pltpu.VMEM((ZE * YE, XE), F32)],
+        scratch_shapes=[
+            pltpu.VMEM((XE, ZE * YE), F32),
+            pltpu.VMEM((2, XE, 384), BF16),
+            pltpu.SemaphoreType.DMA,
+        ],
         compiler_params=pltpu.CompilerParams(vmem_limit_bytes=VMEM_LIMIT),
         cost_estimate=pl.CostEstimate(flops=8_000_000_000, bytes_accessed=2_000_000, transcendentals=0),
         name="spread",
-    )(charge.reshape(1, SITES), frac, cell, xh, xl)
+    )(charge.reshape(1, SITES), frac, cell, waves)
 
 
 def lanes(tiles):
@@ -202,6 +207,7 @@
     return pl.pallas_call(
         pack_body,
         out_shape=jax.ShapeDtypeStruct((N_SLAB, 8, 128), F32),
+        compiler_params=pltpu.CompilerParams(vmem_limit_bytes=VMEM_LIMIT),
         name="pack",
     )(drive.reshape(1, OWN), atom.reshape(1, OWN), cell, frac)
 
@@ -273,7 +279,7 @@
         in_specs=[pl.BlockSpec(memory_space=pltpu.SMEM)] + [pl.BlockSpec(memory_space=pltpu.VMEM)] * 3,
         out_shape=jax.ShapeDtypeStruct((ROWS, COLS), F32),
         scratch_shapes=[pltpu.VMEM((N_FFT, 8, 128), F32), pltpu.VMEM((8, ROWS), F32), pltpu.VMEM((8, 128), F32)],
-        compiler_params=pltpu.CompilerParams(vmem_limit_bytes=12 * 1024 * 1024),
+        compiler_params=pltpu.CompilerParams(vmem_limit_bytes=VMEM_LIMIT),
         cost_estimate=pl.CostEstimate(flops=100_000_000, bytes_accessed=2_000_000, transcendentals=1_000_000),
         name="couple",
     )(place, pos, width.reshape(1, ATOMS), hard.reshape(1, OWN))
@@ -298,7 +304,7 @@
         first_body,
         out_shape=jax.ShapeDtypeStruct((N_FFT, 40, 128), F32),
         scratch_shapes=[pltpu.VMEM((8, ROWS), F32)],
-        compiler_params=pltpu.CompilerParams(vmem_limit_bytes=12 * 1024 * 1024),
+        compiler_params=pltpu.CompilerParams(vmem_limit_bytes=VMEM_LIMIT),
         name="first_product",
     )(got, matrix)
 
@@ -332,7 +338,7 @@
         y_body,
         out_shape=jax.ShapeDtypeStruct((N_FFT, 16, 384), F32),
         scratch_shapes=[pltpu.VMEM((8, 128), F32)],
-        compiler_params=pltpu.CompilerParams(vmem_limit_bytes=24 * 1024 * 1024),
+        compiler_params=pltpu.CompilerParams(vmem_limit_bytes=VMEM_LIMIT),
         cost_estimate=pl.CostEstimate(flops=4_000_000_000, bytes_accessed=5_000_000, transcendentals=0),
         name="along_y",
     )(*operands)
@@ -357,7 +363,7 @@
         ],
         out_specs=pl.BlockSpec((N_SLAB, 8, 128), lambda i: (0, 0, 0)),
         out_shape=jax.ShapeDtypeStruct((N_SLAB, 8, 128), F32),
-        compiler_params=pltpu.CompilerParams(vmem_limit_bytes=8 * 1024 * 1024),
+        compiler_params=pltpu.CompilerParams(vmem_limit_bytes=VMEM_LIMIT),
         name="quad_sum",
     )(place, got)
 
@@ -416,7 +422,7 @@
         ],
         out_specs=pl.BlockSpec((8, 64, ROWS), lambda i: (i, 0, 0)),
         out_shape=jax.ShapeDtypeStruct((N_FFT, 64, ROWS), F32),
-        compiler_params=pltpu.CompilerParams(vmem_limit_bytes=12 * 1024 * 1024),
+        compiler_params=pltpu.CompilerParams(vmem_limit_bytes=VMEM_LIMIT),
         cost_estimate=pl.CostEstimate(flops=2_000_000_000, bytes_accessed=5_000_000, transcendentals=0),
         name="tables",
     )(place, slots, steps)
@@ -459,7 +465,7 @@
         ],
         out_specs=pl.BlockSpec((8, 32, PAIRS), lambda i: (i, 0, 0)),
         out_shape=jax.ShapeDtypeStruct((N_FFT, 32, PAIRS), F32),
-        compiler_params=pltpu.CompilerParams(vmem_limit_bytes=20 * 1024 * 1024),
+        compiler_params=pltpu.CompilerParams(vmem_limit_bytes=VMEM_LIMIT),
         cost_estimate=pl.CostEstimate(flops=4_000_000_000, bytes_accessed=7_000_000, transcendentals=0),
         name="ml_waves",
     )(charges, slots, waves)
@@ -499,7 +505,7 @@
         early_body,
         out_shape=jax.ShapeDtypeStruct((2, 128, 128), F32),
         scratch_shapes=[pltpu.VMEM((128, 128), F32)],
-        compiler_params=pltpu.CompilerParams(vmem_limit_bytes=12 * 1024 * 1024),
+        compiler_params=pltpu.CompilerParams(vmem_limit_bytes=VMEM_LIMIT),
         cost_estimate=pl.CostEstimate(flops=2_000_000_000, bytes_accessed=1_000_000, transcendentals=0),
         name="early",
     )(slots, first)
@@ -565,35 +571,49 @@
             jax.ShapeDtypeStruct((8, 128), F32),
         ),
         scratch_shapes=[pltpu.VMEM((128, 128), F32), pltpu.VMEM((128, 128), F32)],
-        compiler_params=pltpu.CompilerParams(vmem_limit_bytes=12 * 1024 * 1024),
+        compiler_params=pltpu.CompilerParams(vmem_limit_bytes=VMEM_LIMIT),
         cost_estimate=pl.CostEstimate(flops=1_000_000_000, bytes_accessed=1_000_000, transcendentals=0),
         name="moments",
     )(place, slots, before, first, grid)
 
 
-def z_body(grid, ml, quads, rest, perm, ch, cl, sh, sl, out_re, out_im, out_q):
+def z_body(grid, ml, quads, rest, perm_from, waves_from, out_re, out_im, out_q, perm, waves, sems):
+    copies = [
+        pltpu.make_async_copy(perm_from, perm, sems.at[0]),
+        pltpu.make_async_copy(waves_from, waves, sems.at[1]),
+    ]
+    for copy in copies:
+        copy.start()
     m5 = jnp.sum(quads[:, 0, :], 0, keepdims=True)
     step = guarded(rest[3:4], m5 - rest[2:3], m5)[:, 0:1]
     high, low = split(grid[...].reshape(N_FFT * 16, 384))
+    extra = ml[:, 0:16] + step[None] * ml[:, 16:32]
+    out_q[...] = (rest[0:1] + step * rest[1:2])[:, 0:OWN]
+    copies[0].wait()
     total = dot_nn(high, perm[...]) + dot_nn(low, perm[...])
-    extra = ml[:, 0:16] + step[None] * ml[:, 16:32]
     both = split(total + extra.reshape(N_FFT * 16, PAIRS))
-    cos = three(dot_tn, both, (ch[...], cl[...]))
-    sin = three(dot_tn, both, (sh[...], sl[...]))
+    copies[1].wait()
+    cos = three(dot_tn, both, (waves[0], waves[1]))
+    sin = three(dot_tn, both, (waves[2], waves[3]))
     for k in range(KY):
         for first, count, re in ((0, 8, k * 8), (8, 4, 192 + k * 4)):
             im = re + KY * count
             out_re[k, first : first + count] = cos[re : re + count] + sin[im : im + count]
             out_im[k, first : first + count] = cos[im : im + count] - sin[re : re + count]
-    out_q[...] = (rest[0:1] + step * rest[1:2])[:, 0:OWN]
 
 
 def along_z(*operands):
     shape = jax.ShapeDtypeStruct((KY, KX, NG), F32)
     return pl.pallas_call(
         z_body,
+        in_specs=[pl.BlockSpec(memory_space=pltpu.VMEM)] * 4 + [pl.BlockSpec(memory_space=pltpu.HBM)] * 2,
         out_shape=(shape, shape, jax.ShapeDtypeStruct((1, OWN), F32)),
-        compiler_params=pltpu.CompilerParams(vmem_limit_bytes=20 * 1024 * 1024),
+        scratch_shapes=[
+            pltpu.VMEM((384, PAIRS), BF16),
+            pltpu.VMEM((4, N_FFT * 16, NG), BF16),
+            pltpu.SemaphoreType.DMA((2,)),
+        ],
+        compiler_params=pltpu.CompilerParams(vmem_limit_bytes=VMEM_LIMIT),
         cost_estimate=pl.CostEstimate(flops=3_000_000_000, bytes_accessed=5_000_000, transcendentals=0),
         name="along_z",
     )(*operands)
@@ -622,8 +642,7 @@
     got = swap(pack(ml_drive, slot_atom, slot_cell, slot_frac), "slab")
     matrix = couple(place, ml_pos, ml_width, ml_hard)
     got_1 = swap(first_product(got, matrix), "fft")
-    xh, xl = (jnp.asarray(t) for t in two_parts(x_table()))
-    mm = spread(mm_charge, mm_frac, mm_cell, xh, xl)
+    mm = spread(mm_charge, mm_frac, mm_cell, jnp.asarray(np.stack(two_parts(x_table()))))
     first_cols = jnp.sum(got_1[:, :8], 0)
     part = jnp.sum(matrix * first_cols.reshape(1, COLS), 1)
     tail = jnp.concatenate([part.reshape(4, 128), first_cols[:4], first_cols[4:]], 1)
@@ -646,8 +665,8 @@
     waves = tables(place, got_1, steps)
     charges, rest = moments(place, got_1, early(got_1, first_full), first_full, got_3)
     ml = ml_waves(charges, got_1, waves)
-    ch, cl, sh, sl = (jnp.asarray(t) for half in z_tables() for t in two_parts(half))
-    struct_re, struct_im, charge = along_z(got_3, ml, quads, rest, jnp.asarray(perm_z()), ch, cl, sh, sl)
+    z_waves = jnp.asarray(np.stack([t for half in z_tables() for t in two_parts(half)]))
+    struct_re, struct_im, charge = along_z(got_3, ml, quads, rest, jnp.asarray(perm_z()), z_waves)
     return (charge.reshape(OWN), struct_re, struct_im)
 
 

time: 143 us -> 148 us (1.035)
  Pallas kernels: 50 us -> 67.6 us
  local copies, waits for them, and re-layouts: 16.5 us -> 5.62 us
  starting transfers between devices: 35.4 us -> 32.4 us
  blocking collectives: 31 us -> 33.3 us
  waiting for transfers between devices: 7.96 us -> 5.84 us
    unnamed x46 -> x12, local copies, waits for them, and re-layouts: 14.6 us -> 2.16 us
    pallas_call x1, Pallas kernels: 2.43 us -> 6.13 us  [along_y(): pl.pallas_call(y_body, out_shape=jax.ShapeDtypeStruct((N_FFT, 16, 384), F...]
    all_to_all x4, starting transfers between devices: 35.4 us -> 32.4 us  [swap(): return lax.all_to_all(value, axis, 0, 0, tiled=True)]
    pallas_call x1, Pallas kernels: 2.5 us -> 5.16 us  [along_z(): pl.pallas_call(z_body, in_specs=[pl.BlockSpec(memory_space=pltpu.VMEM)] *...]
    all_to_all x1, blocking collectives: 31 us -> 33.3 us  [swap(): return lax.all_to_all(value, axis, 0, 0, tiled=True)]
    pallas_call x1, Pallas kernels: 6.74 us -> 8.88 us  [ml_waves(): pl.pallas_call(ml_body, grid=(4,), in_specs=[pl.BlockSpec((2, 32, 128), l...]
    all_to_all x4, waiting for transfers between devices: 7.96 us -> 5.84 us  [swap(): return lax.all_to_all(value, axis, 0, 0, tiled=True)]
    pallas_call x1, Pallas kernels: 4.53 us -> 6.63 us  [early(): pl.pallas_call(early_body, out_shape=jax.ShapeDtypeStruct((2, 128, 128),...]
  transfers between devices with their start and end apart: 4 -> 4, of which waited for: 1 -> 2; matrix products, arithmetic and copies ran while one was open for 1% -> 3% of each run, Pallas kernels for 29% -> 34%
where the time goes in v4:
time: 148 us; the launch traced here: 147 us
  Pallas kernels  67.6 us (46%)
  blocking collectives  33.3 us (22%)
  starting transfers between devices  32.4 us (22%)
  waiting for transfers between devices  5.84 us (4%)
  local copies, waits for them, and re-layouts  5.62 us (4%)
  other arithmetic  1.68 us (1%)
    all_to_all x1, blocking collectives, swap(): return lax.all_to_all(value, axis, 0, 0, tiled=True)  33.3 us
    all_to_all x4, starting transfers between devices, swap(): return lax.all_to_all(value, axis, 0, 0, tiled=True)  32.4 us
    pallas_call x1, Pallas kernels, spread(): pl.pallas_call(spread_body, grid=(SITES // CHUNK,), in_specs=[pl.BlockSpe...  15.4 us
    pallas_call x1, Pallas kernels, ml_waves(): pl.pallas_call(ml_body, grid=(4,), in_specs=[pl.BlockSpec((2, 32, 128), l...  8.88 us
    pallas_call x1, Pallas kernels, couple(): pl.pallas_call(couple_body, in_specs=[pl.BlockSpec(memory_space=pltpu.SME...  7.66 us
    pallas_call x1, Pallas kernels, early(): pl.pallas_call(early_body, out_shape=jax.ShapeDtypeStruct((2, 128, 128),...  6.63 us
    pallas_call x1, Pallas kernels, tables(): pl.pallas_call(table_body, grid=(4,), in_specs=[pl.BlockSpec(memory_space...  6.55 us
    pallas_call x1, Pallas kernels, along_y(): pl.pallas_call(y_body, out_shape=jax.ShapeDtypeStruct((N_FFT, 16, 384), F...  6.13 us
  transfers between devices with their start and end apart: 4, of which 2 were waited for; matrix products, arithmetic and copies ran while one was open for 3% of the time, Pallas kernels for 34%

profile of v4, /device:TPU:1, one launch (start us, length us, event | category | flops | bytes accessed | tf_op | source)
XLA Modules:
  0.0 147.4 jit_solution(8921895655213397947)
XLA Ops:
  0.6 1.4 pack.1
  2.0 10.2 %all-to-all-start = ((f32[16,8,128]{2,1,0:T(8,128)}), f32[16,8,128]{2,1,0:T(8,128)S(1)}, u32[]{:S(2)}, u32[]{:S(2)}) async-start(f32[16,8,128]{2,1,0:T(8,128)} %pack.1), calls=%async_computation | async-start | bytes 131072 | tf_op jit(solution)/shard_map/all_to_all | solution.py:623
  12.8 7.7 %couple.1.matrix = f32[512,1024]{1,0:T(8,128)} custom-call(s32[2]{0:T(128)} %pad_add_fusion.place, f32[3,16384]{1,0:T(4,128)} %pos.1, f32[1,16384]{1,0:T(1,128)} %bitcast.20, f32[1,32]{1,0:T(1,128)} %bitcast.25), custom_call_target="tpu_custom_call" | custom-call | flops 100000000 | bytes 2000000 | tf_op jit(solution)/shard_map/couple/pallas_call | solution.py:277
  21.1 2.9 %first_product.1 = f32[32,40,128]{2,1,0:T(8,128)} custom-call(f32[16,8,128]{2,1,0:T(8,128)} %copy-done.4, f32[512,1024]{1,0:T(8,128)} %couple.1.matrix), custom_call_target="tpu_custom_call" | custom-call | tf_op jit(solution)/shard_map/first_product/pallas_call | solution.py:303
  24.0 11.4 %all-to-all-start.1 = ((f32[32,40,128]{2,1,0:T(8,128)}), f32[32,40,128]{2,1,0:T(8,128)S(1)}, u32[]{:S(2)}, u32[]{:S(2)}) async-start(f32[32,40,128]{2,1,0:T(8,128)} %first_product.1), calls=%async_computation.1 | async-start | bytes 1310720 | tf_op jit(solution)/shard_map/all_to_all | solution.py:623
  35.4 15.4 %spread.1 = f32[16,32,384]{2,1,0:T(8,128)} custom-call(f32[1,6144]{1,0:T(1,128)} %bitcast.26, f32[3,6144]{1,0:T(4,128)} %frac.2, s32[3,6144]{1,0:T(4,128)} %cell.2, bf16[2,392,384]{2,1,0:T(8,128)(2,1)} %constant.42.clone.waves_from), custom_call_target="tpu_custom_call" | custom-call | flops 8000000000 | bytes 2000000 | tf_op jit(solution)/shard_map/spread/pallas_call | solution.py:171
  50.8 1.5 %all-to-all-done.1.slots = f32[32,40,128]{2,1,0:T(8,128)S(1)} async-done(((f32[32,40,128]{2,1,0:T(8,128)}), f32[32,40,128]{2,1,0:T(8,128)S(1)}, u32[]{:S(2)}, u32[]{:S(2)}) %all-to-all-start.1) | async-done | bytes 655392 | tf_op jit(solution)/shard_map/all_to_all | solution.py:623
  52.7 33.3 %all_to_all.25.grid = f32[16,32,384]{2,1,0:T(8,128)} all-to-all(f32[16,32,384]{2,1,0:T(8,128)S(1)} %pad_maximum_fusion), channel_id=1, replica_groups=mesh['fft'=32,'slab'=16] {'slab'}, dimensions={0} | all-to-all | bytes 1572864 | tf_op jit(solution)/shard_map/all_to_all | solution.py:623
  86.1 6.1 %along_y.1 = f32[32,16,384]{2,1,0:T(8,128)} custom-call(f32[16,32,384]{2,1,0:T(8,128)} %all_to_all.25.grid, f32[512,1024]{1,0:T(8,128)} %couple.1.matrix, bf16[384,384]{1,0:T(8,128)(2,1)} %constant.47.clone.perm, bf16[512,768]{1,0:T(8,128)(2,1)} %constant.43.clone.arh, bf16[512,768]{1,0:T(8,128)(2,1)} %constant.44.clone.arl, ...), custom_call_target="tpu_custom_call" | custom-call | flops 4000000000 | bytes 5000000 | tf_op jit(solution)/shard_map/along_y/pallas_call | solution.py:337
  92.2 6.0 %all-to-all-start.3 = ((f32[32,16,384]{2,1,0:T(8,128)}), f32[32,16,384]{2,1,0:T(8,128)S(1)}, u32[]{:S(2)}, u32[]{:S(2)}) async-start(f32[32,16,384]{2,1,0:T(8,128)} %along_y.1), calls=%async_computation.3 | async-start | bytes 1572864 | tf_op jit(solution)/shard_map/all_to_all | solution.py:623
  98.2 0.7 dynamic-slice_bitcast_fusion
  99.0 0.7 dynamic-slice_bitcast_fusion.1
  99.7 0.7 pad_maximum_fusion.2.steps
  100.4 6.6 %tables.1.waves = f32[32,64,512]{2,1,0:T(8,128)} custom-call(s32[2]{0:T(128)} %pad_add_fusion.place, f32[32,40,128]{2,1,0:T(8,128)} %copy-done.2, f32[16,16]{1,0:T(8,128)} %pad_maximum_fusion.2.steps), custom_call_target="tpu_custom_call" | custom-call | flops 2000000000 | bytes 5000000 | tf_op jit(solution)/shard_map/tables/pallas_call | solution.py:415
  107.0 0.9 fusion
  108.2 0.7 reshape.43.first
  108.9 6.6 %early.1.before = f32[2,128,128]{2,1,0:T(8,128)} custom-call(f32[32,40,128]{2,1,0:T(8,128)} %copy-done.2, f32[128,128]{1,0:T(8,128)} %reshape.43.first), custom_call_target="tpu_custom_call" | custom-call | flops 2000000000 | bytes 1000000 | tf_op jit(solution)/shard_map/early/pallas_call | solution.py:504
  115.5 4.3 %all-to-all-done.3.grid.got = f32[32,16,384]{2,1,0:T(8,128)S(1)} async-done(((f32[32,16,384]{2,1,0:T(8,128)}), f32[32,16,384]{2,1,0:T(8,128)S(1)}, u32[]{:S(2)}, u32[]{:S(2)}) %all-to-all-start.3) | async-done | bytes 786464 | tf_op jit(solution)/shard_map/all_to_all | solution.py:623
  119.9 0.9 copy-done.1
  120.7 1.9 %quad_sum.1 = f32[16,8,128]{2,1,0:T(8,128)} custom-call(s32[2]{0:T(128)} %pad_add_fusion.place, f32[32,16,384]{2,1,0:T(8,128)} %copy-done.1), custom_call_target="tpu_custom_call" | custom-call | tf_op jit(solution)/shard_map/quad_sum/pallas_call | solution.py:357
  122.6 4.9 %all-to-all-start.4 = ((f32[16,8,128]{2,1,0:T(8,128)}), f32[16,8,128]{2,1,0:T(8,128)S(1)}, u32[]{:S(2)}, u32[]{:S(2)}) async-start(f32[16,8,128]{2,1,0:T(8,128)} %quad_sum.1), calls=%async_computation.4 | async-start | bytes 131072 | tf_op jit(solution)/shard_map/all_to_all | solution.py:623
  127.5 5.0 %moments.1 = (f32[2,128,128]{2,1,0:T(8,128)}, f32[8,128]{1,0:T(8,128)}) custom-call(s32[2]{0:T(128)} %pad_add_fusion.place, f32[32,40,128]{2,1,0:T(8,128)} %copy-done.2, f32[2,128,128]{2,1,0:T(8,128)} %early.1.before, f32[128,128]{1,0:T(8,128)} %reshape.43.first, f32[32,16,384]{2,1,0:T(8,128)} %copy-done.1), custom_call_target="tpu_custom_call" | custom-call | flops 1000000000 | bytes 1000000 | tf_op jit(solution)/shard_map/moments/pallas_call | solution.py:555
  132.5 8.9 %ml_waves.1.ml = f32[32,32,288]{2,1,0:T(8,128)} custom-call(f32[2,128,128]{2,1,0:T(8,128)} %get-tuple-element.8.charges, f32[32,40,128]{2,1,0:T(8,128)} %copy-done.2, f32[32,64,512]{2,1,0:T(8,128)} %tables.1.waves), custom_call_target="tpu_custom_call" | custom-call | flops 4000000000 | bytes 7000000 | tf_op jit(solution)/shard_map/ml_waves/pallas_call | solution.py:458
  142.0 5.2 %along_z.1 = (f32[12,12,384]{2,1,0:T(8,128)}, f32[12,12,384]{2,1,0:T(8,128)}, f32[1,32]{1,0:T(1,128)}) custom-call(f32[32,16,384]{2,1,0:T(8,128)} %copy-done.1, f32[32,32,288]{2,1,0:T(8,128)} %ml_waves.1.ml, f32[16,8,128]{2,1,0:T(8,128)} %copy-done.5, f32[8,128]{1,0:T(8,128)} %get-tuple-element.9.rest, bf16[384,288]{1,0:T(8,128)(2,1)} %constant.51.clone.perm_from, ...), custom_call_target="tpu_custom_call" | custom-call | flops 3000000000 | bytes 5000000 | tf_op jit(solution)/shard_map/along_z/pallas_call | solution.py:607
  (25 shorter events, 2.7 us)
Async XLA Ops:
  2.0 18.5 %all-to-all-start = ((f32[16,8,128]{2,1,0:T(8,128)}), f32[16,8,128]{2,1,0:T(8,128)S(1)}, u32[]{:S(2)}, u32[]{:S(2)}) async-start(f32[16,8,128]{2,1,0:T(8,128)} %pack.1), calls=%async_computation | async-start | bytes 131072 | tf_op jit(solution)/shard_map/all_to_all | solution.py:623
  20.5 0.6 copy-start.4
  24.0 28.3 %all-to-all-start.1 = ((f32[32,40,128]{2,1,0:T(8,128)}), f32[32,40,128]{2,1,0:T(8,128)S(1)}, u32[]{:S(2)}, u32[]{:S(2)}) async-start(f32[32,40,128]{2,1,0:T(8,128)} %first_product.1), calls=%async_computation.1 | async-start | bytes 1310720 | tf_op jit(solution)/shard_map/all_to_all | solution.py:623
  35.4 17.0 %copy-start = (f32[512,1024]{1,0:T(8,128)S(1)}, f32[512,1024]{1,0:T(8,128)}, u32[]{:S(2)}) copy-start(f32[512,1024]{1,0:T(8,128)} %couple.1.matrix) | copy-start | bytes 6291460
  50.8 1.8 %copy-start.3 = (f32[16,32,384]{2,1,0:T(8,128)S(1)}, f32[16,32,384]{2,1,0:T(8,128)}, u32[]{:S(2)}) copy-start(f32[16,32,384]{2,1,0:T(8,128)} %spread.1) | copy-start | bytes 2359300
  52.3 33.7 %copy-start.2 = (f32[32,40,128]{2,1,0:T(8,128)}, f32[32,40,128]{2,1,0:T(8,128)S(1)}, u32[]{:S(2)}) copy-start(f32[32,40,128]{2,1,0:T(8,128)S(1)} %all-to-all-done.1.slots) | copy-start | bytes 1966084
  92.2 27.7 %all-to-all-start.3 = ((f32[32,16,384]{2,1,0:T(8,128)}), f32[32,16,384]{2,1,0:T(8,128)S(1)}, u32[]{:S(2)}, u32[]{:S(2)}) async-start(f32[32,16,384]{2,1,0:T(8,128)} %along_y.1), calls=%async_computation.3 | async-start | bytes 1572864 | tf_op jit(solution)/shard_map/all_to_all | solution.py:623
  119.8 0.9 copy-start.1
  122.6 18.7 %all-to-all-start.4 = ((f32[16,8,128]{2,1,0:T(8,128)}), f32[16,8,128]{2,1,0:T(8,128)S(1)}, u32[]{:S(2)}, u32[]{:S(2)}) async-start(f32[16,8,128]{2,1,0:T(8,128)} %quad_sum.1), calls=%async_computation.4 | async-start | bytes 131072 | tf_op jit(solution)/shard_map/all_to_all | solution.py:623
  141.4 0.6 copy-start.5

commit v5 on v4

--- a/solution.py
+++ b/solution.py
@@ -32,7 +32,8 @@
 SQPI = math.sqrt(math.pi)
 F32 = jnp.float32
 BF16 = jnp.bfloat16
-VMEM_LIMIT = 60 * 1024 * 1024
+MOST = 60 * 1024 * 1024
+SOME = 12 * 1024 * 1024
 
 
 def wave(points, freqs):
@@ -184,7 +185,7 @@
             pltpu.VMEM((2, XE, 384), BF16),
             pltpu.SemaphoreType.DMA,
         ],
-        compiler_params=pltpu.CompilerParams(vmem_limit_bytes=VMEM_LIMIT),
+        compiler_params=pltpu.CompilerParams(vmem_limit_bytes=MOST),
         cost_estimate=pl.CostEstimate(flops=8_000_000_000, bytes_accessed=2_000_000, transcendentals=0),
         name="spread",
     )(charge.reshape(1, SITES), frac, cell, waves)
@@ -194,22 +195,53 @@
     return jnp.concatenate([tiles[i : i + 1] for i in range(tiles.shape[0])], 1)
 
 
-def pack_body(drive, atom, cell, frac, out):
+def pack_body(place, drive, atom, cell, frac, hard, pos, width, out, cols, rows, picked):
+    f, s = place[0], place[1]
     out[...] = jnp.zeros_like(out)
     for i in range(N_SLAB):
         out[i, 0:1, 0:OWN] = -drive[...]
         out[i, 1:2, 0:OWN] = atom[...].astype(F32)
         out[i, 2:5, 0:OWN] = cell[...].astype(F32)
         out[i, 5:8, 0:OWN] = frac[...]
-
-
-def pack(drive, atom, cell, frac):
+    for j in range(N_FFT):
+        at = pl.multiple_of(j * ROWS + (s >> 2) * 128, 128)
+        picked[j, 0:3, :] = pos[:, pl.ds(at, 128)]
+        picked[j, 3:4, :] = width[:, pl.ds(at, 128)]
+    lane = lax.broadcasted_iota(jnp.int32, (8, 128), 1) >> 5
+    for tile in range(COLS // 128):
+        value = jnp.zeros((8, 128), F32)
+        for j in range(4):
+            value = jnp.where(lane == j, pltpu.roll(picked[tile * 4 + j], ((j - (s & 3)) & 3) * OWN, 1), value)
+        cols[:, tile * 128 : tile * 128 + 128] = value
+    at = pl.multiple_of(f * ROWS, 128)
+    rows[...] = jnp.zeros_like(rows)
+    rows[0:3, :] = pos[:, pl.ds(at, ROWS)]
+    rows[3:4, :] = width[:, pl.ds(at, ROWS)]
+    rows[4:5, 0:OWN] = hard[...]
+
+
+def pack(place, drive, atom, cell, frac, hard, pos, width):
     return pl.pallas_call(
         pack_body,
-        out_shape=jax.ShapeDtypeStruct((N_SLAB, 8, 128), F32),
-        compiler_params=pltpu.CompilerParams(vmem_limit_bytes=VMEM_LIMIT),
+        in_specs=[pl.BlockSpec(memory_space=pltpu.SMEM)] + [pl.BlockSpec(memory_space=pltpu.VMEM)] * 7,
+        out_shape=(
+            jax.ShapeDtypeStruct((N_SLAB, 8, 128), F32),
+            jax.ShapeDtypeStruct((8, COLS), F32),
+            jax.ShapeDtypeStruct((8, ROWS), F32),
+        ),
+        scratch_shapes=[pltpu.VMEM((N_FFT, 8, 128), F32)],
+        compiler_params=pltpu.CompilerParams(vmem_limit_bytes=MOST),
         name="pack",
-    )(drive.reshape(1, OWN), atom.reshape(1, OWN), cell, frac)
+    )(
+        place,
+        drive.reshape(1, OWN),
+        atom.reshape(1, OWN),
+        cell,
+        frac,
+        hard.reshape(1, OWN),
+        pos,
+        width.reshape(1, ATOMS),
+    )
 
 
 def erf_ratio(value):
@@ -230,26 +262,12 @@
     return value * p, q
 
 
-def couple_body(place, pos, width, hard, out, picked, rows, own):
+def couple_body(place, cols_ref, rows, out, own):
     f, s = place[0], place[1]
-    lane = lax.broadcasted_iota(jnp.int32, (8, 128), 1) >> 5
-    for j in range(N_FFT):
-        at = pl.multiple_of(j * ROWS + (s >> 2) * 128, 128)
-        picked[j, 0:3, :] = pos[:, pl.ds(at, 128)]
-        picked[j, 3:4, :] = width[:, pl.ds(at, 128)]
-    tiles = []
-    for tile in range(COLS // 128):
-        value = jnp.zeros((8, 128), F32)
-        for j in range(4):
-            value = jnp.where(lane == j, pltpu.roll(picked[tile * 4 + j], ((j - (s & 3)) & 3) * OWN, 1), value)
-        tiles.append(value)
-    cols = jnp.concatenate(tiles, 1)
-    at = pl.multiple_of(f * ROWS, 128)
-    rows[0:3, :] = pos[:, pl.ds(at, ROWS)]
-    rows[3:4, :] = width[:, pl.ds(at, ROWS)]
+    cols = cols_ref[...]
     side = jnp.transpose(rows[...])
     own[...] = jnp.zeros_like(own)
-    own[0:1, 0:OWN] = hard[...]
+    own[0:1, 0:OWN] = rows[4:5, 0:OWN]
     own_hard = pltpu.roll(own[...], (f & 3) * OWN, 1)[0:1]
     diag = jnp.concatenate([jnp.where((f >> 2) == t, own_hard, 0.0) for t in range(COLS // 128)], 1)
     diag = diag + KE * (1.0 / (cols[3:4] * SQPI) - 2.0 * ALPHA / SQPI)
@@ -273,16 +291,16 @@
         out[first : first + step] = jnp.where(row_id == col_id, diag, value)
 
 
-def couple(place, pos, width, hard):
+def couple(place, cols, rows):
     return pl.pallas_call(
         couple_body,
-        in_specs=[pl.BlockSpec(memory_space=pltpu.SMEM)] + [pl.BlockSpec(memory_space=pltpu.VMEM)] * 3,
+        in_specs=[pl.BlockSpec(memory_space=pltpu.SMEM)] + [pl.BlockSpec(memory_space=pltpu.VMEM)] * 2,
         out_shape=jax.ShapeDtypeStruct((ROWS, COLS), F32),
-        scratch_shapes=[pltpu.VMEM((N_FFT, 8, 128), F32), pltpu.VMEM((8, ROWS), F32), pltpu.VMEM((8, 128), F32)],
-        compiler_params=pltpu.CompilerParams(vmem_limit_bytes=VMEM_LIMIT),
+        scratch_shapes=[pltpu.VMEM((8, 128), F32)],
+        compiler_params=pltpu.CompilerParams(vmem_limit_bytes=SOME),
         cost_estimate=pl.CostEstimate(flops=100_000_000, bytes_accessed=2_000_000, transcendentals=1_000_000),
         name="couple",
-    )(place, pos, width.reshape(1, ATOMS), hard.reshape(1, OWN))
+    )(place, cols, rows)
 
 
 def first_body(got, matrix, out, slots):
@@ -304,7 +322,7 @@
         first_body,
         out_shape=jax.ShapeDtypeStruct((N_FFT, 40, 128), F32),
         scratch_shapes=[pltpu.VMEM((8, ROWS), F32)],
-        compiler_params=pltpu.CompilerParams(vmem_limit_bytes=VMEM_LIMIT),
+        compiler_params=pltpu.CompilerParams(vmem_limit_bytes=SOME),
         name="first_product",
     )(got, matrix)
 
@@ -338,7 +356,7 @@
         y_body,
         out_shape=jax.ShapeDtypeStruct((N_FFT, 16, 384), F32),
         scratch_shapes=[pltpu.VMEM((8, 128), F32)],
-        compiler_params=pltpu.CompilerParams(vmem_limit_bytes=VMEM_LIMIT),
+        compiler_params=pltpu.CompilerParams(vmem_limit_bytes=2 * SOME),
         cost_estimate=pl.CostEstimate(flops=4_000_000_000, bytes_accessed=5_000_000, transcendentals=0),
         name="along_y",
     )(*operands)
@@ -363,7 +381,7 @@
         ],
         out_specs=pl.BlockSpec((N_SLAB, 8, 128), lambda i: (0, 0, 0)),
         out_shape=jax.ShapeDtypeStruct((N_SLAB, 8, 128), F32),
-        compiler_params=pltpu.CompilerParams(vmem_limit_bytes=VMEM_LIMIT),
+        compiler_params=pltpu.CompilerParams(vmem_limit_bytes=SOME),
         name="quad_sum",
     )(place, got)
 
@@ -422,53 +440,10 @@
         ],
         out_specs=pl.BlockSpec((8, 64, ROWS), lambda i: (i, 0, 0)),
         out_shape=jax.ShapeDtypeStruct((N_FFT, 64, ROWS), F32),
-        compiler_params=pltpu.CompilerParams(vmem_limit_bytes=VMEM_LIMIT),
+        compiler_params=pltpu.CompilerParams(vmem_limit_bytes=SOME),
         cost_estimate=pl.CostEstimate(flops=2_000_000_000, bytes_accessed=5_000_000, transcendentals=0),
         name="tables",
     )(place, slots, steps)
-
-
-def ml_body(charges, slots, waves, out):
-    upper = lax.broadcasted_iota(jnp.int32, (8, 1), 0) < 4
-    for g in range(8):
-        rows = slot_rows(slots, g)
-        placed_z = placed(16, rows[4:5].astype(jnp.int32), spline(rows[7:8]))
-        both = [placed_z * lanes(charges[v, g * 4 : g * 4 + 4, :]) for v in range(2)]
-        z_high, z_low = split(jnp.concatenate(both, 0))
-        x_re, x_im = waves[g, 0:8], waves[g, 16:24]
-        parts_re, parts_im = [], []
-        for k in range(KY):
-            y_re, y_im = waves[g, 32 + k : 33 + k], waves[g, 48 + k : 49 + k]
-            parts_re.append(y_re * x_re - y_im * x_im)
-            parts_im.append(y_re * x_im + y_im * x_re)
-        parts = parts_re + parts_im
-        x_re, x_im = waves[g, 8:16], waves[g, 24:32]
-        parts_re, parts_im = [], []
-        for k in range(0, KY, 2):
-            y_re = jnp.where(upper, waves[g, 32 + k : 33 + k], waves[g, 33 + k : 34 + k])
-            y_im = jnp.where(upper, waves[g, 48 + k : 49 + k], waves[g, 49 + k : 50 + k])
-            parts_re.append(y_re * x_re - y_im * x_im)
-            parts_im.append(y_re * x_im + y_im * x_re)
-        high, low = split(jnp.concatenate(parts + parts_re + parts_im, 0))
-        total = dot_nt(jnp.concatenate([z_high, z_low], 0), high)
-        out[g] = total[:32] + total[32:] + dot_nt(z_high, low)
-
-
-def ml_waves(charges, slots, waves):
-    return pl.pallas_call(
-        ml_body,
-        grid=(4,),
-        in_specs=[
-            pl.BlockSpec((2, 32, 128), lambda i: (0, i, 0)),
-            pl.BlockSpec((8, 40, 128), lambda i: (i, 0, 0)),
-            pl.BlockSpec((8, 64, ROWS), lambda i: (i, 0, 0)),
-        ],
-        out_specs=pl.BlockSpec((8, 32, PAIRS), lambda i: (i, 0, 0)),
-        out_shape=jax.ShapeDtypeStruct((N_FFT, 32, PAIRS), F32),
-        compiler_params=pltpu.CompilerParams(vmem_limit_bytes=VMEM_LIMIT),
-        cost_estimate=pl.CostEstimate(flops=4_000_000_000, bytes_accessed=7_000_000, transcendentals=0),
-        name="ml_waves",
-    )(charges, slots, waves)
 
 
 def guarded(value, pivot, scale):
@@ -505,16 +480,22 @@
         early_body,
         out_shape=jax.ShapeDtypeStruct((2, 128, 128), F32),
         scratch_shapes=[pltpu.VMEM((128, 128), F32)],
-        compiler_params=pltpu.CompilerParams(vmem_limit_bytes=VMEM_LIMIT),
+        compiler_params=pltpu.CompilerParams(vmem_limit_bytes=SOME),
         cost_estimate=pl.CostEstimate(flops=2_000_000_000, bytes_accessed=1_000_000, transcendentals=0),
         name="early",
     )(slots, first)
 
 
-def moment_body(place, slots, before, first, grid, charges, rest, v2, late):
+def late_body(place, slots, before, first, grid, perm, waves_from, out, rest, v2, late, charges, waves, sems):
+    copies = [
+        pltpu.make_async_copy(waves_from.at[pl.ds(i * 8, 8)], waves.at[pl.ds(i * 8, 8)], sems.at[i])
+        for i in range(4)
+    ]
+    for copy in copies:
+        copy.start()
     f, s = place[0], place[1]
     for i in range(4):
-        pieces = [grid[:, i * 4 + j, 96:128] for j in range(4)]
+        pieces = [grid[:, i * 4 + j, 352:384] for j in range(4)]
         v2[pl.ds(i, N_FFT, stride=4), :] = jnp.concatenate(pieces, 1)
     high, low = split(v2[...])
     both = jnp.concatenate([high, low], 1)
@@ -550,49 +531,73 @@
     rest[2:3] = jnp.broadcast_to(l20 * m3 + l21 * e12, (1, 128))
     rest[3:4] = jnp.broadcast_to(g2, (1, 128))
 
-
-def moments(place, slots, before, first, grid):
-    return pl.pallas_call(
-        moment_body,
-        grid=(1,),
-        in_specs=[
-            pl.BlockSpec(memory_space=pltpu.SMEM),
-            pl.BlockSpec((N_FFT, 40, 128), lambda i: (0, 0, 0)),
-            pl.BlockSpec((2, 128, 128), lambda i: (0, 0, 0)),
-            pl.BlockSpec((128, 128), lambda i: (0, 0)),
-            pl.BlockSpec((N_FFT, 16, 128), lambda i: (0, 0, 2)),
-        ],
-        out_specs=(
-            pl.BlockSpec((2, 128, 128), lambda i: (0, 0, 0)),
-            pl.BlockSpec((8, 128), lambda i: (0, 0)),
-        ),
+    upper = lax.broadcasted_iota(jnp.int32, (8, 1), 0) < 4
+
+    def group(i, carry):
+        at = pl.multiple_of(i * 16, 16)
+        charge = [charges[v, pl.ds(at, 16), :] for v in range(2)]
+        high, low = split(grid[pl.ds(i * 4, 4)].reshape(64, 384))
+        base = (dot_nn(high, perm[...]) + dot_nn(low, perm[...])).reshape(4, 16, PAIRS)
+        for j in range(4):
+            g = i * 4 + j
+            rows = slot_rows(slots, g)
+            placed_z = placed(16, rows[4:5].astype(jnp.int32), spline(rows[7:8]))
+            both = [placed_z * lanes(charge[v][j * 4 : j * 4 + 4]) for v in range(2)]
+            z_high, z_low = split(jnp.concatenate(both, 0))
+            x_re, x_im = waves[g, 0:8], waves[g, 16:24]
+            parts_re, parts_im = [], []
+            for k in range(KY):
+                y_re, y_im = waves[g, 32 + k : 33 + k], waves[g, 48 + k : 49 + k]
+                parts_re.append(y_re * x_re - y_im * x_im)
+                parts_im.append(y_re * x_im + y_im * x_re)
+            parts = parts_re + parts_im
+            x_re, x_im = waves[g, 8:16], waves[g, 24:32]
+            parts_re, parts_im = [], []
+            for k in range(0, KY, 2):
+                y_re = jnp.where(upper, waves[g, 32 + k : 33 + k], waves[g, 33 + k : 34 + k])
+                y_im = jnp.where(upper, waves[g, 48 + k : 49 + k], waves[g, 49 + k : 50 + k])
+                parts_re.append(y_re * x_re - y_im * x_im)
+                parts_im.append(y_re * x_im + y_im * x_re)
+            high, low = split(jnp.concatenate(parts + parts_re + parts_im, 0))
+            total = dot_nt(jnp.concatenate([z_high, z_low], 0), high)
+            total = total[:32] + total[32:] + dot_nt(z_high, low)
+            out[g, 0:16] = total[:16] + base[j]
+            out[g, 16:32] = total[16:]
+        return carry
+
+    for i in range(4):
+        copies[i].wait()
+        lax.fori_loop(i * 2, i * 2 + 2, group, 0)
+
+
+def late_waves(*operands):
+    return pl.pallas_call(
+        late_body,
+        in_specs=[pl.BlockSpec(memory_space=pltpu.SMEM)]
+        + [pl.BlockSpec(memory_space=pltpu.VMEM)] * 5
+        + [pl.BlockSpec(memory_space=pl.ANY)],
         out_shape=(
-            jax.ShapeDtypeStruct((2, 128, 128), F32),
+            jax.ShapeDtypeStruct((N_FFT, 32, PAIRS), F32),
             jax.ShapeDtypeStruct((8, 128), F32),
         ),
-        scratch_shapes=[pltpu.VMEM((128, 128), F32), pltpu.VMEM((128, 128), F32)],
-        compiler_params=pltpu.CompilerParams(vmem_limit_bytes=VMEM_LIMIT),
-        cost_estimate=pl.CostEstimate(flops=1_000_000_000, bytes_accessed=1_000_000, transcendentals=0),
-        name="moments",
-    )(place, slots, before, first, grid)
-
-
-def z_body(grid, ml, quads, rest, perm_from, waves_from, out_re, out_im, out_q, perm, waves, sems):
-    copies = [
-        pltpu.make_async_copy(perm_from, perm, sems.at[0]),
-        pltpu.make_async_copy(waves_from, waves, sems.at[1]),
-    ]
-    for copy in copies:
-        copy.start()
+        scratch_shapes=[
+            pltpu.VMEM((128, 128), F32),
+            pltpu.VMEM((128, 128), F32),
+            pltpu.VMEM((2, 128, 128), F32),
+            pltpu.VMEM((N_FFT, 64, ROWS), F32),
+            pltpu.SemaphoreType.DMA((4,)),
+        ],
+        compiler_params=pltpu.CompilerParams(vmem_limit_bytes=MOST),
+        cost_estimate=pl.CostEstimate(flops=5_000_000_000, bytes_accessed=7_000_000, transcendentals=0),
+        name="late_waves",
+    )(*operands)
+
+
+def z_body(ml, quads, rest, waves, out_re, out_im, out_q):
     m5 = jnp.sum(quads[:, 0, :], 0, keepdims=True)
     step = guarded(rest[3:4], m5 - rest[2:3], m5)[:, 0:1]
-    high, low = split(grid[...].reshape(N_FFT * 16, 384))
-    extra = ml[:, 0:16] + step[None] * ml[:, 16:32]
-    out_q[...] = (rest[0:1] + step * rest[1:2])[:, 0:OWN]
-    copies[0].wait()
-    total = dot_nn(high, perm[...]) + dot_nn(low, perm[...])
-    both = split(total + extra.reshape(N_FFT * 16, PAIRS))
-    copies[1].wait()
+    total = ml[:, 0:16] + step[None] * ml[:, 16:32]
+    both = split(total.reshape(N_FFT * 16, PAIRS))
     cos = three(dot_tn, both, (waves[0], waves[1]))
     sin = three(dot_tn, both, (waves[2], waves[3]))
     for k in range(KY):
@@ -600,20 +605,15 @@
             im = re + KY * count
             out_re[k, first : first + count] = cos[re : re + count] + sin[im : im + count]
             out_im[k, first : first + count] = cos[im : im + count] - sin[re : re + count]
+    out_q[...] = (rest[0:1] + step * rest[1:2])[:, 0:OWN]
 
 
 def along_z(*operands):
     shape = jax.ShapeDtypeStruct((KY, KX, NG), F32)
     return pl.pallas_call(
         z_body,
-        in_specs=[pl.BlockSpec(memory_space=pltpu.VMEM)] * 4 + [pl.BlockSpec(memory_space=pltpu.HBM)] * 2,
         out_shape=(shape, shape, jax.ShapeDtypeStruct((1, OWN), F32)),
-        scratch_shapes=[
-            pltpu.VMEM((384, PAIRS), BF16),
-            pltpu.VMEM((4, N_FFT * 16, NG), BF16),
-            pltpu.SemaphoreType.DMA((2,)),
-        ],
-        compiler_params=pltpu.CompilerParams(vmem_limit_bytes=VMEM_LIMIT),
+        compiler_params=pltpu.CompilerParams(vmem_limit_bytes=2 * SOME),
         cost_estimate=pl.CostEstimate(flops=3_000_000_000, bytes_accessed=5_000_000, transcendentals=0),
         name="along_z",
     )(*operands)
@@ -639,8 +639,9 @@
     s = lax.axis_index("slab")
     place = jnp.stack([f, s]).astype(jnp.int32)
 
-    got = swap(pack(ml_drive, slot_atom, slot_cell, slot_frac), "slab")
-    matrix = couple(place, ml_pos, ml_width, ml_hard)
+    sent, cols, rows = pack(place, ml_drive, slot_atom, slot_cell, slot_frac, ml_hard, ml_pos, ml_width)
+    got = swap(sent, "slab")
+    matrix = couple(place, cols, rows)
     got_1 = swap(first_product(got, matrix), "fft")
     mm = spread(mm_charge, mm_frac, mm_cell, jnp.asarray(np.stack(two_parts(x_table()))))
     first_cols = jnp.sum(got_1[:, :8], 0)
@@ -663,10 +664,10 @@
         1,
     )
     waves = tables(place, got_1, steps)
-    charges, rest = moments(place, got_1, early(got_1, first_full), first_full, got_3)
-    ml = ml_waves(charges, got_1, waves)
+    before = early(got_1, first_full)
+    ml, rest = late_waves(place, got_1, before, first_full, got_3, jnp.asarray(perm_z()), waves)
     z_waves = jnp.asarray(np.stack([t for half in z_tables() for t in two_parts(half)]))
-    struct_re, struct_im, charge = along_z(got_3, ml, quads, rest, jnp.asarray(perm_z()), z_waves)
+    struct_re, struct_im, charge = along_z(ml, quads, rest, z_waves)
     return (charge.reshape(OWN), struct_re, struct_im)
 
 

time: 148 us -> 141 us (0.953)
  Pallas kernels: 67.6 us -> 53.7 us
  waiting for transfers between devices: 5.84 us -> 9.6 us
  local copies, waits for them, and re-layouts: 5.62 us -> 9.05 us
    unnamed x12 -> x38, local copies, waits for them, and re-layouts: 2.16 us -> 7.1 us
    all_to_all x4, waiting for transfers between devices: 5.84 us -> 9.6 us  [swap(): return lax.all_to_all(value, axis, 0, 0, tiled=True)]
    pallas_call x1, Pallas kernels: 6.13 us -> 2.43 us  [along_y(): pl.pallas_call(y_body, out_shape=jax.ShapeDtypeStruct((N_FFT, 16, 384), F...]
    pallas_call x4 -> x3, Pallas kernels: 20.4 us -> 17.8 us  [the longest x1 14.1 us: late_waves(): pl.pallas_call(late_body, in_specs=[pl.BlockSpec(memory_space=pltpu.SMEM)...]
    pallas_call x1, Pallas kernels: 6.63 us -> 4.53 us  [early(): pl.pallas_call(early_body, out_shape=jax.ShapeDtypeStruct((2, 128, 128),...]
    pallas_call x1, Pallas kernels: 7.66 us -> 5.81 us  [couple(): pl.pallas_call(couple_body, in_specs=[pl.BlockSpec(memory_space=pltpu.SME...]
    pallas_call x1, Pallas kernels: 2.88 us -> 1.28 us  [first_product(): pl.pallas_call(first_body, out_shape=jax.ShapeDtypeStruct((N_FFT, 40, 128...]
  transfers between devices with their start and end apart: 4 -> 4, of which waited for: 2 -> 2; matrix products, arithmetic and copies ran while one was open for 3% -> 1% of each run, Pallas kernels for 34% -> 32%
where the time goes in v5:
time: 141 us; the launch traced here: 140 us
  Pallas kernels  53.7 us (38%)
  blocking collectives  33.5 us (24%)
  starting transfers between devices  32.1 us (23%)
  waiting for transfers between devices  9.6 us (7%)
  local copies, waits for them, and re-layouts  9.05 us (6%)
    all_to_all x1, blocking collectives, swap(): return lax.all_to_all(value, axis, 0, 0, tiled=True)  33.5 us
    all_to_all x4, starting transfers between devices, swap(): return lax.all_to_all(value, axis, 0, 0, tiled=True)  32.1 us
    pallas_call x1, Pallas kernels, spread(): pl.pallas_call(spread_body, grid=(SITES // CHUNK,), in_specs=[pl.BlockSpe...  15.3 us
    pallas_call x1, Pallas kernels, late_waves(): pl.pallas_call(late_body, in_specs=[pl.BlockSpec(memory_space=pltpu.SMEM)...  14.1 us
    all_to_all x4, waiting for transfers between devices, swap(): return lax.all_to_all(value, axis, 0, 0, tiled=True)  9.6 us
    unnamed x38, local copies, waits for them, and re-layouts  7.1 us
    pallas_call x1, Pallas kernels, couple(): pl.pallas_call(couple_body, in_specs=[pl.BlockSpec(memory_space=pltpu.SME...  5.81 us
    pallas_call x1, Pallas kernels, tables(): pl.pallas_call(table_body, grid=(4,), in_specs=[pl.BlockSpec(memory_space...  5.13 us
  transfers between devices with their start and end apart: 4, of which 2 were waited for; matrix products, arithmetic and copies ran while one was open for 1% of the time, Pallas kernels for 32%

profile of v5, /device:TPU:1, one launch (start us, length us, event | category | flops | bytes accessed | tf_op | source)
XLA Modules:
  0.0 140.0 jit_solution(2868905737865715005)
XLA Ops:
  1.3 1.8 %pack.1 = (f32[16,8,128]{2,1,0:T(8,128)}, f32[8,1024]{1,0:T(8,128)}, f32[8,512]{1,0:T(8,128)}) custom-call(s32[2]{0:T(128)} %pad_add_fusion.place, f32[1,32]{1,0:T(1,128)} %bitcast.23, s32[1,32]{1,0:T(1,128)} %bitcast.24, s32[3,32]{1,0:T(4,128)} %cell.2, f32[3,32]{1,0:T(4,128)} %frac.2, f32[1,32]{1,0:T(1,128)} %bitcast.25, f32[3,16384]{1,0:T(4,128)} %pos.1, ...), custom_call_target="tpu_custom_call" | custom-call | tf_op jit(solution)/shard_map/pack/pallas_call | solution.py:224
  3.1 10.2 %all-to-all-start = ((f32[16,8,128]{2,1,0:T(8,128)}), f32[16,8,128]{2,1,0:T(8,128)S(1)}, u32[]{:S(2)}, u32[]{:S(2)}) async-start(f32[16,8,128]{2,1,0:T(8,128)} %get-tuple-element.11), calls=%async_computation | async-start | bytes 131072 | tf_op jit(solution)/shard_map/all_to_all | solution.py:623
  13.2 0.8 copy-done.4
  14.0 0.7 copy-done.5
  15.4 5.8 %couple.1.matrix = f32[512,1024]{1,0:T(8,128)S(1)} custom-call(s32[2]{0:T(128)S(1)} %copy-done.6, f32[8,1024]{1,0:T(8,128)S(1)} %copy-done.4, f32[8,512]{1,0:T(8,128)S(1)} %copy-done.5), custom_call_target="tpu_custom_call" | custom-call | flops 100000000 | bytes 2000000 | tf_op jit(solution)/shard_map/couple/pallas_call | solution.py:295
  21.2 1.3 first_product.1
  22.5 11.4 %all-to-all-start.1 = ((f32[32,40,128]{2,1,0:T(8,128)}), f32[32,40,128]{2,1,0:T(8,128)S(1)}, u32[]{:S(2)}, u32[]{:S(2)}) async-start(f32[32,40,128]{2,1,0:T(8,128)} %first_product.1), calls=%async_computation.1 | async-start | bytes 1310720 | tf_op jit(solution)/shard_map/all_to_all | solution.py:623
  33.9 15.3 %spread.1 = f32[16,32,384]{2,1,0:T(8,128)} custom-call(f32[1,6144]{1,0:T(1,128)} %bitcast.26, f32[3,6144]{1,0:T(4,128)} %frac.3, s32[3,6144]{1,0:T(4,128)} %cell.3, bf16[2,392,384]{2,1,0:T(8,128)(2,1)} %constant.42.clone.waves_from), custom_call_target="tpu_custom_call" | custom-call | flops 8000000000 | bytes 2000000 | tf_op jit(solution)/shard_map/spread/pallas_call | solution.py:172
  49.1 1.7 %all-to-all-done.1.slots = f32[32,40,128]{2,1,0:T(8,128)S(1)} async-done(((f32[32,40,128]{2,1,0:T(8,128)}), f32[32,40,128]{2,1,0:T(8,128)S(1)}, u32[]{:S(2)}, u32[]{:S(2)}) %all-to-all-start.1) | async-done | bytes 655392 | tf_op jit(solution)/shard_map/all_to_all | solution.py:623
  51.3 33.5 %all_to_all.25.grid = f32[16,32,384]{2,1,0:T(8,128)S(1)} all-to-all(f32[16,32,384]{2,1,0:T(8,128)S(1)} %pad_maximum_fusion), channel_id=1, replica_groups=mesh['fft'=32,'slab'=16] {'slab'}, dimensions={0} | all-to-all | bytes 1572864 | tf_op jit(solution)/shard_map/all_to_all | solution.py:623
  84.8 2.4 %along_y.1 = f32[32,16,384]{2,1,0:T(8,128)S(1)} custom-call(f32[16,32,384]{2,1,0:T(8,128)S(1)} %all_to_all.25.grid, f32[512,1024]{1,0:T(8,128)S(1)} %couple.1.matrix, bf16[384,384]{1,0:T(8,128)(2,1)S(1)} %copy-done.13, bf16[512,768]{1,0:T(8,128)(2,1)S(1)} %copy-done.9, bf16[512,768]{1,0:T(8,128)(2,1)S(1)} %copy-done.10, bf16[512,768]{1,0:T(8,128)(2,1)S(1)} %copy-done.11, ...), custom_call_target="tpu_custom_call" | custom-call | flops 4000000000 | bytes 5000000 | tf_op jit(solution)/shard_map/along_y/pallas_call | solution.py:355
  87.2 0.9 copy-done.2
  88.1 5.7 %all-to-all-start.3 = ((f32[32,16,384]{2,1,0:T(8,128)}), f32[32,16,384]{2,1,0:T(8,128)S(1)}, u32[]{:S(2)}, u32[]{:S(2)}) async-start(f32[32,16,384]{2,1,0:T(8,128)} %copy-done.2), calls=%async_computation.3 | async-start | bytes 1572864 | tf_op jit(solution)/shard_map/all_to_all | solution.py:623
  93.8 0.7 dynamic-slice_bitcast_fusion
  94.6 0.7 dynamic-slice_bitcast_fusion.1
  95.4 5.1 %tables.1.waves_from = f32[32,64,512]{2,1,0:T(8,128)S(1)} custom-call(s32[2]{0:T(128)S(1)} %copy-done.7, f32[32,40,128]{2,1,0:T(8,128)S(1)} %all-to-all-done.1.slots, f32[16,16]{1,0:T(8,128)S(1)} %pad_maximum_fusion.2.steps), custom_call_target="tpu_custom_call" | custom-call | flops 2000000000 | bytes 5000000 | tf_op jit(solution)/shard_map/tables/pallas_call | solution.py:433
  100.6 1.9 %copy-done.14 = f32[32,64,512]{2,1,0:T(8,128)} copy-done((f32[32,64,512]{2,1,0:T(8,128)}, f32[32,64,512]{2,1,0:T(8,128)S(1)}, u32[]{:S(2)}) %copy-start.14) | copy-done | bytes 4194328
  103.0 4.5 %early.1.before = f32[2,128,128]{2,1,0:T(8,128)S(1)} custom-call(f32[32,40,128]{2,1,0:T(8,128)S(1)} %all-to-all-done.1.slots, f32[128,128]{1,0:T(8,128)S(1)} %reshape.43.first), custom_call_target="tpu_custom_call" | custom-call | flops 2000000000 | bytes 1000000 | tf_op jit(solution)/shard_map/early/pallas_call | solution.py:479
  107.5 7.9 %all-to-all-done.3.grid.got = f32[32,16,384]{2,1,0:T(8,128)S(1)} async-done(((f32[32,16,384]{2,1,0:T(8,128)}), f32[32,16,384]{2,1,0:T(8,128)S(1)}, u32[]{:S(2)}, u32[]{:S(2)}) %all-to-all-start.3) | async-done | bytes 786464 | tf_op jit(solution)/shard_map/all_to_all | solution.py:623
  115.5 1.5 %quad_sum.1 = f32[16,8,128]{2,1,0:T(8,128)} custom-call(s32[2]{0:T(128)S(1)} %copy-done.7, f32[32,16,384]{2,1,0:T(8,128)S(1)} %all-to-all-done.3.grid.got), custom_call_target="tpu_custom_call" | custom-call | tf_op jit(solution)/shard_map/quad_sum/pallas_call | solution.py:375
  116.9 4.9 %all-to-all-start.4 = ((f32[16,8,128]{2,1,0:T(8,128)}), f32[16,8,128]{2,1,0:T(8,128)S(1)}, u32[]{:S(2)}, u32[]{:S(2)}) async-start(f32[16,8,128]{2,1,0:T(8,128)} %quad_sum.1), calls=%async_computation.4 | async-start | bytes 131072 | tf_op jit(solution)/shard_map/all_to_all | solution.py:623
  121.8 14.1 %late_waves.1 = (f32[32,32,288]{2,1,0:T(8,128)}, f32[8,128]{1,0:T(8,128)}) custom-call(s32[2]{0:T(128)} %pad_add_fusion.place, f32[32,40,128]{2,1,0:T(8,128)} %copy-done.1, f32[2,128,128]{2,1,0:T(8,128)} %copy-done.16, f32[128,128]{1,0:T(8,128)} %copy-done.3, f32[32,16,384]{2,1,0:T(8,128)} %copy-done, bf16[384,288]{1,0:T(8,128)(2,1)} %constant.50.clone.perm, ...), custom_call_target="tpu_custom_call" | custom-call | flops 5000000000 | bytes 7000000 | tf_op jit(solution)/shard_map/late_waves/pallas_call | solution.py:574
  135.9 1.4 copy-done.15
  138.0 2.0 %along_z.1 = (f32[12,12,384]{2,1,0:T(8,128)}, f32[12,12,384]{2,1,0:T(8,128)}, f32[1,32]{1,0:T(1,128)}) custom-call(f32[32,32,288]{2,1,0:T(8,128)S(1)} %copy-done.15, f32[16,8,128]{2,1,0:T(8,128)S(1)} %all-to-all-done.4.quads, f32[8,128]{1,0:T(8,128)S(1)} %copy-done.17, bf16[4,512,384]{2,1,0:T(8,128)(2,1)S(1)} %copy-done.8), custom_call_target="tpu_custom_call" | custom-call | flops 3000000000 | bytes 5000000 | tf_op jit(solution)/shard_map/along_z/pallas_call | solution.py:613
  (50 shorter events, 3.1 us)
Async XLA Ops:
  3.1 18.1 %all-to-all-start = ((f32[16,8,128]{2,1,0:T(8,128)}), f32[16,8,128]{2,1,0:T(8,128)S(1)}, u32[]{:S(2)}, u32[]{:S(2)}) async-start(f32[16,8,128]{2,1,0:T(8,128)} %get-tuple-element.11), calls=%async_computation | async-start | bytes 131072 | tf_op jit(solution)/shard_map/all_to_all | solution.py:623
  13.2 0.8 copy-start.4
  14.0 0.7 copy-start.5
  14.7 0.7 copy-start.6
  22.5 28.3 %all-to-all-start.1 = ((f32[32,40,128]{2,1,0:T(8,128)}), f32[32,40,128]{2,1,0:T(8,128)S(1)}, u32[]{:S(2)}, u32[]{:S(2)}) async-start(f32[32,40,128]{2,1,0:T(8,128)} %first_product.1), calls=%async_computation.1 | async-start | bytes 1310720 | tf_op jit(solution)/shard_map/all_to_all | solution.py:623
  49.1 2.0 %copy-start.18 = (f32[16,32,384]{2,1,0:T(8,128)S(1)}, f32[16,32,384]{2,1,0:T(8,128)}, u32[]{:S(2)}) copy-start(f32[16,32,384]{2,1,0:T(8,128)} %spread.1) | copy-start | bytes 2359300
  50.8 52.1 %copy-start.1 = (f32[32,40,128]{2,1,0:T(8,128)}, f32[32,40,128]{2,1,0:T(8,128)S(1)}, u32[]{:S(2)}) copy-start(f32[32,40,128]{2,1,0:T(8,128)S(1)} %all-to-all-done.1.slots) | copy-start | bytes 1966084
  50.9 33.9 %copy-start.13 = (bf16[384,384]{1,0:T(8,128)(2,1)S(1)}, bf16[384,384]{1,0:T(8,128)(2,1)}, u32[]{:S(2)}) copy-start(bf16[384,384]{1,0:T(8,128)(2,1)} %constant.47.clone.perm) | copy-start | bytes 884740
  51.1 33.7 %copy-start.9 = (bf16[512,768]{1,0:T(8,128)(2,1)S(1)}, bf16[512,768]{1,0:T(8,128)(2,1)}, u32[]{:S(2)}) copy-start(bf16[512,768]{1,0:T(8,128)(2,1)} %constant.43.clone.arh) | copy-start | bytes 2359300
  51.1 33.7 %copy-start.10 = (bf16[512,768]{1,0:T(8,128)(2,1)S(1)}, bf16[512,768]{1,0:T(8,128)(2,1)}, u32[]{:S(2)}) copy-start(bf16[512,768]{1,0:T(8,128)(2,1)} %constant.44.clone.arl) | copy-start | bytes 2359300
  51.1 33.7 %copy-start.11 = (bf16[512,768]{1,0:T(8,128)(2,1)S(1)}, bf16[512,768]{1,0:T(8,128)(2,1)}, u32[]{:S(2)}) copy-start(bf16[512,768]{1,0:T(8,128)(2,1)} %constant.45.clone.aih) | copy-start | bytes 2359300
  51.1 33.6 %copy-start.12 = (bf16[512,768]{1,0:T(8,128)(2,1)S(1)}, bf16[512,768]{1,0:T(8,128)(2,1)}, u32[]{:S(2)}) copy-start(bf16[512,768]{1,0:T(8,128)(2,1)} %constant.46.clone.ail) | copy-start | bytes 2359300
  84.8 10.6 %copy-start.7 = (s32[2]{0:T(128)S(1)}, s32[2]{0:T(128)}, u32[]{:S(2)}) copy-start(s32[2]{0:T(128)} %pad_add_fusion.place) | copy-start | bytes 28
  87.2 0.9 copy-start.2
  88.1 27.3 %all-to-all-start.3 = ((f32[32,16,384]{2,1,0:T(8,128)}), f32[32,16,384]{2,1,0:T(8,128)S(1)}, u32[]{:S(2)}, u32[]{:S(2)}) async-start(f32[32,16,384]{2,1,0:T(8,128)} %copy-done.2), calls=%async_computation.3 | async-start | bytes 1572864 | tf_op jit(solution)/shard_map/all_to_all | solution.py:623
  100.6 1.9 %copy-start.14 = (f32[32,64,512]{2,1,0:T(8,128)}, f32[32,64,512]{2,1,0:T(8,128)S(1)}, u32[]{:S(2)}) copy-start(f32[32,64,512]{2,1,0:T(8,128)S(1)} %tables.1.waves_from) | copy-start | bytes 12582916
  103.0 4.5 %copy-start.3 = (f32[128,128]{1,0:T(8,128)}, f32[128,128]{1,0:T(8,128)S(1)}, u32[]{:S(2)}) copy-start(f32[128,128]{1,0:T(8,128)S(1)} %reshape.43.first) | copy-start | bytes 196612
  107.5 9.4 %copy-start.16 = (f32[2,128,128]{2,1,0:T(8,128)}, f32[2,128,128]{2,1,0:T(8,128)S(1)}, u32[]{:S(2)}) copy-start(f32[2,128,128]{2,1,0:T(8,128)S(1)} %early.1.before) | copy-start | bytes 393220
  115.5 6.3 %copy-start = (f32[32,16,384]{2,1,0:T(8,128)}, f32[32,16,384]{2,1,0:T(8,128)S(1)}, u32[]{:S(2)}) copy-start(f32[32,16,384]{2,1,0:T(8,128)S(1)} %all-to-all-done.3.grid.got) | copy-start | bytes 2359300
  116.9 19.0 %all-to-all-start.4 = ((f32[16,8,128]{2,1,0:T(8,128)}), f32[16,8,128]{2,1,0:T(8,128)S(1)}, u32[]{:S(2)}, u32[]{:S(2)}) async-start(f32[16,8,128]{2,1,0:T(8,128)} %quad_sum.1), calls=%async_computation.4 | async-start | bytes 131072 | tf_op jit(solution)/shard_map/all_to_all | solution.py:623
  121.8 14.1 %copy-start.8 = (bf16[4,512,384]{2,1,0:T(8,128)(2,1)S(1)}, bf16[4,512,384]{2,1,0:T(8,128)(2,1)}, u32[]{:S(2)}) copy-start(bf16[4,512,384]{2,1,0:T(8,128)(2,1)} %constant.51.clone.waves) | copy-start | bytes 4718596
  135.9 1.4 %copy-start.15 = (f32[32,32,288]{2,1,0:T(8,128)S(1)}, f32[32,32,288]{2,1,0:T(8,128)}, u32[]{:S(2)}) copy-start(f32[32,32,288]{2,1,0:T(8,128)} %get-tuple-element.14.ml) | copy-start | bytes 3538948
  137.3 0.7 copy-start.17

commit v6 on v5

--- a/solution.py
+++ b/solution.py
@@ -34,6 +34,7 @@
 BF16 = jnp.bfloat16
 MOST = 60 * 1024 * 1024
 SOME = 12 * 1024 * 1024
+LATE = 61000000
 
 
 def wave(points, freqs):
@@ -100,6 +101,10 @@
     freqs = (np.arange(count) * 12)[:, None] + local[None, :]
     angle = 2.0 * np.pi * freqs[:, :, None] * np.arange(4)[None, None, :] / NG
     return np.concatenate([np.cos(angle), -np.sin(angle)], 2).astype(np.float32)
+
+
+def my_place():
+    return lax.axis_index("fft"), lax.axis_index("slab")
 
 
 def split(value):
@@ -195,8 +200,8 @@
     return jnp.concatenate([tiles[i : i + 1] for i in range(tiles.shape[0])], 1)
 
 
-def pack_body(place, drive, atom, cell, frac, hard, pos, width, out, cols, rows, picked):
-    f, s = place[0], place[1]
+def pack_body(drive, atom, cell, frac, hard, pos, width, out, near, picked):
+    f, s = my_place()
     out[...] = jnp.zeros_like(out)
     for i in range(N_SLAB):
         out[i, 0:1, 0:OWN] = -drive[...]
@@ -212,28 +217,25 @@
         value = jnp.zeros((8, 128), F32)
         for j in range(4):
             value = jnp.where(lane == j, pltpu.roll(picked[tile * 4 + j], ((j - (s & 3)) & 3) * OWN, 1), value)
-        cols[:, tile * 128 : tile * 128 + 128] = value
+        near[:, tile * 128 : tile * 128 + 128] = value
     at = pl.multiple_of(f * ROWS, 128)
-    rows[...] = jnp.zeros_like(rows)
-    rows[0:3, :] = pos[:, pl.ds(at, ROWS)]
-    rows[3:4, :] = width[:, pl.ds(at, ROWS)]
-    rows[4:5, 0:OWN] = hard[...]
-
-
-def pack(place, drive, atom, cell, frac, hard, pos, width):
+    near[:, COLS:] = jnp.zeros((8, ROWS), F32)
+    near[0:3, COLS:] = pos[:, pl.ds(at, ROWS)]
+    near[3:4, COLS:] = width[:, pl.ds(at, ROWS)]
+    near[4:5, COLS : COLS + OWN] = hard[...]
+
+
+def pack(drive, atom, cell, frac, hard, pos, width):
     return pl.pallas_call(
         pack_body,
-        in_specs=[pl.BlockSpec(memory_space=pltpu.SMEM)] + [pl.BlockSpec(memory_space=pltpu.VMEM)] * 7,
         out_shape=(
             jax.ShapeDtypeStruct((N_SLAB, 8, 128), F32),
-            jax.ShapeDtypeStruct((8, COLS), F32),
-            jax.ShapeDtypeStruct((8, ROWS), F32),
+            jax.ShapeDtypeStruct((8, COLS + ROWS), F32),
         ),
         scratch_shapes=[pltpu.VMEM((N_FFT, 8, 128), F32)],
         compiler_params=pltpu.CompilerParams(vmem_limit_bytes=MOST),
         name="pack",
     )(
-        place,
         drive.reshape(1, OWN),
         atom.reshape(1, OWN),
         cell,
@@ -262,12 +264,12 @@
     return value * p, q
 
 
-def couple_body(place, cols_ref, rows, out, own):
-    f, s = place[0], place[1]
-    cols = cols_ref[...]
-    side = jnp.transpose(rows[...])
+def couple_body(near, out, own):
+    f, s = my_place()
+    cols = near[:, :COLS]
+    side = jnp.transpose(near[:, COLS:])
     own[...] = jnp.zeros_like(own)
-    own[0:1, 0:OWN] = rows[4:5, 0:OWN]
+    own[0:1, 0:OWN] = near[4:5, COLS : COLS + OWN]
     own_hard = pltpu.roll(own[...], (f & 3) * OWN, 1)[0:1]
     diag = jnp.concatenate([jnp.where((f >> 2) == t, own_hard, 0.0) for t in range(COLS // 128)], 1)
     diag = diag + KE * (1.0 / (cols[3:4] * SQPI) - 2.0 * ALPHA / SQPI)
@@ -291,16 +293,15 @@
         out[first : first + step] = jnp.where(row_id == col_id, diag, value)
 
 
-def couple(place, cols, rows):
+def couple(near):
     return pl.pallas_call(
         couple_body,
-        in_specs=[pl.BlockSpec(memory_space=pltpu.SMEM)] + [pl.BlockSpec(memory_space=pltpu.VMEM)] * 2,
         out_shape=jax.ShapeDtypeStruct((ROWS, COLS), F32),
         scratch_shapes=[pltpu.VMEM((8, 128), F32)],
         compiler_params=pltpu.CompilerParams(vmem_limit_bytes=SOME),
         cost_estimate=pl.CostEstimate(flops=100_000_000, bytes_accessed=2_000_000, transcendentals=1_000_000),
         name="couple",
-    )(place, cols, rows)
+    )(near)
 
 
 def first_body(got, matrix, out, slots):
@@ -362,8 +363,8 @@
     )(*operands)
 
 
-def quad_body(place, got, out):
-    s = place[1]
+def quad_body(got, out):
+    s = my_place()[1]
     third = jnp.sum(got[:, :, 32:96], 0)
     second = got[:, pl.ds(s, 1), 96:128].reshape(N_FFT, OWN)
     total = jnp.sum(third[:, 0:OWN] * second[0:16] + third[:, OWN:] * second[16:], 0, keepdims=True)
@@ -371,19 +372,18 @@
     out[...] = jnp.broadcast_to(total[None], out.shape)
 
 
-def quad_sum(place, got):
+def quad_sum(got):
     return pl.pallas_call(
         quad_body,
         grid=(1,),
         in_specs=[
-            pl.BlockSpec(memory_space=pltpu.SMEM),
             pl.BlockSpec((N_FFT, 16, 128), lambda i: (0, 0, 2)),
         ],
         out_specs=pl.BlockSpec((N_SLAB, 8, 128), lambda i: (0, 0, 0)),
         out_shape=jax.ShapeDtypeStruct((N_SLAB, 8, 128), F32),
         compiler_params=pltpu.CompilerParams(vmem_limit_bytes=SOME),
         name="quad_sum",
-    )(place, got)
+    )(got)
 
 
 def unit(turns):
@@ -416,9 +416,10 @@
     return jnp.concatenate([slots[g, 8 + i * 8 : 16 + i * 8, :] for i in range(4)], 1)
 
 
-def table_body(place, slots, steps, out):
+def table_body(slots, steps, out):
+    f, s = my_place()
     block = (lax.broadcasted_iota(jnp.int32, (1, ROWS), 1) // OWN * YL).astype(F32)
-    first_x, first_y = (place[1] * KX).astype(F32), (place[0] * KY).astype(F32)
+    first_x, first_y = (s * KX).astype(F32), (f * KY).astype(F32)
     for g in range(8):
         rows = slot_rows(slots, g)
         x_re, x_im = site_wave(first_x, rows[2:3], rows[5:6], steps[:, 0:8])
@@ -427,23 +428,23 @@
         out[g, 16:32] = x_im
         out[g, 32:48] = y_re
         out[g, 48:64] = y_im
-
-
-def tables(place, slots, steps):
+        out[g, 64:96] = jnp.zeros((32, ROWS), F32)
+
+
+def tables(slots, steps):
     return pl.pallas_call(
         table_body,
         grid=(4,),
         in_specs=[
-            pl.BlockSpec(memory_space=pltpu.SMEM),
             pl.BlockSpec((8, 40, 128), lambda i: (i, 0, 0)),
             pl.BlockSpec((16, 16), lambda i: (0, 0)),
         ],
-        out_specs=pl.BlockSpec((8, 64, ROWS), lambda i: (i, 0, 0)),
-        out_shape=jax.ShapeDtypeStruct((N_FFT, 64, ROWS), F32),
-        compiler_params=pltpu.CompilerParams(vmem_limit_bytes=SOME),
+        out_specs=pl.BlockSpec((8, 96, ROWS), lambda i: (i, 0, 0)),
+        out_shape=jax.ShapeDtypeStruct((N_FFT, 96, ROWS), F32),
+        compiler_params=pltpu.CompilerParams(vmem_limit_bytes=MOST),
         cost_estimate=pl.CostEstimate(flops=2_000_000_000, bytes_accessed=5_000_000, transcendentals=0),
         name="tables",
-    )(place, slots, steps)
+    )(slots, steps)
 
 
 def guarded(value, pivot, scale):
@@ -486,14 +487,16 @@
     )(slots, first)
 
 
-def late_body(place, slots, before, first, grid, perm, waves_from, out, rest, v2, late, charges, waves, sems):
+def late_body(slots, before, first, grid, perm, waves_from, out, rest, v2, late, charges, waves, sems):
     copies = [
-        pltpu.make_async_copy(waves_from.at[pl.ds(i * 8, 8)], waves.at[pl.ds(i * 8, 8)], sems.at[i])
+        pltpu.make_async_copy(
+            waves_from.at[pl.ds(i * 8, 8), pl.ds(0, 64)], waves.at[pl.ds(i * 8, 8)], sems.at[i]
+        )
         for i in range(4)
     ]
     for copy in copies:
         copy.start()
-    f, s = place[0], place[1]
+    f, s = my_place()
     for i in range(4):
         pieces = [grid[:, i * 4 + j, 352:384] for j in range(4)]
         v2[pl.ds(i, N_FFT, stride=4), :] = jnp.concatenate(pieces, 1)
@@ -534,12 +537,12 @@
     upper = lax.broadcasted_iota(jnp.int32, (8, 1), 0) < 4
 
     def group(i, carry):
-        at = pl.multiple_of(i * 16, 16)
-        charge = [charges[v, pl.ds(at, 16), :] for v in range(2)]
-        high, low = split(grid[pl.ds(i * 4, 4)].reshape(64, 384))
-        base = (dot_nn(high, perm[...]) + dot_nn(low, perm[...])).reshape(4, 16, PAIRS)
-        for j in range(4):
-            g = i * 4 + j
+        at = pl.multiple_of(i * 32, 32)
+        charge = [charges[v, pl.ds(at, 32), :] for v in range(2)]
+        high, low = split(grid[pl.ds(i * 8, 8)].reshape(128, 384))
+        base = (dot_nn(high, perm[...]) + dot_nn(low, perm[...])).reshape(8, 16, PAIRS)
+        for j in range(8):
+            g = i * 8 + j
             rows = slot_rows(slots, g)
             placed_z = placed(16, rows[4:5].astype(jnp.int32), spline(rows[7:8]))
             both = [placed_z * lanes(charge[v][j * 4 : j * 4 + 4]) for v in range(2)]
@@ -565,17 +568,15 @@
             out[g, 16:32] = total[16:]
         return carry
 
-    for i in range(4):
-        copies[i].wait()
-        lax.fori_loop(i * 2, i * 2 + 2, group, 0)
+    for copy in copies:
+        copy.wait()
+    lax.fori_loop(0, 4, group, 0)
 
 
 def late_waves(*operands):
     return pl.pallas_call(
         late_body,
-        in_specs=[pl.BlockSpec(memory_space=pltpu.SMEM)]
-        + [pl.BlockSpec(memory_space=pltpu.VMEM)] * 5
-        + [pl.BlockSpec(memory_space=pl.ANY)],
+        in_specs=[pl.BlockSpec(memory_space=pltpu.VMEM)] * 5 + [pl.BlockSpec(memory_space=pl.ANY)],
         out_shape=(
             jax.ShapeDtypeStruct((N_FFT, 32, PAIRS), F32),
             jax.ShapeDtypeStruct((8, 128), F32),
@@ -587,7 +588,7 @@
             pltpu.VMEM((N_FFT, 64, ROWS), F32),
             pltpu.SemaphoreType.DMA((4,)),
         ],
-        compiler_params=pltpu.CompilerParams(vmem_limit_bytes=MOST),
+        compiler_params=pltpu.CompilerParams(vmem_limit_bytes=LATE),
         cost_estimate=pl.CostEstimate(flops=5_000_000_000, bytes_accessed=7_000_000, transcendentals=0),
         name="late_waves",
     )(*operands)
@@ -637,11 +638,10 @@
 ):
     f = lax.axis_index("fft")
     s = lax.axis_index("slab")
-    place = jnp.stack([f, s]).astype(jnp.int32)
-
-    sent, cols, rows = pack(place, ml_drive, slot_atom, slot_cell, slot_frac, ml_hard, ml_pos, ml_width)
+
+    sent, near = pack(ml_drive, slot_atom, slot_cell, slot_frac, ml_hard, ml_pos, ml_width)
     got = swap(sent, "slab")
-    matrix = couple(place, cols, rows)
+    matrix = couple(near)
     got_1 = swap(first_product(got, matrix), "fft")
     mm = spread(mm_charge, mm_frac, mm_cell, jnp.asarray(np.stack(two_parts(x_table()))))
     first_cols = jnp.sum(got_1[:, :8], 0)
@@ -654,7 +654,7 @@
 
     arh, arl, aih, ail = (jnp.asarray(t) for half in y_tables() for t in two_parts(half))
     got_3 = swap(along_y(got_2, matrix, jnp.asarray(perm_y()), arh, arl, aih, ail), "fft")
-    quads = swap(quad_sum(place, got_3), "slab")
+    quads = swap(quad_sum(got_3), "slab")
 
     steps = jnp.concatenate(
         [
@@ -663,9 +663,9 @@
         ],
         1,
     )
-    waves = tables(place, got_1, steps)
+    waves = tables(got_1, steps)
     before = early(got_1, first_full)
-    ml, rest = late_waves(place, got_1, before, first_full, got_3, jnp.asarray(perm_z()), waves)
+    ml, rest = late_waves(got_1, before, first_full, got_3, jnp.asarray(perm_z()), waves)
     z_waves = jnp.asarray(np.stack([t for half in z_tables() for t in two_parts(half)]))
     struct_re, struct_im, charge = along_z(ml, quads, rest, z_waves)
     return (charge.reshape(OWN), struct_re, struct_im)

time: 141 us -> 138 us (0.979)
  local copies, waits for them, and re-layouts: 9.05 us -> 6.42 us
  blocking collectives: 33.5 us -> 32 us
    unnamed x38 -> x32, local copies, waits for them, and re-layouts: 7.1 us -> 4.46 us
    all_to_all x1, blocking collectives: 33.5 us -> 32 us  [swap(): return lax.all_to_all(value, axis, 0, 0, tiled=True)]
  transfers between devices with their start and end apart: 4 -> 4, of which waited for: 2 -> 3; matrix products, arithmetic and copies ran while one was open for 1% -> 2% of each run, Pallas kernels for 32% -> 34%
where the time goes in v6:
time: 138 us; the launch traced here: 137 us
  Pallas kernels  54.7 us (40%)
  starting transfers between devices  32 us (23%)
  blocking collectives  32 us (23%)
  waiting for transfers between devices  10.1 us (7%)
  local copies, waits for them, and re-layouts  6.42 us (5%)
    all_to_all x4, starting transfers between devices, swap(): return lax.all_to_all(value, axis, 0, 0, tiled=True)  32 us
    all_to_all x1, blocking collectives, swap(): return lax.all_to_all(value, axis, 0, 0, tiled=True)  32 us
    pallas_call x1, Pallas kernels, spread(): pl.pallas_call(spread_body, grid=(SITES // CHUNK,), in_specs=[pl.BlockSpe...  15.3 us
    pallas_call x1, Pallas kernels, late_waves(): pl.pallas_call(late_body, in_specs=[pl.BlockSpec(memory_space=pltpu.VMEM)...  14.3 us
    all_to_all x4, waiting for transfers between devices, swap(): return lax.all_to_all(value, axis, 0, 0, tiled=True)  10.1 us
    pallas_call x1, Pallas kernels, tables(): pl.pallas_call(table_body, grid=(4,), in_specs=[pl.BlockSpec((8, 40, 128)...  6.84 us
    pallas_call x1, Pallas kernels, couple(): pl.pallas_call(couple_body, out_shape=jax.ShapeDtypeStruct((ROWS, COLS),...  5.27 us
    pallas_call x1, Pallas kernels, early(): pl.pallas_call(early_body, out_shape=jax.ShapeDtypeStruct((2, 128, 128),...  4.53 us
  transfers between devices with their start and end apart: 4, of which 3 were waited for; matrix products, arithmetic and copies ran while one was open for 2% of the time, Pallas kernels for 34%

profile of v6, /device:TPU:1, one launch (start us, length us, event | category | flops | bytes accessed | tf_op | source)
XLA Modules:
  0.0 137.2 jit_solution(8419765983923543677)
XLA Ops:
  0.6 1.8 %pack.1 = (f32[16,8,128]{2,1,0:T(8,128)}, f32[8,1536]{1,0:T(8,128)}) custom-call(f32[1,32]{1,0:T(1,128)} %bitcast.21, s32[1,32]{1,0:T(1,128)} %bitcast.22, s32[3,32]{1,0:T(4,128)} %cell.2, f32[3,32]{1,0:T(4,128)} %frac.2, f32[1,32]{1,0:T(1,128)} %bitcast.23, f32[3,16384]{1,0:T(4,128)} %pos.1, f32[1,16384]{1,0:T(1,128)} %bitcast.18), custom_call_target="tpu_custom_call" | custom-call | tf_op jit(solution)/shard_map/pack/pallas_call | solution.py:229
  2.4 10.2 %all-to-all-start = ((f32[16,8,128]{2,1,0:T(8,128)}), f32[16,8,128]{2,1,0:T(8,128)S(1)}, u32[]{:S(2)}, u32[]{:S(2)}) async-start(f32[16,8,128]{2,1,0:T(8,128)} %get-tuple-element.10), calls=%async_computation | async-start | bytes 131072 | tf_op jit(solution)/shard_map/all_to_all | solution.py:624
  12.6 0.8 copy-done.5
  13.4 5.3 %couple.1.matrix = f32[512,1024]{1,0:T(8,128)S(1)} custom-call(f32[8,1536]{1,0:T(8,128)S(1)} %copy-done.5), custom_call_target="tpu_custom_call" | custom-call | flops 100000000 | bytes 2000000 | tf_op jit(solution)/shard_map/couple/pallas_call | solution.py:297
  18.7 1.8 %all-to-all-done.got = f32[16,8,128]{2,1,0:T(8,128)S(1)} async-done(((f32[16,8,128]{2,1,0:T(8,128)}), f32[16,8,128]{2,1,0:T(8,128)S(1)}, u32[]{:S(2)}, u32[]{:S(2)}) %all-to-all-start) | async-done | bytes 65568 | tf_op jit(solution)/shard_map/all_to_all | solution.py:624
  20.4 1.3 first_product.1
  21.7 11.3 %all-to-all-start.1 = ((f32[32,40,128]{2,1,0:T(8,128)}), f32[32,40,128]{2,1,0:T(8,128)S(1)}, u32[]{:S(2)}, u32[]{:S(2)}) async-start(f32[32,40,128]{2,1,0:T(8,128)} %first_product.1), calls=%async_computation.1 | async-start | bytes 1310720 | tf_op jit(solution)/shard_map/all_to_all | solution.py:624
  33.0 15.3 %spread.1 = f32[16,32,384]{2,1,0:T(8,128)} custom-call(f32[1,6144]{1,0:T(1,128)} %bitcast.24, f32[3,6144]{1,0:T(4,128)} %frac.3, s32[3,6144]{1,0:T(4,128)} %cell.3, bf16[2,392,384]{2,1,0:T(8,128)(2,1)} %constant.42.clone.waves_from), custom_call_target="tpu_custom_call" | custom-call | flops 8000000000 | bytes 2000000 | tf_op jit(solution)/shard_map/spread/pallas_call | solution.py:177
  48.3 1.5 %all-to-all-done.1.slots = f32[32,40,128]{2,1,0:T(8,128)S(1)} async-done(((f32[32,40,128]{2,1,0:T(8,128)}), f32[32,40,128]{2,1,0:T(8,128)S(1)}, u32[]{:S(2)}, u32[]{:S(2)}) %all-to-all-start.1) | async-done | bytes 655392 | tf_op jit(solution)/shard_map/all_to_all | solution.py:624
  50.2 32.0 %all_to_all.25.grid = f32[16,32,384]{2,1,0:T(8,128)S(1)} all-to-all(f32[16,32,384]{2,1,0:T(8,128)S(1)} %pad_maximum_fusion), channel_id=1, replica_groups=mesh['fft'=32,'slab'=16] {'slab'}, dimensions={0} | all-to-all | bytes 1572864 | tf_op jit(solution)/shard_map/all_to_all | solution.py:624
  82.3 2.4 %along_y.1 = f32[32,16,384]{2,1,0:T(8,128)S(1)} custom-call(f32[16,32,384]{2,1,0:T(8,128)S(1)} %all_to_all.25.grid, f32[512,1024]{1,0:T(8,128)S(1)} %couple.1.matrix, bf16[384,384]{1,0:T(8,128)(2,1)S(1)} %copy-done.11, bf16[512,768]{1,0:T(8,128)(2,1)S(1)} %copy-done.7, bf16[512,768]{1,0:T(8,128)(2,1)S(1)} %copy-done.8, bf16[512,768]{1,0:T(8,128)(2,1)S(1)} %copy-done.9, ...), custom_call_target="tpu_custom_call" | custom-call | flops 4000000000 | bytes 5000000 | tf_op jit(solution)/shard_map/along_y/pallas_call | solution.py:356
  84.7 0.9 copy-done.3
  85.6 5.7 %all-to-all-start.3 = ((f32[32,16,384]{2,1,0:T(8,128)}), f32[32,16,384]{2,1,0:T(8,128)S(1)}, u32[]{:S(2)}, u32[]{:S(2)}) async-start(f32[32,16,384]{2,1,0:T(8,128)} %copy-done.3), calls=%async_computation.3 | async-start | bytes 1572864 | tf_op jit(solution)/shard_map/all_to_all | solution.py:624
  91.3 0.7 dynamic-slice_bitcast_fusion
  92.0 0.7 dynamic-slice_bitcast_fusion.1
  93.5 6.8 %tables.1.waves_from = f32[32,96,512]{2,1,0:T(8,128)} custom-call(f32[32,40,128]{2,1,0:T(8,128)} %copy-done.1, f32[16,16]{1,0:T(8,128)} %pad_maximum_fusion.2.steps), custom_call_target="tpu_custom_call" | custom-call | flops 2000000000 | bytes 5000000 | tf_op jit(solution)/shard_map/tables/pallas_call | solution.py:435
  100.8 4.5 %early.1.before = f32[2,128,128]{2,1,0:T(8,128)S(1)} custom-call(f32[32,40,128]{2,1,0:T(8,128)S(1)} %copy-done.2, f32[128,128]{1,0:T(8,128)S(1)} %reshape.43.first), custom_call_target="tpu_custom_call" | custom-call | flops 2000000000 | bytes 1000000 | tf_op jit(solution)/shard_map/early/pallas_call | solution.py:480
  106.0 6.9 %all-to-all-done.3.grid.got = f32[32,16,384]{2,1,0:T(8,128)S(1)} async-done(((f32[32,16,384]{2,1,0:T(8,128)}), f32[32,16,384]{2,1,0:T(8,128)S(1)}, u32[]{:S(2)}, u32[]{:S(2)}) %all-to-all-start.3) | async-done | bytes 786464 | tf_op jit(solution)/shard_map/all_to_all | solution.py:624
  112.9 1.0 quad_sum.1
  113.9 4.9 %all-to-all-start.4 = ((f32[16,8,128]{2,1,0:T(8,128)}), f32[16,8,128]{2,1,0:T(8,128)S(1)}, u32[]{:S(2)}, u32[]{:S(2)}) async-start(f32[16,8,128]{2,1,0:T(8,128)} %quad_sum.1), calls=%async_computation.4 | async-start | bytes 131072 | tf_op jit(solution)/shard_map/all_to_all | solution.py:624
  118.8 14.3 %late_waves.1 = (f32[32,32,288]{2,1,0:T(8,128)}, f32[8,128]{1,0:T(8,128)}) custom-call(f32[32,40,128]{2,1,0:T(8,128)} %copy-done.1, f32[2,128,128]{2,1,0:T(8,128)} %copy-done.13, f32[128,128]{1,0:T(8,128)} %copy-done.4, f32[32,16,384]{2,1,0:T(8,128)} %copy-done, bf16[384,288]{1,0:T(8,128)(2,1)} %constant.50.clone.perm, f32[32,96,512]{2,1,0:T(8,128)} %tables.1.waves_from), custom_call_target="tpu_custom_call" | custom-call | flops 5000000000 | bytes 7000000 | tf_op jit(solution)/shard_map/late_waves/pallas_call | solution.py:577
  133.1 1.4 %copy-done.12 = f32[32,32,288]{2,1,0:T(8,128)S(1)} copy-done((f32[32,32,288]{2,1,0:T(8,128)S(1)}, f32[32,32,288]{2,1,0:T(8,128)}, u32[]{:S(2)}) %copy-start.12) | copy-done | bytes 1179672
  134.5 0.7 copy-done.14
  135.2 2.0 %along_z.1 = (f32[12,12,384]{2,1,0:T(8,128)}, f32[12,12,384]{2,1,0:T(8,128)}, f32[1,32]{1,0:T(1,128)}) custom-call(f32[32,32,288]{2,1,0:T(8,128)S(1)} %copy-done.12, f32[16,8,128]{2,1,0:T(8,128)S(1)} %all-to-all-done.4.quads, f32[8,128]{1,0:T(8,128)S(1)} %copy-done.14, bf16[4,512,384]{2,1,0:T(8,128)(2,1)S(1)} %copy-done.6), custom_call_target="tpu_custom_call" | custom-call | flops 3000000000 | bytes 5000000 | tf_op jit(solution)/shard_map/along_z/pallas_call | solution.py:614
  (43 shorter events, 2.3 us)
Async XLA Ops:
  2.4 18.0 %all-to-all-start = ((f32[16,8,128]{2,1,0:T(8,128)}), f32[16,8,128]{2,1,0:T(8,128)S(1)}, u32[]{:S(2)}, u32[]{:S(2)}) async-start(f32[16,8,128]{2,1,0:T(8,128)} %get-tuple-element.10), calls=%async_computation | async-start | bytes 131072 | tf_op jit(solution)/shard_map/all_to_all | solution.py:624
  12.6 0.8 copy-start.5
  21.7 28.1 %all-to-all-start.1 = ((f32[32,40,128]{2,1,0:T(8,128)}), f32[32,40,128]{2,1,0:T(8,128)S(1)}, u32[]{:S(2)}, u32[]{:S(2)}) async-start(f32[32,40,128]{2,1,0:T(8,128)} %first_product.1), calls=%async_computation.1 | async-start | bytes 1310720 | tf_op jit(solution)/shard_map/all_to_all | solution.py:624
  48.3 1.8 %copy-start.15 = (f32[16,32,384]{2,1,0:T(8,128)S(1)}, f32[16,32,384]{2,1,0:T(8,128)}, u32[]{:S(2)}) copy-start(f32[16,32,384]{2,1,0:T(8,128)} %spread.1) | copy-start | bytes 2359300
  49.8 32.4 %copy-start.1 = (f32[32,40,128]{2,1,0:T(8,128)}, f32[32,40,128]{2,1,0:T(8,128)S(1)}, u32[]{:S(2)}) copy-start(f32[32,40,128]{2,1,0:T(8,128)S(1)} %all-to-all-done.1.slots) | copy-start | bytes 1966084
  49.8 32.4 %copy-start.11 = (bf16[384,384]{1,0:T(8,128)(2,1)S(1)}, bf16[384,384]{1,0:T(8,128)(2,1)}, u32[]{:S(2)}) copy-start(bf16[384,384]{1,0:T(8,128)(2,1)} %constant.47.clone.perm) | copy-start | bytes 884740
  50.0 32.2 %copy-start.7 = (bf16[512,768]{1,0:T(8,128)(2,1)S(1)}, bf16[512,768]{1,0:T(8,128)(2,1)}, u32[]{:S(2)}) copy-start(bf16[512,768]{1,0:T(8,128)(2,1)} %constant.43.clone.arh) | copy-start | bytes 2359300
  50.1 32.2 %copy-start.8 = (bf16[512,768]{1,0:T(8,128)(2,1)S(1)}, bf16[512,768]{1,0:T(8,128)(2,1)}, u32[]{:S(2)}) copy-start(bf16[512,768]{1,0:T(8,128)(2,1)} %constant.44.clone.arl) | copy-start | bytes 2359300
  50.1 32.2 %copy-start.9 = (bf16[512,768]{1,0:T(8,128)(2,1)S(1)}, bf16[512,768]{1,0:T(8,128)(2,1)}, u32[]{:S(2)}) copy-start(bf16[512,768]{1,0:T(8,128)(2,1)} %constant.45.clone.aih) | copy-start | bytes 2359300
  50.1 32.2 %copy-start.10 = (bf16[512,768]{1,0:T(8,128)(2,1)S(1)}, bf16[512,768]{1,0:T(8,128)(2,1)}, u32[]{:S(2)}) copy-start(bf16[512,768]{1,0:T(8,128)(2,1)} %constant.46.clone.ail) | copy-start | bytes 2359300
  84.7 0.9 copy-start.3
  85.6 27.3 %all-to-all-start.3 = ((f32[32,16,384]{2,1,0:T(8,128)}), f32[32,16,384]{2,1,0:T(8,128)S(1)}, u32[]{:S(2)}, u32[]{:S(2)}) async-start(f32[32,16,384]{2,1,0:T(8,128)} %copy-done.3), calls=%async_computation.3 | async-start | bytes 1572864 | tf_op jit(solution)/shard_map/all_to_all | solution.py:624
  93.5 7.3 %copy-start.2 = (f32[32,40,128]{2,1,0:T(8,128)S(1)}, f32[32,40,128]{2,1,0:T(8,128)}, u32[]{:S(2)}) copy-start(f32[32,40,128]{2,1,0:T(8,128)} %copy-done.1) | copy-start | bytes 1966084
  100.8 4.6 %copy-start.4 = (f32[128,128]{1,0:T(8,128)}, f32[128,128]{1,0:T(8,128)S(1)}, u32[]{:S(2)}) copy-start(f32[128,128]{1,0:T(8,128)S(1)} %reshape.43.first) | copy-start | bytes 196612
  105.3 0.7 copy-start.13
  112.9 5.8 %copy-start = (f32[32,16,384]{2,1,0:T(8,128)}, f32[32,16,384]{2,1,0:T(8,128)S(1)}, u32[]{:S(2)}) copy-start(f32[32,16,384]{2,1,0:T(8,128)S(1)} %all-to-all-done.3.grid.got) | copy-start | bytes 2359300
  113.9 19.2 %all-to-all-start.4 = ((f32[16,8,128]{2,1,0:T(8,128)}), f32[16,8,128]{2,1,0:T(8,128)S(1)}, u32[]{:S(2)}, u32[]{:S(2)}) async-start(f32[16,8,128]{2,1,0:T(8,128)} %quad_sum.1), calls=%async_computation.4 | async-start | bytes 131072 | tf_op jit(solution)/shard_map/all_to_all | solution.py:624
  118.8 14.4 %copy-start.6 = (bf16[4,512,384]{2,1,0:T(8,128)(2,1)S(1)}, bf16[4,512,384]{2,1,0:T(8,128)(2,1)}, u32[]{:S(2)}) copy-start(bf16[4,512,384]{2,1,0:T(8,128)(2,1)} %constant.51.clone.waves) | copy-start | bytes 4718596
  133.1 1.4 %copy-start.12 = (f32[32,32,288]{2,1,0:T(8,128)S(1)}, f32[32,32,288]{2,1,0:T(8,128)}, u32[]{:S(2)}) copy-start(f32[32,32,288]{2,1,0:T(8,128)} %get-tuple-element.12.ml) | copy-start | bytes 3538948
  134.5 0.7 copy-start.14

commit v7 on v6

--- a/solution.py
+++ b/solution.py
@@ -34,7 +34,6 @@
 BF16 = jnp.bfloat16
 MOST = 60 * 1024 * 1024
 SOME = 12 * 1024 * 1024
-LATE = 61000000
 
 
 def wave(points, freqs):
@@ -97,8 +96,7 @@
 
 
 def step_table(count):
-    local = np.concatenate([np.arange(12), np.arange(8, 12)])
-    freqs = (np.arange(count) * 12)[:, None] + local[None, :]
+    freqs = (np.arange(count) * 12)[:, None] + np.arange(12)[None, :]
     angle = 2.0 * np.pi * freqs[:, :, None] * np.arange(4)[None, None, :] / NG
     return np.concatenate([np.cos(angle), -np.sin(angle)], 2).astype(np.float32)
 
@@ -400,13 +398,17 @@
     return 2.0 * sine * sine - 1.0, 2.0 * sine * cosine
 
 
-def site_wave(first, base, fraction, steps):
-    local = lax.broadcasted_iota(jnp.int32, (16, 1), 0)
-    freq = first + jnp.where(local < 12, local, local - 4).astype(F32)
-    phase = freq * base
+def site_waves(freq, base, fraction, steps):
+    upper = lax.broadcasted_iota(jnp.int32, (8, 1), 0) < 4
+
+    def in_rows(x, y):
+        wide = [jnp.broadcast_to(v, (8, ROWS)) for v in (x, y)]
+        return jnp.concatenate(wide + [jnp.where(upper, x, y)], 0)
+
+    phase = freq * in_rows(*base)
     phase = phase - NG * jnp.floor(phase * (1.0 / NG))
     re, im = unit(phase * (1.0 / NG))
-    weights = spline(fraction)
+    weights = [in_rows(x, y) for x, y in zip(spline(fraction[0]), spline(fraction[1]), strict=True)]
     w_re = sum(steps[:, i : i + 1] * weights[i] for i in range(4))
     w_im = sum(steps[:, 4 + i : 5 + i] * weights[i] for i in range(1, 4))
     return re * w_re - im * w_im, re * w_im + im * w_re
@@ -414,37 +416,6 @@
 
 def slot_rows(slots, g):
     return jnp.concatenate([slots[g, 8 + i * 8 : 16 + i * 8, :] for i in range(4)], 1)
-
-
-def table_body(slots, steps, out):
-    f, s = my_place()
-    block = (lax.broadcasted_iota(jnp.int32, (1, ROWS), 1) // OWN * YL).astype(F32)
-    first_x, first_y = (s * KX).astype(F32), (f * KY).astype(F32)
-    for g in range(8):
-        rows = slot_rows(slots, g)
-        x_re, x_im = site_wave(first_x, rows[2:3], rows[5:6], steps[:, 0:8])
-        y_re, y_im = site_wave(first_y, rows[3:4] + block, rows[6:7], steps[:, 8:16])
-        out[g, 0:16] = x_re
-        out[g, 16:32] = x_im
-        out[g, 32:48] = y_re
-        out[g, 48:64] = y_im
-        out[g, 64:96] = jnp.zeros((32, ROWS), F32)
-
-
-def tables(slots, steps):
-    return pl.pallas_call(
-        table_body,
-        grid=(4,),
-        in_specs=[
-            pl.BlockSpec((8, 40, 128), lambda i: (i, 0, 0)),
-            pl.BlockSpec((16, 16), lambda i: (0, 0)),
-        ],
-        out_specs=pl.BlockSpec((8, 96, ROWS), lambda i: (i, 0, 0)),
-        out_shape=jax.ShapeDtypeStruct((N_FFT, 96, ROWS), F32),
-        compiler_params=pltpu.CompilerParams(vmem_limit_bytes=MOST),
-        cost_estimate=pl.CostEstimate(flops=2_000_000_000, bytes_accessed=5_000_000, transcendentals=0),
-        name="tables",
-    )(slots, steps)
 
 
 def guarded(value, pivot, scale):
@@ -487,15 +458,7 @@
     )(slots, first)
 
 
-def late_body(slots, before, first, grid, perm, waves_from, out, rest, v2, late, charges, waves, sems):
-    copies = [
-        pltpu.make_async_copy(
-            waves_from.at[pl.ds(i * 8, 8), pl.ds(0, 64)], waves.at[pl.ds(i * 8, 8)], sems.at[i]
-        )
-        for i in range(4)
-    ]
-    for copy in copies:
-        copy.start()
+def late_body(slots, before, first, grid, perm, steps, out, rest, v2, late, charges):
     f, s = my_place()
     for i in range(4):
         pieces = [grid[:, i * 4 + j, 352:384] for j in range(4)]
@@ -535,6 +498,10 @@
     rest[3:4] = jnp.broadcast_to(g2, (1, 128))
 
     upper = lax.broadcasted_iota(jnp.int32, (8, 1), 0) < 4
+    block = (lax.broadcasted_iota(jnp.int32, (1, ROWS), 1) // OWN * YL).astype(F32)
+    local = lax.broadcasted_iota(jnp.int32, (24, 1), 0)
+    freq = jnp.where(local < 8, s * KX + local, f * KY + local - 8)
+    freq = jnp.where(local < 16, freq, jnp.where(local < 20, s * KX + local - 8, f * KY + local - 12)).astype(F32)
 
     def group(i, carry):
         at = pl.multiple_of(i * 32, 32)
@@ -547,20 +514,23 @@
             placed_z = placed(16, rows[4:5].astype(jnp.int32), spline(rows[7:8]))
             both = [placed_z * lanes(charge[v][j * 4 : j * 4 + 4]) for v in range(2)]
             z_high, z_low = split(jnp.concatenate(both, 0))
-            x_re, x_im = waves[g, 0:8], waves[g, 16:24]
+            re, im = site_waves(freq, (rows[2:3], rows[3:4] + block), (rows[5:6], rows[6:7]), steps[...])
+            x_re, x_im = re[0:8], im[0:8]
+            y_re = [re[8 + k : 9 + k] for k in range(8)] + [re[20 + k : 21 + k] for k in range(4)]
+            y_im = [im[8 + k : 9 + k] for k in range(8)] + [im[20 + k : 21 + k] for k in range(4)]
             parts_re, parts_im = [], []
             for k in range(KY):
-                y_re, y_im = waves[g, 32 + k : 33 + k], waves[g, 48 + k : 49 + k]
-                parts_re.append(y_re * x_re - y_im * x_im)
-                parts_im.append(y_re * x_im + y_im * x_re)
+                a, b = y_re[k], y_im[k]
+                parts_re.append(a * x_re - b * x_im)
+                parts_im.append(a * x_im + b * x_re)
             parts = parts_re + parts_im
-            x_re, x_im = waves[g, 8:16], waves[g, 24:32]
+            x_re, x_im = (jnp.where(upper, v[16:24], pltpu.roll(v[16:24], 4, 0)) for v in (re, im))
             parts_re, parts_im = [], []
             for k in range(0, KY, 2):
-                y_re = jnp.where(upper, waves[g, 32 + k : 33 + k], waves[g, 33 + k : 34 + k])
-                y_im = jnp.where(upper, waves[g, 48 + k : 49 + k], waves[g, 49 + k : 50 + k])
-                parts_re.append(y_re * x_re - y_im * x_im)
-                parts_im.append(y_re * x_im + y_im * x_re)
+                a = jnp.where(upper, y_re[k], y_re[k + 1])
+                b = jnp.where(upper, y_im[k], y_im[k + 1])
+                parts_re.append(a * x_re - b * x_im)
+                parts_im.append(a * x_im + b * x_re)
             high, low = split(jnp.concatenate(parts + parts_re + parts_im, 0))
             total = dot_nt(jnp.concatenate([z_high, z_low], 0), high)
             total = total[:32] + total[32:] + dot_nt(z_high, low)
@@ -568,15 +538,12 @@
             out[g, 16:32] = total[16:]
         return carry
 
-    for copy in copies:
-        copy.wait()
     lax.fori_loop(0, 4, group, 0)
 
 
 def late_waves(*operands):
     return pl.pallas_call(
         late_body,
-        in_specs=[pl.BlockSpec(memory_space=pltpu.VMEM)] * 5 + [pl.BlockSpec(memory_space=pl.ANY)],
         out_shape=(
             jax.ShapeDtypeStruct((N_FFT, 32, PAIRS), F32),
             jax.ShapeDtypeStruct((8, 128), F32),
@@ -585,10 +552,8 @@
             pltpu.VMEM((128, 128), F32),
             pltpu.VMEM((128, 128), F32),
             pltpu.VMEM((2, 128, 128), F32),
-            pltpu.VMEM((N_FFT, 64, ROWS), F32),
-            pltpu.SemaphoreType.DMA((4,)),
         ],
-        compiler_params=pltpu.CompilerParams(vmem_limit_bytes=LATE),
+        compiler_params=pltpu.CompilerParams(vmem_limit_bytes=SOME),
         cost_estimate=pl.CostEstimate(flops=5_000_000_000, bytes_accessed=7_000_000, transcendentals=0),
         name="late_waves",
     )(*operands)
@@ -614,7 +579,7 @@
     return pl.pallas_call(
         z_body,
         out_shape=(shape, shape, jax.ShapeDtypeStruct((1, OWN), F32)),
-        compiler_params=pltpu.CompilerParams(vmem_limit_bytes=2 * SOME),
+        compiler_params=pltpu.CompilerParams(vmem_limit_bytes=SOME),
         cost_estimate=pl.CostEstimate(flops=3_000_000_000, bytes_accessed=5_000_000, transcendentals=0),
         name="along_z",
     )(*operands)
@@ -656,16 +621,11 @@
     got_3 = swap(along_y(got_2, matrix, jnp.asarray(perm_y()), arh, arl, aih, ail), "fft")
     quads = swap(quad_sum(got_3), "slab")
 
-    steps = jnp.concatenate(
-        [
-            lax.dynamic_index_in_dim(jnp.asarray(step_table(N_SLAB)), s, 0, False),
-            lax.dynamic_index_in_dim(jnp.asarray(step_table(N_FFT)), f, 0, False),
-        ],
-        1,
-    )
-    waves = tables(got_1, steps)
+    steps_x = lax.dynamic_index_in_dim(jnp.asarray(step_table(N_SLAB)), s, 0, False)
+    steps_y = lax.dynamic_index_in_dim(jnp.asarray(step_table(N_FFT)), f, 0, False)
+    steps = jnp.concatenate([steps_x[:8], steps_y[:8], steps_x[8:], steps_y[8:]], 0)
     before = early(got_1, first_full)
-    ml, rest = late_waves(got_1, before, first_full, got_3, jnp.asarray(perm_z()), waves)
+    ml, rest = late_waves(got_1, before, first_full, got_3, jnp.asarray(perm_z()), steps)
     z_waves = jnp.asarray(np.stack([t for half in z_tables() for t in two_parts(half)]))
     struct_re, struct_im, charge = along_z(ml, quads, rest, z_waves)
     return (charge.reshape(OWN), struct_re, struct_im)

time: 138 us -> 139 us (level)
  waiting for transfers between devices: 10.1 us -> 18.5 us
  Pallas kernels: 54.7 us -> 47 us
    all_to_all x4, waiting for transfers between devices: 10.1 us -> 18.5 us  [swap(): return lax.all_to_all(value, axis, 0, 0, tiled=True)]
    pallas_call x2 -> x1, Pallas kernels: 21.2 us -> 13.5 us  [late_waves(): pl.pallas_call(late_body, out_shape=(jax.ShapeDtypeStruct((N_FFT, 32, PAI...]
    squeeze x4 -> x0, local copies, waits for them, and re-layouts: 1.53 us -> none  [the longest x2 0.77 us: on_device(): lax.dynamic_index_in_dim(jnp.asarray(step_table(N_FFT)), f, 0, False)]
    slice x0 -> x2, local copies, waits for them, and re-layouts: none -> 1.42 us  [the longest x1 0.71 us: on_device(): steps_y[8:]]
    unnamed x32 -> x24, local copies, waits for them, and re-layouts: 4.46 us -> 5.7 us
  transfers between devices with their start and end apart: 4 -> 4, of which waited for: 3 -> 3; matrix products, arithmetic and copies ran while one was open for 2% -> 1% of each run, Pallas kernels for 34% -> 28%
where the time goes in v7:
time: 139 us; the launch traced here: 138 us
  Pallas kernels  47 us (34%)
  starting transfers between devices  31.9 us (23%)
  blocking collectives  31.9 us (23%)
  waiting for transfers between devices  18.5 us (13%)
  local copies, waits for them, and re-layouts  7.54 us (5%)
    all_to_all x4, starting transfers between devices, swap(): return lax.all_to_all(value, axis, 0, 0, tiled=True)  31.9 us
    all_to_all x1, blocking collectives, swap(): return lax.all_to_all(value, axis, 0, 0, tiled=True)  31.9 us
    all_to_all x4, waiting for transfers between devices, swap(): return lax.all_to_all(value, axis, 0, 0, tiled=True)  18.5 us
    pallas_call x1, Pallas kernels, spread(): pl.pallas_call(spread_body, grid=(SITES // CHUNK,), in_specs=[pl.BlockSpe...  15.3 us
    pallas_call x1, Pallas kernels, late_waves(): pl.pallas_call(late_body, out_shape=(jax.ShapeDtypeStruct((N_FFT, 32, PAI...  13.5 us
    unnamed x24, local copies, waits for them, and re-layouts  5.7 us
    pallas_call x1, Pallas kernels, couple(): pl.pallas_call(couple_body, out_shape=jax.ShapeDtypeStruct((ROWS, COLS),...  5.27 us
    pallas_call x1, Pallas kernels, early(): pl.pallas_call(early_body, out_shape=jax.ShapeDtypeStruct((2, 128, 128),...  4.53 us
  transfers between devices with their start and end apart: 4, of which 3 were waited for; matrix products, arithmetic and copies ran while one was open for 1% of the time, Pallas kernels for 28%

profile of v7, /device:TPU:1, one launch (start us, length us, event | category | flops | bytes accessed | tf_op | source)
XLA Modules:
  0.0 138.0 jit_solution(4367209312222222611)
XLA Ops:
  0.6 1.8 %pack.1 = (f32[16,8,128]{2,1,0:T(8,128)}, f32[8,1536]{1,0:T(8,128)}) custom-call(f32[1,32]{1,0:T(1,128)} %bitcast.25, s32[1,32]{1,0:T(1,128)} %bitcast.26, s32[3,32]{1,0:T(4,128)} %cell.2, f32[3,32]{1,0:T(4,128)} %frac.2, f32[1,32]{1,0:T(1,128)} %bitcast.27, f32[3,16384]{1,0:T(4,128)} %pos.1, f32[1,16384]{1,0:T(1,128)} %bitcast.22), custom_call_target="tpu_custom_call" | custom-call | tf_op jit(solution)/shard_map/pack/pallas_call | solution.py:227
  2.4 10.2 %all-to-all-start = ((f32[16,8,128]{2,1,0:T(8,128)}), f32[16,8,128]{2,1,0:T(8,128)S(1)}, u32[]{:S(2)}, u32[]{:S(2)}) async-start(f32[16,8,128]{2,1,0:T(8,128)} %get-tuple-element.10), calls=%async_computation | async-start | bytes 131072 | tf_op jit(solution)/shard_map/all_to_all | solution.py:589
  12.6 0.8 copy-done.1
  13.4 5.3 %couple.1.matrix = f32[512,1024]{1,0:T(8,128)S(1)} custom-call(f32[8,1536]{1,0:T(8,128)S(1)} %copy-done.1), custom_call_target="tpu_custom_call" | custom-call | flops 100000000 | bytes 2000000 | tf_op jit(solution)/shard_map/couple/pallas_call | solution.py:295
  18.7 1.8 %all-to-all-done.got = f32[16,8,128]{2,1,0:T(8,128)S(1)} async-done(((f32[16,8,128]{2,1,0:T(8,128)}), f32[16,8,128]{2,1,0:T(8,128)S(1)}, u32[]{:S(2)}, u32[]{:S(2)}) %all-to-all-start) | async-done | bytes 65568 | tf_op jit(solution)/shard_map/all_to_all | solution.py:589
  20.4 1.3 first_product.1
  21.7 11.3 %all-to-all-start.1 = ((f32[32,40,128]{2,1,0:T(8,128)}), f32[32,40,128]{2,1,0:T(8,128)S(1)}, u32[]{:S(2)}, u32[]{:S(2)}) async-start(f32[32,40,128]{2,1,0:T(8,128)} %first_product.1), calls=%async_computation.1 | async-start | bytes 1310720 | tf_op jit(solution)/shard_map/all_to_all | solution.py:589
  33.0 15.3 %spread.1 = f32[16,32,384]{2,1,0:T(8,128)} custom-call(f32[1,6144]{1,0:T(1,128)} %bitcast.28, f32[3,6144]{1,0:T(4,128)} %frac.3, s32[3,6144]{1,0:T(4,128)} %cell.3, bf16[2,392,384]{2,1,0:T(8,128)(2,1)} %constant.42.clone.waves_from), custom_call_target="tpu_custom_call" | custom-call | flops 8000000000 | bytes 2000000 | tf_op jit(solution)/shard_map/spread/pallas_call | solution.py:175
  48.3 1.5 %all-to-all-done.1.slots = f32[32,40,128]{2,1,0:T(8,128)S(1)} async-done(((f32[32,40,128]{2,1,0:T(8,128)}), f32[32,40,128]{2,1,0:T(8,128)S(1)}, u32[]{:S(2)}, u32[]{:S(2)}) %all-to-all-start.1) | async-done | bytes 655392 | tf_op jit(solution)/shard_map/all_to_all | solution.py:589
  50.2 31.9 %all_to_all.25.grid = f32[16,32,384]{2,1,0:T(8,128)S(1)} all-to-all(f32[16,32,384]{2,1,0:T(8,128)S(1)} %pad_maximum_fusion), channel_id=1, replica_groups=mesh['fft'=32,'slab'=16] {'slab'}, dimensions={0} | all-to-all | bytes 1572864 | tf_op jit(solution)/shard_map/all_to_all | solution.py:589
  82.1 2.4 %along_y.1 = f32[32,16,384]{2,1,0:T(8,128)S(1)} custom-call(f32[16,32,384]{2,1,0:T(8,128)S(1)} %all_to_all.25.grid, f32[512,1024]{1,0:T(8,128)S(1)} %couple.1.matrix, bf16[384,384]{1,0:T(8,128)(2,1)S(1)} %copy-done.8, bf16[512,768]{1,0:T(8,128)(2,1)S(1)} %copy-done.6, bf16[512,768]{1,0:T(8,128)(2,1)S(1)} %copy-done.5, bf16[512,768]{1,0:T(8,128)(2,1)S(1)} %copy-done.4, ...), custom_call_target="tpu_custom_call" | custom-call | flops 4000000000 | bytes 5000000 | tf_op jit(solution)/shard_map/along_y/pallas_call | solution.py:354
  84.6 0.9 copy-done
  85.4 5.6 %all-to-all-start.3 = ((f32[32,16,384]{2,1,0:T(8,128)}), f32[32,16,384]{2,1,0:T(8,128)S(1)}, u32[]{:S(2)}, u32[]{:S(2)}) async-start(f32[32,16,384]{2,1,0:T(8,128)} %copy-done), calls=%async_computation.3 | async-start | bytes 1572864 | tf_op jit(solution)/shard_map/all_to_all | solution.py:589
  91.0 0.7 dynamic-slice_bitcast_fusion.2
  91.7 0.7 dynamic-slice_bitcast_fusion
  92.9 4.5 %early.1.before = f32[2,128,128]{2,1,0:T(8,128)S(1)} custom-call(f32[32,40,128]{2,1,0:T(8,128)S(1)} %all-to-all-done.1.slots, f32[128,128]{1,0:T(8,128)S(1)} %reshape.47.first), custom_call_target="tpu_custom_call" | custom-call | flops 2000000000 | bytes 1000000 | tf_op jit(solution)/shard_map/early/pallas_call | solution.py:451
  97.4 15.2 %all-to-all-done.3.grid.got = f32[32,16,384]{2,1,0:T(8,128)S(1)} async-done(((f32[32,16,384]{2,1,0:T(8,128)}), f32[32,16,384]{2,1,0:T(8,128)S(1)}, u32[]{:S(2)}, u32[]{:S(2)}) %all-to-all-start.3) | async-done | bytes 786464 | tf_op jit(solution)/shard_map/all_to_all | solution.py:589
  112.6 1.0 quad_sum.1
  113.6 4.9 %all-to-all-start.4 = ((f32[16,8,128]{2,1,0:T(8,128)}), f32[16,8,128]{2,1,0:T(8,128)S(1)}, u32[]{:S(2)}, u32[]{:S(2)}) async-start(f32[16,8,128]{2,1,0:T(8,128)} %quad_sum.1), calls=%async_computation.4 | async-start | bytes 131072 | tf_op jit(solution)/shard_map/all_to_all | solution.py:589
  118.5 13.5 %late_waves.1 = (f32[32,32,288]{2,1,0:T(8,128)S(1)}, f32[8,128]{1,0:T(8,128)S(1)}) custom-call(f32[32,40,128]{2,1,0:T(8,128)S(1)} %all-to-all-done.1.slots, f32[2,128,128]{2,1,0:T(8,128)S(1)} %early.1.before, f32[128,128]{1,0:T(8,128)S(1)} %reshape.47.first, f32[32,16,384]{2,1,0:T(8,128)S(1)} %all-to-all-done.3.grid.got, bf16[384,288]{1,0:T(8,128)(2,1)S(1)} %copy-done.7, ...), custom_call_target="tpu_custom_call" | custom-call | flops 5000000000 | bytes 7000000 | tf_op jit(solution)/shard_map/late_waves/pallas_call | solution.py:545
  132.0 1.2 copy-done.9
  133.2 1.4 %copy-done.2 = bf16[4,512,384]{2,1,0:T(8,128)(2,1)S(1)} copy-done((bf16[4,512,384]{2,1,0:T(8,128)(2,1)S(1)}, bf16[4,512,384]{2,1,0:T(8,128)(2,1)}, u32[]{:S(2)}) %copy-start.2) | copy-done | bytes 1572888
  134.6 1.4 %copy-done.10 = f32[32,32,288]{2,1,0:T(8,128)S(1)} copy-done((f32[32,32,288]{2,1,0:T(8,128)S(1)}, f32[32,32,288]{2,1,0:T(8,128)}, u32[]{:S(2)}) %copy-start.10) | copy-done | bytes 1179672
  136.0 2.0 %along_z.1 = (f32[12,12,384]{2,1,0:T(8,128)}, f32[12,12,384]{2,1,0:T(8,128)}, f32[1,32]{1,0:T(1,128)}) custom-call(f32[32,32,288]{2,1,0:T(8,128)S(1)} %copy-done.10, f32[16,8,128]{2,1,0:T(8,128)S(1)} %all-to-all-done.4.quads, f32[8,128]{1,0:T(8,128)S(1)} %get-tuple-element.13.rest, bf16[4,512,384]{2,1,0:T(8,128)(2,1)S(1)} %copy-done.2), custom_call_target="tpu_custom_call" | custom-call | flops 3000000000 | bytes 5000000 | tf_op jit(solution)/shard_map/along_z/pallas_call | solution.py:579
  (32 shorter events, 0.8 us)
Async XLA Ops:
  2.4 18.0 %all-to-all-start = ((f32[16,8,128]{2,1,0:T(8,128)}), f32[16,8,128]{2,1,0:T(8,128)S(1)}, u32[]{:S(2)}, u32[]{:S(2)}) async-start(f32[16,8,128]{2,1,0:T(8,128)} %get-tuple-element.10), calls=%async_computation | async-start | bytes 131072 | tf_op jit(solution)/shard_map/all_to_all | solution.py:589
  12.6 0.8 copy-start.1
  21.7 28.1 %all-to-all-start.1 = ((f32[32,40,128]{2,1,0:T(8,128)}), f32[32,40,128]{2,1,0:T(8,128)S(1)}, u32[]{:S(2)}, u32[]{:S(2)}) async-start(f32[32,40,128]{2,1,0:T(8,128)} %first_product.1), calls=%async_computation.1 | async-start | bytes 1310720 | tf_op jit(solution)/shard_map/all_to_all | solution.py:589
  48.3 1.9 %copy-start.11 = (f32[16,32,384]{2,1,0:T(8,128)S(1)}, f32[16,32,384]{2,1,0:T(8,128)}, u32[]{:S(2)}) copy-start(f32[16,32,384]{2,1,0:T(8,128)} %spread.1) | copy-start | bytes 2359300
  49.8 32.3 %copy-start.8 = (bf16[384,384]{1,0:T(8,128)(2,1)S(1)}, bf16[384,384]{1,0:T(8,128)(2,1)}, u32[]{:S(2)}) copy-start(bf16[384,384]{1,0:T(8,128)(2,1)} %constant.47.clone.perm) | copy-start | bytes 884740
  50.0 32.0 %copy-start.3 = (bf16[512,768]{1,0:T(8,128)(2,1)S(1)}, bf16[512,768]{1,0:T(8,128)(2,1)}, u32[]{:S(2)}) copy-start(bf16[512,768]{1,0:T(8,128)(2,1)} %constant.46.clone.ail) | copy-start | bytes 2359300
  50.0 32.0 %copy-start.4 = (bf16[512,768]{1,0:T(8,128)(2,1)S(1)}, bf16[512,768]{1,0:T(8,128)(2,1)}, u32[]{:S(2)}) copy-start(bf16[512,768]{1,0:T(8,128)(2,1)} %constant.45.clone.aih) | copy-start | bytes 2359300
  50.1 32.0 %copy-start.5 = (bf16[512,768]{1,0:T(8,128)(2,1)S(1)}, bf16[512,768]{1,0:T(8,128)(2,1)}, u32[]{:S(2)}) copy-start(bf16[512,768]{1,0:T(8,128)(2,1)} %constant.44.clone.arl) | copy-start | bytes 2359300
  50.1 32.0 %copy-start.6 = (bf16[512,768]{1,0:T(8,128)(2,1)S(1)}, bf16[512,768]{1,0:T(8,128)(2,1)}, u32[]{:S(2)}) copy-start(bf16[512,768]{1,0:T(8,128)(2,1)} %constant.43.clone.arh) | copy-start | bytes 2359300
  84.5 0.9 copy-start
  85.4 27.2 %all-to-all-start.3 = ((f32[32,16,384]{2,1,0:T(8,128)}), f32[32,16,384]{2,1,0:T(8,128)S(1)}, u32[]{:S(2)}, u32[]{:S(2)}) async-start(f32[32,16,384]{2,1,0:T(8,128)} %copy-done), calls=%async_computation.3 | async-start | bytes 1572864 | tf_op jit(solution)/shard_map/all_to_all | solution.py:589
  92.9 25.6 %copy-start.7 = (bf16[384,288]{1,0:T(8,128)(2,1)S(1)}, bf16[384,288]{1,0:T(8,128)(2,1)}, u32[]{:S(2)}) copy-start(bf16[384,288]{1,0:T(8,128)(2,1)} %constant.50.clone.perm) | copy-start | bytes 663556
  113.6 19.6 %all-to-all-start.4 = ((f32[16,8,128]{2,1,0:T(8,128)}), f32[16,8,128]{2,1,0:T(8,128)S(1)}, u32[]{:S(2)}, u32[]{:S(2)}) async-start(f32[16,8,128]{2,1,0:T(8,128)} %quad_sum.1), calls=%async_computation.4 | async-start | bytes 131072 | tf_op jit(solution)/shard_map/all_to_all | solution.py:589
  132.0 1.2 copy-start.9
  133.2 1.4 %copy-start.2 = (bf16[4,512,384]{2,1,0:T(8,128)(2,1)S(1)}, bf16[4,512,384]{2,1,0:T(8,128)(2,1)}, u32[]{:S(2)}) copy-start(bf16[4,512,384]{2,1,0:T(8,128)(2,1)} %constant.51.clone.waves) | copy-start | bytes 4718596
  134.6 1.4 %copy-start.10 = (f32[32,32,288]{2,1,0:T(8,128)S(1)}, f32[32,32,288]{2,1,0:T(8,128)}, u32[]{:S(2)}) copy-start(f32[32,32,288]{2,1,0:T(8,128)} %copy-done.9) | copy-start | bytes 3538948

commit v8 on v7

--- a/solution.py
+++ b/solution.py
@@ -458,7 +458,47 @@
     )(slots, first)
 
 
-def late_body(slots, before, first, grid, perm, steps, out, rest, v2, late, charges):
+def ml_group(i, slots, charges, grid, perm, steps, store):
+    f, s = my_place()
+    upper = lax.broadcasted_iota(jnp.int32, (8, 1), 0) < 4
+    block = (lax.broadcasted_iota(jnp.int32, (1, ROWS), 1) // OWN * YL).astype(F32)
+    local = lax.broadcasted_iota(jnp.int32, (24, 1), 0)
+    freq = jnp.where(local < 8, s * KX + local, f * KY + local - 8)
+    freq = jnp.where(local < 16, freq, jnp.where(local < 20, s * KX + local - 8, f * KY + local - 12)).astype(F32)
+    at = pl.multiple_of(i * 32, 32)
+    charge = [charges[v, pl.ds(at, 32), :] for v in range(2)]
+    high, low = split(grid[pl.ds(i * 8, 8)].reshape(128, 384))
+    base = (dot_nn(high, perm[...]) + dot_nn(low, perm[...])).reshape(8, 16, PAIRS)
+    for j in range(8):
+        g = i * 8 + j
+        rows = slot_rows(slots, g)
+        placed_z = placed(16, rows[4:5].astype(jnp.int32), spline(rows[7:8]))
+        both = [placed_z * lanes(charge[v][j * 4 : j * 4 + 4]) for v in range(2)]
+        z_high, z_low = split(jnp.concatenate(both, 0))
+        re, im = site_waves(freq, (rows[2:3], rows[3:4] + block), (rows[5:6], rows[6:7]), steps[...])
+        x_re, x_im = re[0:8], im[0:8]
+        y_re = [re[8 + k : 9 + k] for k in range(8)] + [re[20 + k : 21 + k] for k in range(4)]
+        y_im = [im[8 + k : 9 + k] for k in range(8)] + [im[20 + k : 21 + k] for k in range(4)]
+        parts_re, parts_im = [], []
+        for k in range(KY):
+            a, b = y_re[k], y_im[k]
+            parts_re.append(a * x_re - b * x_im)
+            parts_im.append(a * x_im + b * x_re)
+        parts = parts_re + parts_im
+        x_re, x_im = (jnp.where(upper, v[16:24], pltpu.roll(v[16:24], 4, 0)) for v in (re, im))
+        parts_re, parts_im = [], []
+        for k in range(0, KY, 2):
+            a = jnp.where(upper, y_re[k], y_re[k + 1])
+            b = jnp.where(upper, y_im[k], y_im[k + 1])
+            parts_re.append(a * x_re - b * x_im)
+            parts_im.append(a * x_im + b * x_re)
+        high, low = split(jnp.concatenate(parts + parts_re + parts_im, 0))
+        total = dot_nt(jnp.concatenate([z_high, z_low], 0), high)
+        total = total[:32] + total[32:] + dot_nt(z_high, low)
+        store(g, total[:16] + base[j], total[16:])
+
+
+def solve_body(slots, before, first, grid, perm, steps, out, rest, charges, v2, late):
     f, s = my_place()
     for i in range(4):
         pieces = [grid[:, i * 4 + j, 352:384] for j in range(4)]
@@ -497,73 +537,68 @@
     rest[2:3] = jnp.broadcast_to(l20 * m3 + l21 * e12, (1, 128))
     rest[3:4] = jnp.broadcast_to(g2, (1, 128))
 
-    upper = lax.broadcasted_iota(jnp.int32, (8, 1), 0) < 4
-    block = (lax.broadcasted_iota(jnp.int32, (1, ROWS), 1) // OWN * YL).astype(F32)
-    local = lax.broadcasted_iota(jnp.int32, (24, 1), 0)
-    freq = jnp.where(local < 8, s * KX + local, f * KY + local - 8)
-    freq = jnp.where(local < 16, freq, jnp.where(local < 20, s * KX + local - 8, f * KY + local - 12)).astype(F32)
+    def store(g, base, last):
+        out[g, 0:16] = base
+        out[g, 16:32] = last
 
     def group(i, carry):
-        at = pl.multiple_of(i * 32, 32)
-        charge = [charges[v, pl.ds(at, 32), :] for v in range(2)]
-        high, low = split(grid[pl.ds(i * 8, 8)].reshape(128, 384))
-        base = (dot_nn(high, perm[...]) + dot_nn(low, perm[...])).reshape(8, 16, PAIRS)
-        for j in range(8):
-            g = i * 8 + j
-            rows = slot_rows(slots, g)
-            placed_z = placed(16, rows[4:5].astype(jnp.int32), spline(rows[7:8]))
-            both = [placed_z * lanes(charge[v][j * 4 : j * 4 + 4]) for v in range(2)]
-            z_high, z_low = split(jnp.concatenate(both, 0))
-            re, im = site_waves(freq, (rows[2:3], rows[3:4] + block), (rows[5:6], rows[6:7]), steps[...])
-            x_re, x_im = re[0:8], im[0:8]
-            y_re = [re[8 + k : 9 + k] for k in range(8)] + [re[20 + k : 21 + k] for k in range(4)]
-            y_im = [im[8 + k : 9 + k] for k in range(8)] + [im[20 + k : 21 + k] for k in range(4)]
-            parts_re, parts_im = [], []
-            for k in range(KY):
-                a, b = y_re[k], y_im[k]
-                parts_re.append(a * x_re - b * x_im)
-                parts_im.append(a * x_im + b * x_re)
-            parts = parts_re + parts_im
-            x_re, x_im = (jnp.where(upper, v[16:24], pltpu.roll(v[16:24], 4, 0)) for v in (re, im))
-            parts_re, parts_im = [], []
-            for k in range(0, KY, 2):
-                a = jnp.where(upper, y_re[k], y_re[k + 1])
-                b = jnp.where(upper, y_im[k], y_im[k + 1])
-                parts_re.append(a * x_re - b * x_im)
-                parts_im.append(a * x_im + b * x_re)
-            high, low = split(jnp.concatenate(parts + parts_re + parts_im, 0))
-            total = dot_nt(jnp.concatenate([z_high, z_low], 0), high)
-            total = total[:32] + total[32:] + dot_nt(z_high, low)
-            out[g, 0:16] = total[:16] + base[j]
-            out[g, 16:32] = total[16:]
+        ml_group(i, slots, charges, grid, perm, steps, store)
         return carry
 
-    lax.fori_loop(0, 4, group, 0)
-
-
-def late_waves(*operands):
-    return pl.pallas_call(
-        late_body,
+    lax.fori_loop(0, 2, group, 0)
+
+
+def solve(*operands):
+    return pl.pallas_call(
+        solve_body,
         out_shape=(
-            jax.ShapeDtypeStruct((N_FFT, 32, PAIRS), F32),
+            jax.ShapeDtypeStruct((N_FFT // 2, 32, PAIRS), F32),
             jax.ShapeDtypeStruct((8, 128), F32),
+            jax.ShapeDtypeStruct((2, 128, 128), F32),
         ),
-        scratch_shapes=[
-            pltpu.VMEM((128, 128), F32),
-            pltpu.VMEM((128, 128), F32),
-            pltpu.VMEM((2, 128, 128), F32),
-        ],
+        scratch_shapes=[pltpu.VMEM((128, 128), F32), pltpu.VMEM((128, 128), F32)],
         compiler_params=pltpu.CompilerParams(vmem_limit_bytes=SOME),
-        cost_estimate=pl.CostEstimate(flops=5_000_000_000, bytes_accessed=7_000_000, transcendentals=0),
-        name="late_waves",
+        cost_estimate=pl.CostEstimate(flops=5_000_000_000, bytes_accessed=4_000_000, transcendentals=0),
+        name="solve",
     )(*operands)
 
 
-def z_body(ml, quads, rest, waves, out_re, out_im, out_q):
+def last_step(quads, rest):
     m5 = jnp.sum(quads[:, 0, :], 0, keepdims=True)
-    step = guarded(rest[3:4], m5 - rest[2:3], m5)[:, 0:1]
-    total = ml[:, 0:16] + step[None] * ml[:, 16:32]
-    both = split(total.reshape(N_FFT * 16, PAIRS))
+    return guarded(rest[3:4], m5 - rest[2:3], m5)[:, 0:1]
+
+
+def join_body(slots, charges, grid, perm, steps, early_half, quads, rest, out, out_q):
+    step = last_step(quads, rest)
+    half = N_FFT // 2
+    out[0:half] = early_half[:, 0:16] + step[None] * early_half[:, 16:32]
+    out_q[...] = (rest[0:1] + step * rest[1:2])[:, 0:OWN]
+
+    def store(g, base, last):
+        out[g] = base + step * last
+
+    def group(i, carry):
+        ml_group(i, slots, charges, grid, perm, steps, store)
+        return carry
+
+    lax.fori_loop(2, 4, group, 0)
+
+
+def join(*operands):
+    return pl.pallas_call(
+        join_body,
+        out_shape=(
+            jax.ShapeDtypeStruct((N_FFT, 16, PAIRS), F32),
+            jax.ShapeDtypeStruct((1, OWN), F32),
+        ),
+        compiler_params=pltpu.CompilerParams(vmem_limit_bytes=SOME),
+        cost_estimate=pl.CostEstimate(flops=4_000_000_000, bytes_accessed=4_000_000, transcendentals=0),
+        name="join",
+    )(*operands)
+
+
+def z_body(grid, waves, out_re, out_im):
+    both = split(grid[...].reshape(N_FFT * 16, PAIRS))
     cos = three(dot_tn, both, (waves[0], waves[1]))
     sin = three(dot_tn, both, (waves[2], waves[3]))
     for k in range(KY):
@@ -571,14 +606,13 @@
             im = re + KY * count
             out_re[k, first : first + count] = cos[re : re + count] + sin[im : im + count]
             out_im[k, first : first + count] = cos[im : im + count] - sin[re : re + count]
-    out_q[...] = (rest[0:1] + step * rest[1:2])[:, 0:OWN]
 
 
 def along_z(*operands):
     shape = jax.ShapeDtypeStruct((KY, KX, NG), F32)
     return pl.pallas_call(
         z_body,
-        out_shape=(shape, shape, jax.ShapeDtypeStruct((1, OWN), F32)),
+        out_shape=(shape, shape),
         compiler_params=pltpu.CompilerParams(vmem_limit_bytes=SOME),
         cost_estimate=pl.CostEstimate(flops=3_000_000_000, bytes_accessed=5_000_000, transcendentals=0),
         name="along_z",
@@ -625,9 +659,11 @@
     steps_y = lax.dynamic_index_in_dim(jnp.asarray(step_table(N_FFT)), f, 0, False)
     steps = jnp.concatenate([steps_x[:8], steps_y[:8], steps_x[8:], steps_y[8:]], 0)
     before = early(got_1, first_full)
-    ml, rest = late_waves(got_1, before, first_full, got_3, jnp.asarray(perm_z()), steps)
-    z_waves = jnp.asarray(np.stack([t for half in z_tables() for t in two_parts(half)]))
-    struct_re, struct_im, charge = along_z(ml, quads, rest, z_waves)
+    perm = jnp.asarray(perm_z())
+    half, rest, charges = solve(got_1, before, first_full, got_3, perm, steps)
+    total, charge = join(got_1, charges, got_3, perm, steps, half, quads, rest)
+    z_waves = jnp.asarray(np.stack([t for part in z_tables() for t in two_parts(part)]))
+    struct_re, struct_im = along_z(total, z_waves)
     return (charge.reshape(OWN), struct_re, struct_im)
 
 

time: 139 us -> 135 us (0.971)
  local copies, waits for them, and re-layouts: 7.54 us -> 3.56 us
    unnamed x24 -> x20, local copies, waits for them, and re-layouts: 5.7 us -> 1.72 us
    pallas_call x2 -> x3, Pallas kernels: 15.5 us -> 15.8 us  [the longest x1 8.32 us: solve(): pl.pallas_call(solve_body, out_shape=(jax.ShapeDtypeStruct((N_FFT // 2, 3...]
  transfers between devices with their start and end apart: 4 -> 4, of which waited for: 3 -> 3; matrix products, arithmetic and copies ran while one was open for 1% -> 1% of each run, Pallas kernels for 28% -> 25%
where the time goes in v8:
time: 135 us; the launch traced here: 134 us
  Pallas kernels  47.3 us (35%)
  starting transfers between devices  31.9 us (24%)
  blocking collectives  31.9 us (24%)
  waiting for transfers between devices  18.4 us (14%)
  local copies, waits for them, and re-layouts  3.56 us (3%)
    all_to_all x4, starting transfers between devices, swap(): return lax.all_to_all(value, axis, 0, 0, tiled=True)  31.9 us
    all_to_all x1, blocking collectives, swap(): return lax.all_to_all(value, axis, 0, 0, tiled=True)  31.9 us
    all_to_all x4, waiting for transfers between devices, swap(): return lax.all_to_all(value, axis, 0, 0, tiled=True)  18.4 us
    pallas_call x1, Pallas kernels, spread(): pl.pallas_call(spread_body, grid=(SITES // CHUNK,), in_specs=[pl.BlockSpe...  15.3 us
    pallas_call x1, Pallas kernels, solve(): pl.pallas_call(solve_body, out_shape=(jax.ShapeDtypeStruct((N_FFT // 2, 3...  8.32 us
    pallas_call x1, Pallas kernels, join(): pl.pallas_call(join_body, out_shape=(jax.ShapeDtypeStruct((N_FFT, 16, PAI...  5.52 us
    pallas_call x1, Pallas kernels, couple(): pl.pallas_call(couple_body, out_shape=jax.ShapeDtypeStruct((ROWS, COLS),...  5.27 us
    pallas_call x1, Pallas kernels, early(): pl.pallas_call(early_body, out_shape=jax.ShapeDtypeStruct((2, 128, 128),...  4.53 us
  transfers between devices with their start and end apart: 4, of which 3 were waited for; matrix products, arithmetic and copies ran while one was open for 1% of the time, Pallas kernels for 25%

profile of v8, /device:TPU:1, one launch (start us, length us, event | category | flops | bytes accessed | tf_op | source)
XLA Modules:
  0.0 134.3 jit_solution(5534933564732698056)
XLA Ops:
  0.6 1.8 %pack.1 = (f32[16,8,128]{2,1,0:T(8,128)}, f32[8,1536]{1,0:T(8,128)}) custom-call(f32[1,32]{1,0:T(1,128)} %bitcast.25, s32[1,32]{1,0:T(1,128)} %bitcast.26, s32[3,32]{1,0:T(4,128)} %cell.2, f32[3,32]{1,0:T(4,128)} %frac.2, f32[1,32]{1,0:T(1,128)} %bitcast.27, f32[3,16384]{1,0:T(4,128)} %pos.1, f32[1,16384]{1,0:T(1,128)} %bitcast.22), custom_call_target="tpu_custom_call" | custom-call | tf_op jit(solution)/shard_map/pack/pallas_call | solution.py:227
  2.4 10.2 %all-to-all-start = ((f32[16,8,128]{2,1,0:T(8,128)}), f32[16,8,128]{2,1,0:T(8,128)S(1)}, u32[]{:S(2)}, u32[]{:S(2)}) async-start(f32[16,8,128]{2,1,0:T(8,128)} %get-tuple-element.12), calls=%async_computation | async-start | bytes 131072 | tf_op jit(solution)/shard_map/all_to_all | solution.py:623
  12.6 0.8 copy-done.1
  13.4 5.3 %couple.1.matrix = f32[512,1024]{1,0:T(8,128)S(1)} custom-call(f32[8,1536]{1,0:T(8,128)S(1)} %copy-done.1), custom_call_target="tpu_custom_call" | custom-call | flops 100000000 | bytes 2000000 | tf_op jit(solution)/shard_map/couple/pallas_call | solution.py:295
  18.7 1.8 %all-to-all-done.got = f32[16,8,128]{2,1,0:T(8,128)S(1)} async-done(((f32[16,8,128]{2,1,0:T(8,128)}), f32[16,8,128]{2,1,0:T(8,128)S(1)}, u32[]{:S(2)}, u32[]{:S(2)}) %all-to-all-start) | async-done | bytes 65568 | tf_op jit(solution)/shard_map/all_to_all | solution.py:623
  20.4 1.3 first_product.1
  21.7 11.3 %all-to-all-start.1 = ((f32[32,40,128]{2,1,0:T(8,128)}), f32[32,40,128]{2,1,0:T(8,128)S(1)}, u32[]{:S(2)}, u32[]{:S(2)}) async-start(f32[32,40,128]{2,1,0:T(8,128)} %first_product.1), calls=%async_computation.1 | async-start | bytes 1310720 | tf_op jit(solution)/shard_map/all_to_all | solution.py:623
  33.0 15.3 %spread.1 = f32[16,32,384]{2,1,0:T(8,128)} custom-call(f32[1,6144]{1,0:T(1,128)} %bitcast.28, f32[3,6144]{1,0:T(4,128)} %frac.3, s32[3,6144]{1,0:T(4,128)} %cell.3, bf16[2,392,384]{2,1,0:T(8,128)(2,1)} %constant.42.clone.waves_from), custom_call_target="tpu_custom_call" | custom-call | flops 8000000000 | bytes 2000000 | tf_op jit(solution)/shard_map/spread/pallas_call | solution.py:175
  48.3 1.5 %all-to-all-done.1.slots = f32[32,40,128]{2,1,0:T(8,128)S(1)} async-done(((f32[32,40,128]{2,1,0:T(8,128)}), f32[32,40,128]{2,1,0:T(8,128)S(1)}, u32[]{:S(2)}, u32[]{:S(2)}) %all-to-all-start.1) | async-done | bytes 655392 | tf_op jit(solution)/shard_map/all_to_all | solution.py:623
  49.8 0.2 multiply_reduce_fusion
  50.2 31.9 %all_to_all.25.grid = f32[16,32,384]{2,1,0:T(8,128)S(1)} all-to-all(f32[16,32,384]{2,1,0:T(8,128)S(1)} %pad_maximum_fusion), channel_id=1, replica_groups=mesh['fft'=32,'slab'=16] {'slab'}, dimensions={0} | all-to-all | bytes 1572864 | tf_op jit(solution)/shard_map/all_to_all | solution.py:623
  82.1 2.4 %along_y.1 = f32[32,16,384]{2,1,0:T(8,128)S(1)} custom-call(f32[16,32,384]{2,1,0:T(8,128)S(1)} %all_to_all.25.grid, f32[512,1024]{1,0:T(8,128)S(1)} %couple.1.matrix, bf16[384,384]{1,0:T(8,128)(2,1)S(1)} %copy-done.8, bf16[512,768]{1,0:T(8,128)(2,1)S(1)} %copy-done.6, bf16[512,768]{1,0:T(8,128)(2,1)S(1)} %copy-done.5, bf16[512,768]{1,0:T(8,128)(2,1)S(1)} %copy-done.4, ...), custom_call_target="tpu_custom_call" | custom-call | flops 4000000000 | bytes 5000000 | tf_op jit(solution)/shard_map/along_y/pallas_call | solution.py:354
  84.5 0.9 copy-done
  85.4 5.6 %all-to-all-start.3 = ((f32[32,16,384]{2,1,0:T(8,128)}), f32[32,16,384]{2,1,0:T(8,128)S(1)}, u32[]{:S(2)}, u32[]{:S(2)}) async-start(f32[32,16,384]{2,1,0:T(8,128)} %copy-done), calls=%async_computation.3 | async-start | bytes 1572864 | tf_op jit(solution)/shard_map/all_to_all | solution.py:623
  91.0 0.7 dynamic-slice_bitcast_fusion.2
  91.7 0.7 dynamic-slice_bitcast_fusion
  92.6 0.2 copy.33
  92.9 4.5 %early.1.before = f32[2,128,128]{2,1,0:T(8,128)S(1)} custom-call(f32[32,40,128]{2,1,0:T(8,128)S(1)} %all-to-all-done.1.slots, f32[128,128]{1,0:T(8,128)S(1)} %reshape.47.first), custom_call_target="tpu_custom_call" | custom-call | flops 2000000000 | bytes 1000000 | tf_op jit(solution)/shard_map/early/pallas_call | solution.py:451
  97.4 15.2 %all-to-all-done.3.grid.got = f32[32,16,384]{2,1,0:T(8,128)S(1)} async-done(((f32[32,16,384]{2,1,0:T(8,128)}), f32[32,16,384]{2,1,0:T(8,128)S(1)}, u32[]{:S(2)}, u32[]{:S(2)}) %all-to-all-start.3) | async-done | bytes 786464 | tf_op jit(solution)/shard_map/all_to_all | solution.py:623
  112.6 1.0 quad_sum.1
  113.6 4.9 %all-to-all-start.4 = ((f32[16,8,128]{2,1,0:T(8,128)}), f32[16,8,128]{2,1,0:T(8,128)S(1)}, u32[]{:S(2)}, u32[]{:S(2)}) async-start(f32[16,8,128]{2,1,0:T(8,128)} %quad_sum.1), calls=%async_computation.4 | async-start | bytes 131072 | tf_op jit(solution)/shard_map/all_to_all | solution.py:623
  118.5 8.3 %solve.1 = (f32[16,32,288]{2,1,0:T(8,128)S(1)}, f32[8,128]{1,0:T(8,128)S(1)}, f32[2,128,128]{2,1,0:T(8,128)S(1)}) custom-call(f32[32,40,128]{2,1,0:T(8,128)S(1)} %all-to-all-done.1.slots, f32[2,128,128]{2,1,0:T(8,128)S(1)} %early.1.before, f32[128,128]{1,0:T(8,128)S(1)} %reshape.47.first, f32[32,16,384]{2,1,0:T(8,128)S(1)} %all-to-all-done.3.grid.got, ...), custom_call_target="tpu_custom_call" | custom-call | flops 5000000000 | bytes 4000000 | tf_op jit(solution)/shard_map/solve/pallas_call | solution.py:552
  126.8 5.5 %join.1 = (f32[32,16,288]{2,1,0:T(8,128)S(1)}, f32[1,32]{1,0:T(1,128)}) custom-call(f32[32,40,128]{2,1,0:T(8,128)S(1)} %all-to-all-done.1.slots, f32[2,128,128]{2,1,0:T(8,128)S(1)} %get-tuple-element.14.charges, f32[32,16,384]{2,1,0:T(8,128)S(1)} %all-to-all-done.3.grid.got, bf16[384,288]{1,0:T(8,128)(2,1)S(1)} %copy-done.7, ...), custom_call_target="tpu_custom_call" | custom-call | flops 4000000000 | bytes 4000000 | tf_op jit(solution)/shard_map/join/pallas_call | solution.py:588
  132.3 1.9 %along_z.1 = (f32[12,12,384]{2,1,0:T(8,128)}, f32[12,12,384]{2,1,0:T(8,128)}) custom-call(f32[32,16,288]{2,1,0:T(8,128)S(1)} %get-tuple-element.18.grid, bf16[4,512,384]{2,1,0:T(8,128)(2,1)S(1)} %copy-done.2), custom_call_target="tpu_custom_call" | custom-call | flops 3000000000 | bytes 5000000 | tf_op jit(solution)/shard_map/along_z/pallas_call | solution.py:613
  (29 shorter events, 0.5 us)
Async XLA Ops:
  2.4 18.0 %all-to-all-start = ((f32[16,8,128]{2,1,0:T(8,128)}), f32[16,8,128]{2,1,0:T(8,128)S(1)}, u32[]{:S(2)}, u32[]{:S(2)}) async-start(f32[16,8,128]{2,1,0:T(8,128)} %get-tuple-element.12), calls=%async_computation | async-start | bytes 131072 | tf_op jit(solution)/shard_map/all_to_all | solution.py:623
  12.6 0.8 copy-start.1
  21.7 28.1 %all-to-all-start.1 = ((f32[32,40,128]{2,1,0:T(8,128)}), f32[32,40,128]{2,1,0:T(8,128)S(1)}, u32[]{:S(2)}, u32[]{:S(2)}) async-start(f32[32,40,128]{2,1,0:T(8,128)} %first_product.1), calls=%async_computation.1 | async-start | bytes 1310720 | tf_op jit(solution)/shard_map/all_to_all | solution.py:623
  48.3 1.8 %copy-start.9 = (f32[16,32,384]{2,1,0:T(8,128)S(1)}, f32[16,32,384]{2,1,0:T(8,128)}, u32[]{:S(2)}) copy-start(f32[16,32,384]{2,1,0:T(8,128)} %spread.1) | copy-start | bytes 2359300
  49.8 32.3 %copy-start.8 = (bf16[384,384]{1,0:T(8,128)(2,1)S(1)}, bf16[384,384]{1,0:T(8,128)(2,1)}, u32[]{:S(2)}) copy-start(bf16[384,384]{1,0:T(8,128)(2,1)} %constant.47.clone.perm) | copy-start | bytes 884740
  50.0 32.0 %copy-start.3 = (bf16[512,768]{1,0:T(8,128)(2,1)S(1)}, bf16[512,768]{1,0:T(8,128)(2,1)}, u32[]{:S(2)}) copy-start(bf16[512,768]{1,0:T(8,128)(2,1)} %constant.46.clone.ail) | copy-start | bytes 2359300
  50.0 32.0 %copy-start.4 = (bf16[512,768]{1,0:T(8,128)(2,1)S(1)}, bf16[512,768]{1,0:T(8,128)(2,1)}, u32[]{:S(2)}) copy-start(bf16[512,768]{1,0:T(8,128)(2,1)} %constant.45.clone.aih) | copy-start | bytes 2359300
  50.0 32.0 %copy-start.5 = (bf16[512,768]{1,0:T(8,128)(2,1)S(1)}, bf16[512,768]{1,0:T(8,128)(2,1)}, u32[]{:S(2)}) copy-start(bf16[512,768]{1,0:T(8,128)(2,1)} %constant.44.clone.arl) | copy-start | bytes 2359300
  50.1 32.0 %copy-start.6 = (bf16[512,768]{1,0:T(8,128)(2,1)S(1)}, bf16[512,768]{1,0:T(8,128)(2,1)}, u32[]{:S(2)}) copy-start(bf16[512,768]{1,0:T(8,128)(2,1)} %constant.43.clone.arh) | copy-start | bytes 2359300
  84.5 0.9 copy-start
  85.4 27.2 %all-to-all-start.3 = ((f32[32,16,384]{2,1,0:T(8,128)}), f32[32,16,384]{2,1,0:T(8,128)S(1)}, u32[]{:S(2)}, u32[]{:S(2)}) async-start(f32[32,16,384]{2,1,0:T(8,128)} %copy-done), calls=%async_computation.3 | async-start | bytes 1572864 | tf_op jit(solution)/shard_map/all_to_all | solution.py:623
  92.9 25.6 %copy-start.7 = (bf16[384,288]{1,0:T(8,128)(2,1)S(1)}, bf16[384,288]{1,0:T(8,128)(2,1)}, u32[]{:S(2)}) copy-start(bf16[384,288]{1,0:T(8,128)(2,1)} %constant.50.clone.perm) | copy-start | bytes 663556
  113.6 13.2 %all-to-all-start.4 = ((f32[16,8,128]{2,1,0:T(8,128)}), f32[16,8,128]{2,1,0:T(8,128)S(1)}, u32[]{:S(2)}, u32[]{:S(2)}) async-start(f32[16,8,128]{2,1,0:T(8,128)} %quad_sum.1), calls=%async_computation.4 | async-start | bytes 131072 | tf_op jit(solution)/shard_map/all_to_all | solution.py:623
  126.8 5.5 %copy-start.2 = (bf16[4,512,384]{2,1,0:T(8,128)(2,1)S(1)}, bf16[4,512,384]{2,1,0:T(8,128)(2,1)}, u32[]{:S(2)}) copy-start(bf16[4,512,384]{2,1,0:T(8,128)(2,1)} %constant.51.clone.waves) | copy-start | bytes 4718596

commit v9 on v8

--- a/solution.py
+++ b/solution.py
@@ -434,7 +434,11 @@
     ]
 
 
-def early_body(slots, first, out, v0):
+def early_body(slots, first, steps, out, ready_0, ready_2, v0):
+    waves = phases(steps)
+    for ready, start in ((ready_0, 0), (ready_2, 16)):
+        for j in range(8):
+            ready[j, 0:24], ready[j, 24:48] = waves(j, slot_rows(slots, start + j))
     for i in range(4):
         v0[pl.ds(i, N_FFT, stride=4), :] = slots[:, 8 + i * 8, :]
     both = jnp.concatenate([v0[...], first[...]], 0)
@@ -447,24 +451,40 @@
                 out[v, g * 4 + i : g * 4 + i + 1, :] = found[v][:, i * 128 : i * 128 + 128]
 
 
-def early(slots, first):
+def early(slots, first, steps):
     return pl.pallas_call(
         early_body,
-        out_shape=jax.ShapeDtypeStruct((2, 128, 128), F32),
+        out_shape=(
+            jax.ShapeDtypeStruct((2, 128, 128), F32),
+            jax.ShapeDtypeStruct((8, 48, ROWS), F32),
+            jax.ShapeDtypeStruct((8, 48, ROWS), F32),
+        ),
         scratch_shapes=[pltpu.VMEM((128, 128), F32)],
         compiler_params=pltpu.CompilerParams(vmem_limit_bytes=SOME),
         cost_estimate=pl.CostEstimate(flops=2_000_000_000, bytes_accessed=1_000_000, transcendentals=0),
         name="early",
-    )(slots, first)
-
-
-def ml_group(i, slots, charges, grid, perm, steps, store):
+    )(slots, first, steps)
+
+
+def phases(steps):
     f, s = my_place()
-    upper = lax.broadcasted_iota(jnp.int32, (8, 1), 0) < 4
     block = (lax.broadcasted_iota(jnp.int32, (1, ROWS), 1) // OWN * YL).astype(F32)
     local = lax.broadcasted_iota(jnp.int32, (24, 1), 0)
     freq = jnp.where(local < 8, s * KX + local, f * KY + local - 8)
     freq = jnp.where(local < 16, freq, jnp.where(local < 20, s * KX + local - 8, f * KY + local - 12)).astype(F32)
+
+    def waves(_, rows):
+        return site_waves(freq, (rows[2:3], rows[3:4] + block), (rows[5:6], rows[6:7]), steps[...])
+
+    return waves
+
+
+def kept(ref):
+    return lambda j, _: (ref[j, 0:24], ref[j, 24:48])
+
+
+def ml_group(i, slots, charges, grid, perm, waves, store):
+    upper = lax.broadcasted_iota(jnp.int32, (8, 1), 0) < 4
     at = pl.multiple_of(i * 32, 32)
     charge = [charges[v, pl.ds(at, 32), :] for v in range(2)]
     high, low = split(grid[pl.ds(i * 8, 8)].reshape(128, 384))
@@ -475,7 +495,7 @@
         placed_z = placed(16, rows[4:5].astype(jnp.int32), spline(rows[7:8]))
         both = [placed_z * lanes(charge[v][j * 4 : j * 4 + 4]) for v in range(2)]
         z_high, z_low = split(jnp.concatenate(both, 0))
-        re, im = site_waves(freq, (rows[2:3], rows[3:4] + block), (rows[5:6], rows[6:7]), steps[...])
+        re, im = waves(j, rows)
         x_re, x_im = re[0:8], im[0:8]
         y_re = [re[8 + k : 9 + k] for k in range(8)] + [re[20 + k : 21 + k] for k in range(4)]
         y_im = [im[8 + k : 9 + k] for k in range(8)] + [im[20 + k : 21 + k] for k in range(4)]
@@ -498,7 +518,7 @@
         store(g, total[:16] + base[j], total[16:])
 
 
-def solve_body(slots, before, first, grid, perm, steps, out, rest, charges, v2, late):
+def solve_body(slots, before, first, grid, perm, steps, ready, out, rest, charges, v2, late):
     f, s = my_place()
     for i in range(4):
         pieces = [grid[:, i * 4 + j, 352:384] for j in range(4)]
@@ -541,11 +561,8 @@
         out[g, 0:16] = base
         out[g, 16:32] = last
 
-    def group(i, carry):
-        ml_group(i, slots, charges, grid, perm, steps, store)
-        return carry
-
-    lax.fori_loop(0, 2, group, 0)
+    ml_group(0, slots, charges, grid, perm, kept(ready), store)
+    ml_group(1, slots, charges, grid, perm, phases(steps), store)
 
 
 def solve(*operands):
@@ -568,7 +585,7 @@
     return guarded(rest[3:4], m5 - rest[2:3], m5)[:, 0:1]
 
 
-def join_body(slots, charges, grid, perm, steps, early_half, quads, rest, out, out_q):
+def join_body(slots, charges, grid, perm, steps, ready, early_half, quads, rest, out, out_q):
     step = last_step(quads, rest)
     half = N_FFT // 2
     out[0:half] = early_half[:, 0:16] + step[None] * early_half[:, 16:32]
@@ -577,11 +594,8 @@
     def store(g, base, last):
         out[g] = base + step * last
 
-    def group(i, carry):
-        ml_group(i, slots, charges, grid, perm, steps, store)
-        return carry
-
-    lax.fori_loop(2, 4, group, 0)
+    ml_group(2, slots, charges, grid, perm, kept(ready), store)
+    ml_group(3, slots, charges, grid, perm, phases(steps), store)
 
 
 def join(*operands):
@@ -658,10 +672,10 @@
     steps_x = lax.dynamic_index_in_dim(jnp.asarray(step_table(N_SLAB)), s, 0, False)
     steps_y = lax.dynamic_index_in_dim(jnp.asarray(step_table(N_FFT)), f, 0, False)
     steps = jnp.concatenate([steps_x[:8], steps_y[:8], steps_x[8:], steps_y[8:]], 0)
-    before = early(got_1, first_full)
+    before, ready_0, ready_2 = early(got_1, first_full, steps)
     perm = jnp.asarray(perm_z())
-    half, rest, charges = solve(got_1, before, first_full, got_3, perm, steps)
-    total, charge = join(got_1, charges, got_3, perm, steps, half, quads, rest)
+    half, rest, charges = solve(got_1, before, first_full, got_3, perm, steps, ready_0)
+    total, charge = join(got_1, charges, got_3, perm, steps, ready_2, half, quads, rest)
     z_waves = jnp.asarray(np.stack([t for part in z_tables() for t in two_parts(part)]))
     struct_re, struct_im = along_z(total, z_waves)
     return (charge.reshape(OWN), struct_re, struct_im)

time: 135 us -> 138 us (1.022)
  local copies, waits for them, and re-layouts: 3.56 us -> 8.73 us
  waiting for transfers between devices: 18.4 us -> 15.9 us
    unnamed x20 -> x32, local copies, waits for them, and re-layouts: 1.72 us -> 6.89 us
    all_to_all x4, waiting for transfers between devices: 18.4 us -> 15.9 us  [swap(): return lax.all_to_all(value, axis, 0, 0, tiled=True)]
    pallas_call x1, Pallas kernels: 4.53 us -> 6.37 us  [early(): pl.pallas_call(early_body, out_shape=(jax.ShapeDtypeStruct((2, 128, 128),...]
where the time goes in v9:
time: 138 us; the launch traced here: 137 us
  Pallas kernels  47.2 us (34%)
  starting transfers between devices  31.9 us (23%)
  blocking collectives  31.9 us (23%)
  waiting for transfers between devices  15.9 us (12%)
  local copies, waits for them, and re-layouts  8.73 us (6%)
    all_to_all x4, starting transfers between devices, swap(): return lax.all_to_all(value, axis, 0, 0, tiled=True)  31.9 us
    all_to_all x1, blocking collectives, swap(): return lax.all_to_all(value, axis, 0, 0, tiled=True)  31.9 us
    all_to_all x4, waiting for transfers between devices, swap(): return lax.all_to_all(value, axis, 0, 0, tiled=True)  15.9 us
    pallas_call x1, Pallas kernels, spread(): pl.pallas_call(spread_body, grid=(SITES // CHUNK,), in_specs=[pl.BlockSpe...  15.3 us
    pallas_call x1, Pallas kernels, solve(): pl.pallas_call(solve_body, out_shape=(jax.ShapeDtypeStruct((N_FFT // 2, 3...  7.2 us
    unnamed x32, local copies, waits for them, and re-layouts  6.89 us
    pallas_call x1, Pallas kernels, early(): pl.pallas_call(early_body, out_shape=(jax.ShapeDtypeStruct((2, 128, 128),...  6.37 us
    pallas_call x1, Pallas kernels, couple(): pl.pallas_call(couple_body, out_shape=jax.ShapeDtypeStruct((ROWS, COLS),...  5.27 us
  transfers between devices with their start and end apart: 4, of which 3 were waited for; matrix products, arithmetic and copies ran while one was open for 1% of the time, Pallas kernels for 25%

profile of v9, /device:TPU:1, one launch (start us, length us, event | category | flops | bytes accessed | tf_op | source)
XLA Modules:
  0.0 136.9 jit_solution(17606984046788017404)
XLA Ops:
  0.6 1.8 %pack.1 = (f32[16,8,128]{2,1,0:T(8,128)}, f32[8,1536]{1,0:T(8,128)}) custom-call(f32[1,32]{1,0:T(1,128)} %bitcast.25, s32[1,32]{1,0:T(1,128)} %bitcast.26, s32[3,32]{1,0:T(4,128)} %cell.2, f32[3,32]{1,0:T(4,128)} %frac.2, f32[1,32]{1,0:T(1,128)} %bitcast.27, f32[3,16384]{1,0:T(4,128)} %pos.1, f32[1,16384]{1,0:T(1,128)} %bitcast.22), custom_call_target="tpu_custom_call" | custom-call | tf_op jit(solution)/shard_map/pack/pallas_call | solution.py:227
  2.4 10.2 %all-to-all-start = ((f32[16,8,128]{2,1,0:T(8,128)}), f32[16,8,128]{2,1,0:T(8,128)S(1)}, u32[]{:S(2)}, u32[]{:S(2)}) async-start(f32[16,8,128]{2,1,0:T(8,128)} %get-tuple-element.15), calls=%async_computation | async-start | bytes 131072 | tf_op jit(solution)/shard_map/all_to_all | solution.py:637
  12.6 0.8 copy-done.1
  13.4 5.3 %couple.1.matrix = f32[512,1024]{1,0:T(8,128)S(1)} custom-call(f32[8,1536]{1,0:T(8,128)S(1)} %copy-done.1), custom_call_target="tpu_custom_call" | custom-call | flops 100000000 | bytes 2000000 | tf_op jit(solution)/shard_map/couple/pallas_call | solution.py:295
  18.7 1.8 %all-to-all-done.got = f32[16,8,128]{2,1,0:T(8,128)S(1)} async-done(((f32[16,8,128]{2,1,0:T(8,128)}), f32[16,8,128]{2,1,0:T(8,128)S(1)}, u32[]{:S(2)}, u32[]{:S(2)}) %all-to-all-start) | async-done | bytes 65568 | tf_op jit(solution)/shard_map/all_to_all | solution.py:637
  20.4 1.3 first_product.1
  21.7 11.3 %all-to-all-start.1 = ((f32[32,40,128]{2,1,0:T(8,128)}), f32[32,40,128]{2,1,0:T(8,128)S(1)}, u32[]{:S(2)}, u32[]{:S(2)}) async-start(f32[32,40,128]{2,1,0:T(8,128)} %first_product.1), calls=%async_computation.1 | async-start | bytes 1310720 | tf_op jit(solution)/shard_map/all_to_all | solution.py:637
  33.0 15.3 %spread.1 = f32[16,32,384]{2,1,0:T(8,128)} custom-call(f32[1,6144]{1,0:T(1,128)} %bitcast.28, f32[3,6144]{1,0:T(4,128)} %frac.3, s32[3,6144]{1,0:T(4,128)} %cell.3, bf16[2,392,384]{2,1,0:T(8,128)(2,1)} %constant.42.clone.waves_from), custom_call_target="tpu_custom_call" | custom-call | flops 8000000000 | bytes 2000000 | tf_op jit(solution)/shard_map/spread/pallas_call | solution.py:175
  48.3 1.5 %all-to-all-done.1.slots = f32[32,40,128]{2,1,0:T(8,128)S(1)} async-done(((f32[32,40,128]{2,1,0:T(8,128)}), f32[32,40,128]{2,1,0:T(8,128)S(1)}, u32[]{:S(2)}, u32[]{:S(2)}) %all-to-all-start.1) | async-done | bytes 655392 | tf_op jit(solution)/shard_map/all_to_all | solution.py:637
  50.2 31.9 %all_to_all.25.grid = f32[16,32,384]{2,1,0:T(8,128)S(1)} all-to-all(f32[16,32,384]{2,1,0:T(8,128)S(1)} %pad_maximum_fusion), channel_id=1, replica_groups=mesh['fft'=32,'slab'=16] {'slab'}, dimensions={0} | all-to-all | bytes 1572864 | tf_op jit(solution)/shard_map/all_to_all | solution.py:637
  82.1 2.4 %along_y.1 = f32[32,16,384]{2,1,0:T(8,128)S(1)} custom-call(f32[16,32,384]{2,1,0:T(8,128)S(1)} %all_to_all.25.grid, f32[512,1024]{1,0:T(8,128)S(1)} %couple.1.matrix, bf16[384,384]{1,0:T(8,128)(2,1)S(1)} %copy-done.8, bf16[512,768]{1,0:T(8,128)(2,1)S(1)} %copy-done.6, bf16[512,768]{1,0:T(8,128)(2,1)S(1)} %copy-done.5, bf16[512,768]{1,0:T(8,128)(2,1)S(1)} %copy-done.4, ...), custom_call_target="tpu_custom_call" | custom-call | flops 4000000000 | bytes 5000000 | tf_op jit(solution)/shard_map/along_y/pallas_call | solution.py:354
  84.5 0.9 copy-done
  85.4 5.6 %all-to-all-start.3 = ((f32[32,16,384]{2,1,0:T(8,128)}), f32[32,16,384]{2,1,0:T(8,128)S(1)}, u32[]{:S(2)}, u32[]{:S(2)}) async-start(f32[32,16,384]{2,1,0:T(8,128)} %copy-done), calls=%async_computation.3 | async-start | bytes 1572864 | tf_op jit(solution)/shard_map/all_to_all | solution.py:637
  92.9 6.4 %early.1 = (f32[2,128,128]{2,1,0:T(8,128)S(1)}, f32[8,48,512]{2,1,0:T(8,128)S(1)}, f32[8,48,512]{2,1,0:T(8,128)S(1)}) custom-call(f32[32,40,128]{2,1,0:T(8,128)S(1)} %all-to-all-done.1.slots, f32[128,128]{1,0:T(8,128)S(1)} %reshape.47.first, f32[24,8]{1,0:T(8,128)S(1)} %pad_maximum_fusion.2.steps), custom_call_target="tpu_custom_call" | custom-call | flops 2000000000 | bytes 1000000 | tf_op jit(solution)/shard_map/early/pallas_call | solution.py:455
  99.9 12.7 %all-to-all-done.3.grid.got = f32[32,16,384]{2,1,0:T(8,128)S(1)} async-done(((f32[32,16,384]{2,1,0:T(8,128)}), f32[32,16,384]{2,1,0:T(8,128)S(1)}, u32[]{:S(2)}, u32[]{:S(2)}) %all-to-all-start.3) | async-done | bytes 786464 | tf_op jit(solution)/shard_map/all_to_all | solution.py:637
  112.6 1.0 quad_sum.1
  113.6 4.9 %all-to-all-start.4 = ((f32[16,8,128]{2,1,0:T(8,128)}), f32[16,8,128]{2,1,0:T(8,128)S(1)}, u32[]{:S(2)}, u32[]{:S(2)}) async-start(f32[16,8,128]{2,1,0:T(8,128)} %quad_sum.1), calls=%async_computation.4 | async-start | bytes 131072 | tf_op jit(solution)/shard_map/all_to_all | solution.py:637
  118.5 0.9 copy-done.12
  119.4 7.2 %solve.1 = (f32[16,32,288]{2,1,0:T(8,128)S(1)}, f32[8,128]{1,0:T(8,128)S(1)}, f32[2,128,128]{2,1,0:T(8,128)S(1)}) custom-call(f32[32,40,128]{2,1,0:T(8,128)S(1)} %all-to-all-done.1.slots, f32[2,128,128]{2,1,0:T(8,128)S(1)} %copy-done.12, f32[128,128]{1,0:T(8,128)S(1)} %reshape.47.first, f32[32,16,384]{2,1,0:T(8,128)S(1)} %all-to-all-done.3.grid.got, ...), custom_call_target="tpu_custom_call" | custom-call | flops 5000000000 | bytes 4000000 | tf_op jit(solution)/shard_map/solve/pallas_call | solution.py:569
  126.6 0.9 copy-done.9
  128.2 1.1 copy-done.10
  129.3 0.9 copy-done.14
  130.2 4.7 %join.1 = (f32[32,16,288]{2,1,0:T(8,128)S(1)}, f32[1,32]{1,0:T(1,128)}) custom-call(f32[32,40,128]{2,1,0:T(8,128)S(1)} %all-to-all-done.1.slots, f32[2,128,128]{2,1,0:T(8,128)S(1)} %copy-done.14, f32[32,16,384]{2,1,0:T(8,128)S(1)} %all-to-all-done.3.grid.got, bf16[384,288]{1,0:T(8,128)(2,1)S(1)} %copy-done.7, f32[24,8]{1,0:T(8,128)S(1)} %pad_maximum_fusion.2.steps, ...), custom_call_target="tpu_custom_call" | custom-call | flops 4000000000 | bytes 4000000 | tf_op jit(solution)/shard_map/join/pallas_call | solution.py:602
  135.0 1.9 %along_z.1 = (f32[12,12,384]{2,1,0:T(8,128)}, f32[12,12,384]{2,1,0:T(8,128)}) custom-call(f32[32,16,288]{2,1,0:T(8,128)S(1)} %get-tuple-element.24.grid, bf16[4,512,384]{2,1,0:T(8,128)(2,1)S(1)} %copy-done.2), custom_call_target="tpu_custom_call" | custom-call | flops 3000000000 | bytes 5000000 | tf_op jit(solution)/shard_map/along_z/pallas_call | solution.py:627
  (41 shorter events, 3.6 us)
Async XLA Ops:
  2.4 18.0 %all-to-all-start = ((f32[16,8,128]{2,1,0:T(8,128)}), f32[16,8,128]{2,1,0:T(8,128)S(1)}, u32[]{:S(2)}, u32[]{:S(2)}) async-start(f32[16,8,128]{2,1,0:T(8,128)} %get-tuple-element.15), calls=%async_computation | async-start | bytes 131072 | tf_op jit(solution)/shard_map/all_to_all | solution.py:637
  12.6 0.8 copy-start.1
  21.7 28.1 %all-to-all-start.1 = ((f32[32,40,128]{2,1,0:T(8,128)}), f32[32,40,128]{2,1,0:T(8,128)S(1)}, u32[]{:S(2)}, u32[]{:S(2)}) async-start(f32[32,40,128]{2,1,0:T(8,128)} %first_product.1), calls=%async_computation.1 | async-start | bytes 1310720 | tf_op jit(solution)/shard_map/all_to_all | solution.py:637
  48.3 1.8 %copy-start.15 = (f32[16,32,384]{2,1,0:T(8,128)S(1)}, f32[16,32,384]{2,1,0:T(8,128)}, u32[]{:S(2)}) copy-start(f32[16,32,384]{2,1,0:T(8,128)} %spread.1) | copy-start | bytes 2359300
  49.8 32.3 %copy-start.8 = (bf16[384,384]{1,0:T(8,128)(2,1)S(1)}, bf16[384,384]{1,0:T(8,128)(2,1)}, u32[]{:S(2)}) copy-start(bf16[384,384]{1,0:T(8,128)(2,1)} %constant.47.clone.perm) | copy-start | bytes 884740
  50.0 32.0 %copy-start.3 = (bf16[512,768]{1,0:T(8,128)(2,1)S(1)}, bf16[512,768]{1,0:T(8,128)(2,1)}, u32[]{:S(2)}) copy-start(bf16[512,768]{1,0:T(8,128)(2,1)} %constant.46.clone.ail) | copy-start | bytes 2359300
  50.0 32.0 %copy-start.4 = (bf16[512,768]{1,0:T(8,128)(2,1)S(1)}, bf16[512,768]{1,0:T(8,128)(2,1)}, u32[]{:S(2)}) copy-start(bf16[512,768]{1,0:T(8,128)(2,1)} %constant.45.clone.aih) | copy-start | bytes 2359300
  50.0 32.0 %copy-start.5 = (bf16[512,768]{1,0:T(8,128)(2,1)S(1)}, bf16[512,768]{1,0:T(8,128)(2,1)}, u32[]{:S(2)}) copy-start(bf16[512,768]{1,0:T(8,128)(2,1)} %constant.44.clone.arl) | copy-start | bytes 2359300
  50.1 32.0 %copy-start.6 = (bf16[512,768]{1,0:T(8,128)(2,1)S(1)}, bf16[512,768]{1,0:T(8,128)(2,1)}, u32[]{:S(2)}) copy-start(bf16[512,768]{1,0:T(8,128)(2,1)} %constant.43.clone.arh) | copy-start | bytes 2359300
  84.5 0.9 copy-start
  85.4 27.2 %all-to-all-start.3 = ((f32[32,16,384]{2,1,0:T(8,128)}), f32[32,16,384]{2,1,0:T(8,128)S(1)}, u32[]{:S(2)}, u32[]{:S(2)}) async-start(f32[32,16,384]{2,1,0:T(8,128)} %copy-done), calls=%async_computation.3 | async-start | bytes 1572864 | tf_op jit(solution)/shard_map/all_to_all | solution.py:637
  92.9 25.6 %copy-start.7 = (bf16[384,288]{1,0:T(8,128)(2,1)S(1)}, bf16[384,288]{1,0:T(8,128)(2,1)}, u32[]{:S(2)}) copy-start(bf16[384,288]{1,0:T(8,128)(2,1)} %constant.50.clone.perm) | copy-start | bytes 663556
  99.3 0.7 copy-start.11
  113.6 14.6 %all-to-all-start.4 = ((f32[16,8,128]{2,1,0:T(8,128)}), f32[16,8,128]{2,1,0:T(8,128)S(1)}, u32[]{:S(2)}, u32[]{:S(2)}) async-start(f32[16,8,128]{2,1,0:T(8,128)} %quad_sum.1), calls=%async_computation.4 | async-start | bytes 131072 | tf_op jit(solution)/shard_map/all_to_all | solution.py:637
  118.5 0.9 copy-start.12
  126.6 0.9 copy-start.9
  127.5 0.7 copy-start.13
  128.2 1.1 copy-start.10
  129.3 0.9 copy-start.14
  130.2 4.7 %copy-start.2 = (bf16[4,512,384]{2,1,0:T(8,128)(2,1)S(1)}, bf16[4,512,384]{2,1,0:T(8,128)(2,1)}, u32[]{:S(2)}) copy-start(bf16[4,512,384]{2,1,0:T(8,128)(2,1)} %constant.51.clone.waves) | copy-start | bytes 4718596

commit v10 on v9

--- a/solution.py
+++ b/solution.py
@@ -198,14 +198,17 @@
     return jnp.concatenate([tiles[i : i + 1] for i in range(tiles.shape[0])], 1)
 
 
-def pack_body(drive, atom, cell, frac, hard, pos, width, out, near, picked):
-    f, s = my_place()
+def pack_body(drive, atom, cell, frac, out):
     out[...] = jnp.zeros_like(out)
     for i in range(N_SLAB):
         out[i, 0:1, 0:OWN] = -drive[...]
         out[i, 1:2, 0:OWN] = atom[...].astype(F32)
         out[i, 2:5, 0:OWN] = cell[...].astype(F32)
         out[i, 5:8, 0:OWN] = frac[...]
+
+
+def near_body(hard, pos, width, near, picked):
+    f, s = my_place()
     for j in range(N_FFT):
         at = pl.multiple_of(j * ROWS + (s >> 2) * 128, 128)
         picked[j, 0:3, :] = pos[:, pl.ds(at, 128)]
@@ -223,25 +226,23 @@
     near[4:5, COLS : COLS + OWN] = hard[...]
 
 
-def pack(drive, atom, cell, frac, hard, pos, width):
+def pack(drive, atom, cell, frac):
     return pl.pallas_call(
         pack_body,
-        out_shape=(
-            jax.ShapeDtypeStruct((N_SLAB, 8, 128), F32),
-            jax.ShapeDtypeStruct((8, COLS + ROWS), F32),
-        ),
+        out_shape=jax.ShapeDtypeStruct((N_SLAB, 8, 128), F32),
+        compiler_params=pltpu.CompilerParams(vmem_limit_bytes=MOST),
+        name="pack",
+    )(drive.reshape(1, OWN), atom.reshape(1, OWN), cell, frac)
+
+
+def near_atoms(hard, pos, width):
+    return pl.pallas_call(
+        near_body,
+        out_shape=jax.ShapeDtypeStruct((8, COLS + ROWS), F32),
         scratch_shapes=[pltpu.VMEM((N_FFT, 8, 128), F32)],
         compiler_params=pltpu.CompilerParams(vmem_limit_bytes=MOST),
-        name="pack",
-    )(
-        drive.reshape(1, OWN),
-        atom.reshape(1, OWN),
-        cell,
-        frac,
-        hard.reshape(1, OWN),
-        pos,
-        width.reshape(1, ATOMS),
-    )
+        name="near_atoms",
+    )(hard.reshape(1, OWN), pos, width.reshape(1, ATOMS))
 
 
 def erf_ratio(value):
@@ -419,7 +420,7 @@
 
 
 def guarded(value, pivot, scale):
-    good = pivot > 1e-6 * scale
+    good = jnp.abs(pivot) > 1e-6 * jnp.abs(scale)
     return jnp.where(good, value / jnp.where(good, pivot, 1.0), 0.0)
 
 
@@ -434,11 +435,10 @@
     ]
 
 
-def early_body(slots, first, steps, out, ready_0, ready_2, v0):
+def early_body(slots, first, steps, out, ready, v0):
     waves = phases(steps)
-    for ready, start in ((ready_0, 0), (ready_2, 16)):
-        for j in range(8):
-            ready[j, 0:24], ready[j, 24:48] = waves(j, slot_rows(slots, start + j))
+    for j in range(8):
+        ready[j, 0:24], ready[j, 24:48] = waves(j, slot_rows(slots, j))
     for i in range(4):
         v0[pl.ds(i, N_FFT, stride=4), :] = slots[:, 8 + i * 8, :]
     both = jnp.concatenate([v0[...], first[...]], 0)
@@ -456,7 +456,6 @@
         early_body,
         out_shape=(
             jax.ShapeDtypeStruct((2, 128, 128), F32),
-            jax.ShapeDtypeStruct((8, 48, ROWS), F32),
             jax.ShapeDtypeStruct((8, 48, ROWS), F32),
         ),
         scratch_shapes=[pltpu.VMEM((128, 128), F32)],
@@ -585,7 +584,7 @@
     return guarded(rest[3:4], m5 - rest[2:3], m5)[:, 0:1]
 
 
-def join_body(slots, charges, grid, perm, steps, ready, early_half, quads, rest, out, out_q):
+def join_body(slots, charges, grid, perm, steps, early_half, quads, rest, out, out_q):
     step = last_step(quads, rest)
     half = N_FFT // 2
     out[0:half] = early_half[:, 0:16] + step[None] * early_half[:, 16:32]
@@ -594,8 +593,11 @@
     def store(g, base, last):
         out[g] = base + step * last
 
-    ml_group(2, slots, charges, grid, perm, kept(ready), store)
-    ml_group(3, slots, charges, grid, perm, phases(steps), store)
+    def group(i, carry):
+        ml_group(i, slots, charges, grid, perm, phases(steps), store)
+        return carry
+
+    lax.fori_loop(2, 4, group, 0)
 
 
 def join(*operands):
@@ -652,9 +654,8 @@
     f = lax.axis_index("fft")
     s = lax.axis_index("slab")
 
-    sent, near = pack(ml_drive, slot_atom, slot_cell, slot_frac, ml_hard, ml_pos, ml_width)
-    got = swap(sent, "slab")
-    matrix = couple(near)
+    got = swap(pack(ml_drive, slot_atom, slot_cell, slot_frac), "slab")
+    matrix = couple(near_atoms(ml_hard, ml_pos, ml_width))
     got_1 = swap(first_product(got, matrix), "fft")
     mm = spread(mm_charge, mm_frac, mm_cell, jnp.asarray(np.stack(two_parts(x_table()))))
     first_cols = jnp.sum(got_1[:, :8], 0)
@@ -672,10 +673,10 @@
     steps_x = lax.dynamic_index_in_dim(jnp.asarray(step_table(N_SLAB)), s, 0, False)
     steps_y = lax.dynamic_index_in_dim(jnp.asarray(step_table(N_FFT)), f, 0, False)
     steps = jnp.concatenate([steps_x[:8], steps_y[:8], steps_x[8:], steps_y[8:]], 0)
-    before, ready_0, ready_2 = early(got_1, first_full, steps)
+    before, ready = early(got_1, first_full, steps)
     perm = jnp.asarray(perm_z())
-    half, rest, charges = solve(got_1, before, first_full, got_3, perm, steps, ready_0)
-    total, charge = join(got_1, charges, got_3, perm, steps, ready_2, half, quads, rest)
+    half, rest, charges = solve(got_1, before, first_full, got_3, perm, steps, ready)
+    total, charge = join(got_1, charges, got_3, perm, steps, half, quads, rest)
     z_waves = jnp.asarray(np.stack([t for part in z_tables() for t in two_parts(part)]))
     struct_re, struct_im = along_z(total, z_waves)
     return (charge.reshape(OWN), struct_re, struct_im)

time: 138 us -> 138 us (level)
  local copies, waits for them, and re-layouts: 8.73 us -> 6.71 us
  blocking collectives: 31.9 us -> 33.6 us
    unnamed x32 -> x28, local copies, waits for them, and re-layouts: 6.89 us -> 4.87 us
    all_to_all x1, blocking collectives: 31.9 us -> 33.6 us  [swap(): return lax.all_to_all(value, axis, 0, 0, tiled=True)]
    pallas_call x1 -> x2, Pallas kernels: 1.78 us -> 3.1 us  [the longest x1 1.72 us: near_atoms(): pl.pallas_call(near_body, out_shape=jax.ShapeDtypeStruct((8, COLS + ROWS)...]
  transfers between devices with their start and end apart: 4 -> 4, of which waited for: 3 -> 2; matrix products, arithmetic and copies ran while one was open for 1% -> 1% of each run, Pallas kernels for 25% -> 25%
where the time goes in v10:
time: 138 us; the launch traced here: 137 us
  Pallas kernels  48.4 us (35%)
  blocking collectives  33.6 us (24%)
  starting transfers between devices  31.9 us (23%)
  waiting for transfers between devices  15.2 us (11%)
  local copies, waits for them, and re-layouts  6.71 us (5%)
    all_to_all x1, blocking collectives, swap(): return lax.all_to_all(value, axis, 0, 0, tiled=True)  33.6 us
    all_to_all x4, starting transfers between devices, swap(): return lax.all_to_all(value, axis, 0, 0, tiled=True)  31.9 us
    pallas_call x1, Pallas kernels, spread(): pl.pallas_call(spread_body, grid=(SITES // CHUNK,), in_specs=[pl.BlockSpe...  15.3 us
    all_to_all x4, waiting for transfers between devices, swap(): return lax.all_to_all(value, axis, 0, 0, tiled=True)  15.2 us
    pallas_call x1, Pallas kernels, solve(): pl.pallas_call(solve_body, out_shape=(jax.ShapeDtypeStruct((N_FFT // 2, 3...  7.25 us
    pallas_call x1, Pallas kernels, join(): pl.pallas_call(join_body, out_shape=(jax.ShapeDtypeStruct((N_FFT, 16, PAI...  5.51 us
    pallas_call x1, Pallas kernels, early(): pl.pallas_call(early_body, out_shape=(jax.ShapeDtypeStruct((2, 128, 128),...  5.44 us
    pallas_call x1, Pallas kernels, couple(): pl.pallas_call(couple_body, out_shape=jax.ShapeDtypeStruct((ROWS, COLS),...  5.27 us
  transfers between devices with their start and end apart: 4, of which 2 were waited for; matrix products, arithmetic and copies ran while one was open for 1% of the time, Pallas kernels for 25%

profile of v10, /device:TPU:1, one launch (start us, length us, event | category | flops | bytes accessed | tf_op | source)
XLA Modules:
  0.0 137.0 jit_solution(18071960531812317074)
XLA Ops:
  0.6 1.4 %pack.1 = f32[16,8,128]{2,1,0:T(8,128)} custom-call(f32[1,32]{1,0:T(1,128)} %bitcast.25, s32[1,32]{1,0:T(1,128)} %bitcast.26, s32[3,32]{1,0:T(4,128)} %cell.2, f32[3,32]{1,0:T(4,128)} %frac.2), custom_call_target="tpu_custom_call" | custom-call | tf_op jit(solution)/shard_map/pack/pallas_call | solution.py:230
  2.0 10.2 %all-to-all-start = ((f32[16,8,128]{2,1,0:T(8,128)}), f32[16,8,128]{2,1,0:T(8,128)S(1)}, u32[]{:S(2)}, u32[]{:S(2)}) async-start(f32[16,8,128]{2,1,0:T(8,128)} %pack.1), calls=%async_computation | async-start | bytes 131072 | tf_op jit(solution)/shard_map/all_to_all | solution.py:639
  12.2 1.7 %near_atoms.1.near = f32[8,1536]{1,0:T(8,128)} custom-call(f32[1,32]{1,0:T(1,128)} %bitcast.27, f32[3,16384]{1,0:T(4,128)} %pos.1, f32[1,16384]{1,0:T(1,128)} %bitcast.22), custom_call_target="tpu_custom_call" | custom-call | tf_op jit(solution)/shard_map/near_atoms/pallas_call | solution.py:239
  13.9 0.8 copy-done.1
  14.7 5.3 %couple.1.matrix = f32[512,1024]{1,0:T(8,128)S(1)} custom-call(f32[8,1536]{1,0:T(8,128)S(1)} %copy-done.1), custom_call_target="tpu_custom_call" | custom-call | flops 100000000 | bytes 2000000 | tf_op jit(solution)/shard_map/couple/pallas_call | solution.py:296
  20.0 1.3 first_product.1
  21.3 11.3 %all-to-all-start.1 = ((f32[32,40,128]{2,1,0:T(8,128)}), f32[32,40,128]{2,1,0:T(8,128)S(1)}, u32[]{:S(2)}, u32[]{:S(2)}) async-start(f32[32,40,128]{2,1,0:T(8,128)} %first_product.1), calls=%async_computation.1 | async-start | bytes 1310720 | tf_op jit(solution)/shard_map/all_to_all | solution.py:639
  32.6 15.3 %spread.1 = f32[16,32,384]{2,1,0:T(8,128)} custom-call(f32[1,6144]{1,0:T(1,128)} %bitcast.28, f32[3,6144]{1,0:T(4,128)} %frac.3, s32[3,6144]{1,0:T(4,128)} %cell.3, bf16[2,392,384]{2,1,0:T(8,128)(2,1)} %constant.42.clone.waves_from), custom_call_target="tpu_custom_call" | custom-call | flops 8000000000 | bytes 2000000 | tf_op jit(solution)/shard_map/spread/pallas_call | solution.py:175
  47.9 1.5 %all-to-all-done.1.slots = f32[32,40,128]{2,1,0:T(8,128)S(1)} async-done(((f32[32,40,128]{2,1,0:T(8,128)}), f32[32,40,128]{2,1,0:T(8,128)S(1)}, u32[]{:S(2)}, u32[]{:S(2)}) %all-to-all-start.1) | async-done | bytes 655392 | tf_op jit(solution)/shard_map/all_to_all | solution.py:639
  49.8 33.6 %all_to_all.25.grid = f32[16,32,384]{2,1,0:T(8,128)S(1)} all-to-all(f32[16,32,384]{2,1,0:T(8,128)S(1)} %pad_maximum_fusion), channel_id=1, replica_groups=mesh['fft'=32,'slab'=16] {'slab'}, dimensions={0} | all-to-all | bytes 1572864 | tf_op jit(solution)/shard_map/all_to_all | solution.py:639
  83.4 2.4 %along_y.1 = f32[32,16,384]{2,1,0:T(8,128)S(1)} custom-call(f32[16,32,384]{2,1,0:T(8,128)S(1)} %all_to_all.25.grid, f32[512,1024]{1,0:T(8,128)S(1)} %couple.1.matrix, bf16[384,384]{1,0:T(8,128)(2,1)S(1)} %copy-done.8, bf16[512,768]{1,0:T(8,128)(2,1)S(1)} %copy-done.6, bf16[512,768]{1,0:T(8,128)(2,1)S(1)} %copy-done.5, bf16[512,768]{1,0:T(8,128)(2,1)S(1)} %copy-done.4, ...), custom_call_target="tpu_custom_call" | custom-call | flops 4000000000 | bytes 5000000 | tf_op jit(solution)/shard_map/along_y/pallas_call | solution.py:355
  85.9 0.9 copy-done
  86.7 5.6 %all-to-all-start.3 = ((f32[32,16,384]{2,1,0:T(8,128)}), f32[32,16,384]{2,1,0:T(8,128)S(1)}, u32[]{:S(2)}, u32[]{:S(2)}) async-start(f32[32,16,384]{2,1,0:T(8,128)} %copy-done), calls=%async_computation.3 | async-start | bytes 1572864 | tf_op jit(solution)/shard_map/all_to_all | solution.py:639
  92.3 0.7 dynamic-slice_bitcast_fusion.2
  93.0 0.7 dynamic-slice_bitcast_fusion
  94.2 5.4 %early.1 = (f32[2,128,128]{2,1,0:T(8,128)S(1)}, f32[8,48,512]{2,1,0:T(8,128)S(1)}) custom-call(f32[32,40,128]{2,1,0:T(8,128)S(1)} %all-to-all-done.1.slots, f32[128,128]{1,0:T(8,128)S(1)} %reshape.47.first, f32[24,8]{1,0:T(8,128)S(1)} %pad_maximum_fusion.2.steps), custom_call_target="tpu_custom_call" | custom-call | flops 2000000000 | bytes 1000000 | tf_op jit(solution)/shard_map/early/pallas_call | solution.py:455
  100.3 13.6 %all-to-all-done.3.grid.got = f32[32,16,384]{2,1,0:T(8,128)S(1)} async-done(((f32[32,16,384]{2,1,0:T(8,128)}), f32[32,16,384]{2,1,0:T(8,128)S(1)}, u32[]{:S(2)}, u32[]{:S(2)}) %all-to-all-start.3) | async-done | bytes 786464 | tf_op jit(solution)/shard_map/all_to_all | solution.py:639
  114.0 1.0 quad_sum.1
  114.9 4.9 %all-to-all-start.4 = ((f32[16,8,128]{2,1,0:T(8,128)}), f32[16,8,128]{2,1,0:T(8,128)S(1)}, u32[]{:S(2)}, u32[]{:S(2)}) async-start(f32[16,8,128]{2,1,0:T(8,128)} %quad_sum.1), calls=%async_computation.4 | async-start | bytes 131072 | tf_op jit(solution)/shard_map/all_to_all | solution.py:639
  119.8 0.9 copy-done.10
  120.7 7.3 %solve.1 = (f32[16,32,288]{2,1,0:T(8,128)S(1)}, f32[8,128]{1,0:T(8,128)S(1)}, f32[2,128,128]{2,1,0:T(8,128)S(1)}) custom-call(f32[32,40,128]{2,1,0:T(8,128)S(1)} %all-to-all-done.1.slots, f32[2,128,128]{2,1,0:T(8,128)S(1)} %copy-done.10, f32[128,128]{1,0:T(8,128)S(1)} %reshape.47.first, f32[32,16,384]{2,1,0:T(8,128)S(1)} %all-to-all-done.3.grid.got, ...), custom_call_target="tpu_custom_call" | custom-call | flops 5000000000 | bytes 4000000 | tf_op jit(solution)/shard_map/solve/pallas_call | solution.py:568
  128.7 0.9 copy-done.12
  129.6 5.5 %join.1 = (f32[32,16,288]{2,1,0:T(8,128)S(1)}, f32[1,32]{1,0:T(1,128)}) custom-call(f32[32,40,128]{2,1,0:T(8,128)S(1)} %all-to-all-done.1.slots, f32[2,128,128]{2,1,0:T(8,128)S(1)} %copy-done.12, f32[32,16,384]{2,1,0:T(8,128)S(1)} %all-to-all-done.3.grid.got, bf16[384,288]{1,0:T(8,128)(2,1)S(1)} %copy-done.7, f32[24,8]{1,0:T(8,128)S(1)} %pad_maximum_fusion.2.steps, ...), custom_call_target="tpu_custom_call" | custom-call | flops 4000000000 | bytes 4000000 | tf_op jit(solution)/shard_map/join/pallas_call | solution.py:604
  135.1 1.9 %along_z.1 = (f32[12,12,384]{2,1,0:T(8,128)}, f32[12,12,384]{2,1,0:T(8,128)}) custom-call(f32[32,16,288]{2,1,0:T(8,128)S(1)} %get-tuple-element.18.grid, bf16[4,512,384]{2,1,0:T(8,128)(2,1)S(1)} %copy-done.2), custom_call_target="tpu_custom_call" | custom-call | flops 3000000000 | bytes 5000000 | tf_op jit(solution)/shard_map/along_z/pallas_call | solution.py:629
  (38 shorter events, 2.2 us)
Async XLA Ops:
  2.0 18.0 %all-to-all-start = ((f32[16,8,128]{2,1,0:T(8,128)}), f32[16,8,128]{2,1,0:T(8,128)S(1)}, u32[]{:S(2)}, u32[]{:S(2)}) async-start(f32[16,8,128]{2,1,0:T(8,128)} %pack.1), calls=%async_computation | async-start | bytes 131072 | tf_op jit(solution)/shard_map/all_to_all | solution.py:639
  13.9 0.8 copy-start.1
  21.3 28.1 %all-to-all-start.1 = ((f32[32,40,128]{2,1,0:T(8,128)}), f32[32,40,128]{2,1,0:T(8,128)S(1)}, u32[]{:S(2)}, u32[]{:S(2)}) async-start(f32[32,40,128]{2,1,0:T(8,128)} %first_product.1), calls=%async_computation.1 | async-start | bytes 1310720 | tf_op jit(solution)/shard_map/all_to_all | solution.py:639
  47.9 1.8 %copy-start.13 = (f32[16,32,384]{2,1,0:T(8,128)S(1)}, f32[16,32,384]{2,1,0:T(8,128)}, u32[]{:S(2)}) copy-start(f32[16,32,384]{2,1,0:T(8,128)} %spread.1) | copy-start | bytes 2359300
  49.4 34.0 %copy-start.8 = (bf16[384,384]{1,0:T(8,128)(2,1)S(1)}, bf16[384,384]{1,0:T(8,128)(2,1)}, u32[]{:S(2)}) copy-start(bf16[384,384]{1,0:T(8,128)(2,1)} %constant.47.clone.perm) | copy-start | bytes 884740
  49.6 33.8 %copy-start.3 = (bf16[512,768]{1,0:T(8,128)(2,1)S(1)}, bf16[512,768]{1,0:T(8,128)(2,1)}, u32[]{:S(2)}) copy-start(bf16[512,768]{1,0:T(8,128)(2,1)} %constant.46.clone.ail) | copy-start | bytes 2359300
  49.7 33.8 %copy-start.4 = (bf16[512,768]{1,0:T(8,128)(2,1)S(1)}, bf16[512,768]{1,0:T(8,128)(2,1)}, u32[]{:S(2)}) copy-start(bf16[512,768]{1,0:T(8,128)(2,1)} %constant.45.clone.aih) | copy-start | bytes 2359300
  49.7 33.7 %copy-start.5 = (bf16[512,768]{1,0:T(8,128)(2,1)S(1)}, bf16[512,768]{1,0:T(8,128)(2,1)}, u32[]{:S(2)}) copy-start(bf16[512,768]{1,0:T(8,128)(2,1)} %constant.44.clone.arl) | copy-start | bytes 2359300
  49.7 33.7 %copy-start.6 = (bf16[512,768]{1,0:T(8,128)(2,1)S(1)}, bf16[512,768]{1,0:T(8,128)(2,1)}, u32[]{:S(2)}) copy-start(bf16[512,768]{1,0:T(8,128)(2,1)} %constant.43.clone.arh) | copy-start | bytes 2359300
  85.9 0.9 copy-start
  86.7 27.2 %all-to-all-start.3 = ((f32[32,16,384]{2,1,0:T(8,128)}), f32[32,16,384]{2,1,0:T(8,128)S(1)}, u32[]{:S(2)}, u32[]{:S(2)}) async-start(f32[32,16,384]{2,1,0:T(8,128)} %copy-done), calls=%async_computation.3 | async-start | bytes 1572864 | tf_op jit(solution)/shard_map/all_to_all | solution.py:639
  94.2 25.6 %copy-start.7 = (bf16[384,288]{1,0:T(8,128)(2,1)S(1)}, bf16[384,288]{1,0:T(8,128)(2,1)}, u32[]{:S(2)}) copy-start(bf16[384,288]{1,0:T(8,128)(2,1)} %constant.50.clone.perm) | copy-start | bytes 663556
  99.7 0.7 copy-start.9
  114.9 13.8 %all-to-all-start.4 = ((f32[16,8,128]{2,1,0:T(8,128)}), f32[16,8,128]{2,1,0:T(8,128)S(1)}, u32[]{:S(2)}, u32[]{:S(2)}) async-start(f32[16,8,128]{2,1,0:T(8,128)} %quad_sum.1), calls=%async_computation.4 | async-start | bytes 131072 | tf_op jit(solution)/shard_map/all_to_all | solution.py:639
  119.8 0.9 copy-start.10
  128.0 0.7 copy-start.11
  128.7 0.9 copy-start.12
  129.6 5.5 %copy-start.2 = (bf16[4,512,384]{2,1,0:T(8,128)(2,1)S(1)}, bf16[4,512,384]{2,1,0:T(8,128)(2,1)}, u32[]{:S(2)}) copy-start(bf16[4,512,384]{2,1,0:T(8,128)(2,1)} %constant.51.clone.waves) | copy-start | bytes 4718596

commit v11 on v8

--- a/solution.py
+++ b/solution.py
@@ -419,7 +419,7 @@
 
 
 def guarded(value, pivot, scale):
-    good = pivot > 1e-6 * scale
+    good = jnp.abs(pivot) > 1e-6 * jnp.abs(scale)
     return jnp.where(good, value / jnp.where(good, pivot, 1.0), 0.0)
 
 

time: 135 us -> 135 us (level)
  no operation moved by 1% of the time
where the time goes in v11:
time: 135 us; the launch traced here: 134 us
  Pallas kernels  47.3 us (35%)
  starting transfers between devices  31.9 us (24%)
  blocking collectives  31.9 us (24%)
  waiting for transfers between devices  18.4 us (14%)
  local copies, waits for them, and re-layouts  3.56 us (3%)
    all_to_all x4, starting transfers between devices, swap(): return lax.all_to_all(value, axis, 0, 0, tiled=True)  31.9 us
    all_to_all x1, blocking collectives, swap(): return lax.all_to_all(value, axis, 0, 0, tiled=True)  31.9 us
    all_to_all x4, waiting for transfers between devices, swap(): return lax.all_to_all(value, axis, 0, 0, tiled=True)  18.4 us
    pallas_call x1, Pallas kernels, spread(): pl.pallas_call(spread_body, grid=(SITES // CHUNK,), in_specs=[pl.BlockSpe...  15.3 us
    pallas_call x1, Pallas kernels, solve(): pl.pallas_call(solve_body, out_shape=(jax.ShapeDtypeStruct((N_FFT // 2, 3...  8.33 us
    pallas_call x1, Pallas kernels, join(): pl.pallas_call(join_body, out_shape=(jax.ShapeDtypeStruct((N_FFT, 16, PAI...  5.52 us
    pallas_call x1, Pallas kernels, couple(): pl.pallas_call(couple_body, out_shape=jax.ShapeDtypeStruct((ROWS, COLS),...  5.27 us
    pallas_call x1, Pallas kernels, early(): pl.pallas_call(early_body, out_shape=jax.ShapeDtypeStruct((2, 128, 128),...  4.53 us
  transfers between devices with their start and end apart: 4, of which 3 were waited for; matrix products, arithmetic and copies ran while one was open for 1% of the time, Pallas kernels for 25%

profile of v11, /device:TPU:1, one launch (start us, length us, event | category | flops | bytes accessed | tf_op | source)
XLA Modules:
  0.0 134.3 jit_solution(10465494202059939338)
XLA Ops:
  0.6 1.8 %pack.1 = (f32[16,8,128]{2,1,0:T(8,128)}, f32[8,1536]{1,0:T(8,128)}) custom-call(f32[1,32]{1,0:T(1,128)} %bitcast.25, s32[1,32]{1,0:T(1,128)} %bitcast.26, s32[3,32]{1,0:T(4,128)} %cell.2, f32[3,32]{1,0:T(4,128)} %frac.2, f32[1,32]{1,0:T(1,128)} %bitcast.27, f32[3,16384]{1,0:T(4,128)} %pos.1, f32[1,16384]{1,0:T(1,128)} %bitcast.22), custom_call_target="tpu_custom_call" | custom-call | tf_op jit(solution)/shard_map/pack/pallas_call | solution.py:227
  2.4 10.2 %all-to-all-start = ((f32[16,8,128]{2,1,0:T(8,128)}), f32[16,8,128]{2,1,0:T(8,128)S(1)}, u32[]{:S(2)}, u32[]{:S(2)}) async-start(f32[16,8,128]{2,1,0:T(8,128)} %get-tuple-element.12), calls=%async_computation | async-start | bytes 131072 | tf_op jit(solution)/shard_map/all_to_all | solution.py:623
  12.6 0.8 copy-done.1
  13.4 5.3 %couple.1.matrix = f32[512,1024]{1,0:T(8,128)S(1)} custom-call(f32[8,1536]{1,0:T(8,128)S(1)} %copy-done.1), custom_call_target="tpu_custom_call" | custom-call | flops 100000000 | bytes 2000000 | tf_op jit(solution)/shard_map/couple/pallas_call | solution.py:295
  18.7 1.8 %all-to-all-done.got = f32[16,8,128]{2,1,0:T(8,128)S(1)} async-done(((f32[16,8,128]{2,1,0:T(8,128)}), f32[16,8,128]{2,1,0:T(8,128)S(1)}, u32[]{:S(2)}, u32[]{:S(2)}) %all-to-all-start) | async-done | bytes 65568 | tf_op jit(solution)/shard_map/all_to_all | solution.py:623
  20.4 1.3 first_product.1
  21.7 11.3 %all-to-all-start.1 = ((f32[32,40,128]{2,1,0:T(8,128)}), f32[32,40,128]{2,1,0:T(8,128)S(1)}, u32[]{:S(2)}, u32[]{:S(2)}) async-start(f32[32,40,128]{2,1,0:T(8,128)} %first_product.1), calls=%async_computation.1 | async-start | bytes 1310720 | tf_op jit(solution)/shard_map/all_to_all | solution.py:623
  33.0 15.3 %spread.1 = f32[16,32,384]{2,1,0:T(8,128)} custom-call(f32[1,6144]{1,0:T(1,128)} %bitcast.28, f32[3,6144]{1,0:T(4,128)} %frac.3, s32[3,6144]{1,0:T(4,128)} %cell.3, bf16[2,392,384]{2,1,0:T(8,128)(2,1)} %constant.42.clone.waves_from), custom_call_target="tpu_custom_call" | custom-call | flops 8000000000 | bytes 2000000 | tf_op jit(solution)/shard_map/spread/pallas_call | solution.py:175
  48.3 1.5 %all-to-all-done.1.slots = f32[32,40,128]{2,1,0:T(8,128)S(1)} async-done(((f32[32,40,128]{2,1,0:T(8,128)}), f32[32,40,128]{2,1,0:T(8,128)S(1)}, u32[]{:S(2)}, u32[]{:S(2)}) %all-to-all-start.1) | async-done | bytes 655392 | tf_op jit(solution)/shard_map/all_to_all | solution.py:623
  49.8 0.2 multiply_reduce_fusion
  50.2 31.9 %all_to_all.25.grid = f32[16,32,384]{2,1,0:T(8,128)S(1)} all-to-all(f32[16,32,384]{2,1,0:T(8,128)S(1)} %pad_maximum_fusion), channel_id=1, replica_groups=mesh['fft'=32,'slab'=16] {'slab'}, dimensions={0} | all-to-all | bytes 1572864 | tf_op jit(solution)/shard_map/all_to_all | solution.py:623
  82.1 2.4 %along_y.1 = f32[32,16,384]{2,1,0:T(8,128)S(1)} custom-call(f32[16,32,384]{2,1,0:T(8,128)S(1)} %all_to_all.25.grid, f32[512,1024]{1,0:T(8,128)S(1)} %couple.1.matrix, bf16[384,384]{1,0:T(8,128)(2,1)S(1)} %copy-done.8, bf16[512,768]{1,0:T(8,128)(2,1)S(1)} %copy-done.6, bf16[512,768]{1,0:T(8,128)(2,1)S(1)} %copy-done.5, bf16[512,768]{1,0:T(8,128)(2,1)S(1)} %copy-done.4, ...), custom_call_target="tpu_custom_call" | custom-call | flops 4000000000 | bytes 5000000 | tf_op jit(solution)/shard_map/along_y/pallas_call | solution.py:354
  84.5 0.9 copy-done
  85.4 5.6 %all-to-all-start.3 = ((f32[32,16,384]{2,1,0:T(8,128)}), f32[32,16,384]{2,1,0:T(8,128)S(1)}, u32[]{:S(2)}, u32[]{:S(2)}) async-start(f32[32,16,384]{2,1,0:T(8,128)} %copy-done), calls=%async_computation.3 | async-start | bytes 1572864 | tf_op jit(solution)/shard_map/all_to_all | solution.py:623
  91.0 0.7 dynamic-slice_bitcast_fusion.2
  91.7 0.7 dynamic-slice_bitcast_fusion
  92.6 0.2 copy.33
  92.9 4.5 %early.1.before = f32[2,128,128]{2,1,0:T(8,128)S(1)} custom-call(f32[32,40,128]{2,1,0:T(8,128)S(1)} %all-to-all-done.1.slots, f32[128,128]{1,0:T(8,128)S(1)} %reshape.47.first), custom_call_target="tpu_custom_call" | custom-call | flops 2000000000 | bytes 1000000 | tf_op jit(solution)/shard_map/early/pallas_call | solution.py:451
  97.4 15.2 %all-to-all-done.3.grid.got = f32[32,16,384]{2,1,0:T(8,128)S(1)} async-done(((f32[32,16,384]{2,1,0:T(8,128)}), f32[32,16,384]{2,1,0:T(8,128)S(1)}, u32[]{:S(2)}, u32[]{:S(2)}) %all-to-all-start.3) | async-done | bytes 786464 | tf_op jit(solution)/shard_map/all_to_all | solution.py:623
  112.6 1.0 quad_sum.1
  113.6 4.9 %all-to-all-start.4 = ((f32[16,8,128]{2,1,0:T(8,128)}), f32[16,8,128]{2,1,0:T(8,128)S(1)}, u32[]{:S(2)}, u32[]{:S(2)}) async-start(f32[16,8,128]{2,1,0:T(8,128)} %quad_sum.1), calls=%async_computation.4 | async-start | bytes 131072 | tf_op jit(solution)/shard_map/all_to_all | solution.py:623
  118.5 8.3 %solve.1 = (f32[16,32,288]{2,1,0:T(8,128)S(1)}, f32[8,128]{1,0:T(8,128)S(1)}, f32[2,128,128]{2,1,0:T(8,128)S(1)}) custom-call(f32[32,40,128]{2,1,0:T(8,128)S(1)} %all-to-all-done.1.slots, f32[2,128,128]{2,1,0:T(8,128)S(1)} %early.1.before, f32[128,128]{1,0:T(8,128)S(1)} %reshape.47.first, f32[32,16,384]{2,1,0:T(8,128)S(1)} %all-to-all-done.3.grid.got, ...), custom_call_target="tpu_custom_call" | custom-call | flops 5000000000 | bytes 4000000 | tf_op jit(solution)/shard_map/solve/pallas_call | solution.py:552
  126.8 5.5 %join.1 = (f32[32,16,288]{2,1,0:T(8,128)S(1)}, f32[1,32]{1,0:T(1,128)}) custom-call(f32[32,40,128]{2,1,0:T(8,128)S(1)} %all-to-all-done.1.slots, f32[2,128,128]{2,1,0:T(8,128)S(1)} %get-tuple-element.14.charges, f32[32,16,384]{2,1,0:T(8,128)S(1)} %all-to-all-done.3.grid.got, bf16[384,288]{1,0:T(8,128)(2,1)S(1)} %copy-done.7, ...), custom_call_target="tpu_custom_call" | custom-call | flops 4000000000 | bytes 4000000 | tf_op jit(solution)/shard_map/join/pallas_call | solution.py:588
  132.3 1.9 %along_z.1 = (f32[12,12,384]{2,1,0:T(8,128)}, f32[12,12,384]{2,1,0:T(8,128)}) custom-call(f32[32,16,288]{2,1,0:T(8,128)S(1)} %get-tuple-element.18.grid, bf16[4,512,384]{2,1,0:T(8,128)(2,1)S(1)} %copy-done.2), custom_call_target="tpu_custom_call" | custom-call | flops 3000000000 | bytes 5000000 | tf_op jit(solution)/shard_map/along_z/pallas_call | solution.py:613
  (29 shorter events, 0.5 us)
Async XLA Ops:
  2.4 18.0 %all-to-all-start = ((f32[16,8,128]{2,1,0:T(8,128)}), f32[16,8,128]{2,1,0:T(8,128)S(1)}, u32[]{:S(2)}, u32[]{:S(2)}) async-start(f32[16,8,128]{2,1,0:T(8,128)} %get-tuple-element.12), calls=%async_computation | async-start | bytes 131072 | tf_op jit(solution)/shard_map/all_to_all | solution.py:623
  12.6 0.8 copy-start.1
  21.7 28.1 %all-to-all-start.1 = ((f32[32,40,128]{2,1,0:T(8,128)}), f32[32,40,128]{2,1,0:T(8,128)S(1)}, u32[]{:S(2)}, u32[]{:S(2)}) async-start(f32[32,40,128]{2,1,0:T(8,128)} %first_product.1), calls=%async_computation.1 | async-start | bytes 1310720 | tf_op jit(solution)/shard_map/all_to_all | solution.py:623
  48.3 1.8 %copy-start.9 = (f32[16,32,384]{2,1,0:T(8,128)S(1)}, f32[16,32,384]{2,1,0:T(8,128)}, u32[]{:S(2)}) copy-start(f32[16,32,384]{2,1,0:T(8,128)} %spread.1) | copy-start | bytes 2359300
  49.8 32.3 %copy-start.8 = (bf16[384,384]{1,0:T(8,128)(2,1)S(1)}, bf16[384,384]{1,0:T(8,128)(2,1)}, u32[]{:S(2)}) copy-start(bf16[384,384]{1,0:T(8,128)(2,1)} %constant.47.clone.perm) | copy-start | bytes 884740
  50.0 32.0 %copy-start.3 = (bf16[512,768]{1,0:T(8,128)(2,1)S(1)}, bf16[512,768]{1,0:T(8,128)(2,1)}, u32[]{:S(2)}) copy-start(bf16[512,768]{1,0:T(8,128)(2,1)} %constant.46.clone.ail) | copy-start | bytes 2359300
  50.0 32.0 %copy-start.4 = (bf16[512,768]{1,0:T(8,128)(2,1)S(1)}, bf16[512,768]{1,0:T(8,128)(2,1)}, u32[]{:S(2)}) copy-start(bf16[512,768]{1,0:T(8,128)(2,1)} %constant.45.clone.aih) | copy-start | bytes 2359300
  50.0 32.0 %copy-start.5 = (bf16[512,768]{1,0:T(8,128)(2,1)S(1)}, bf16[512,768]{1,0:T(8,128)(2,1)}, u32[]{:S(2)}) copy-start(bf16[512,768]{1,0:T(8,128)(2,1)} %constant.44.clone.arl) | copy-start | bytes 2359300
  50.1 32.0 %copy-start.6 = (bf16[512,768]{1,0:T(8,128)(2,1)S(1)}, bf16[512,768]{1,0:T(8,128)(2,1)}, u32[]{:S(2)}) copy-start(bf16[512,768]{1,0:T(8,128)(2,1)} %constant.43.clone.arh) | copy-start | bytes 2359300
  84.5 0.9 copy-start
  85.4 27.2 %all-to-all-start.3 = ((f32[32,16,384]{2,1,0:T(8,128)}), f32[32,16,384]{2,1,0:T(8,128)S(1)}, u32[]{:S(2)}, u32[]{:S(2)}) async-start(f32[32,16,384]{2,1,0:T(8,128)} %copy-done), calls=%async_computation.3 | async-start | bytes 1572864 | tf_op jit(solution)/shard_map/all_to_all | solution.py:623
  92.9 25.6 %copy-start.7 = (bf16[384,288]{1,0:T(8,128)(2,1)S(1)}, bf16[384,288]{1,0:T(8,128)(2,1)}, u32[]{:S(2)}) copy-start(bf16[384,288]{1,0:T(8,128)(2,1)} %constant.50.clone.perm) | copy-start | bytes 663556
  113.6 13.2 %all-to-all-start.4 = ((f32[16,8,128]{2,1,0:T(8,128)}), f32[16,8,128]{2,1,0:T(8,128)S(1)}, u32[]{:S(2)}, u32[]{:S(2)}) async-start(f32[16,8,128]{2,1,0:T(8,128)} %quad_sum.1), calls=%async_computation.4 | async-start | bytes 131072 | tf_op jit(solution)/shard_map/all_to_all | solution.py:623
  126.8 5.5 %copy-start.2 = (bf16[4,512,384]{2,1,0:T(8,128)(2,1)S(1)}, bf16[4,512,384]{2,1,0:T(8,128)(2,1)}, u32[]{:S(2)}) copy-start(bf16[4,512,384]{2,1,0:T(8,128)(2,1)} %constant.51.clone.waves) | copy-start | bytes 4718596
